TPU v7x, 1024 devices: a whole 4x8x16 slice. The times are simulated.
1024 devices in a mesh: dp: 32 (over x, z_lo, core), mp: 32 (over y, z_hi).
Axes of the slice: x: 4, y: 8, z: 16 (z_hi: 4, z_lo: 4; z = z_hi * 4 + z_lo), core: 2. Of those that a mesh axis runs over, the one named last changes fastest.
Arguments:
- patches: bfloat16 [32, 256, 6144], P('dp', None, 'mp'), may hold values from -6 to 6
- norm_gain: float32 [6144], replicated, may hold values from 0.1 to 1.9
- w_in: bfloat16 [6144, 24576], P(None, 'mp'), may hold values from -0.076546554 to 0.076546554
- q_gain: float32 [32, 128], P('mp'), may hold values from 0.5 to 9
- k_gain: float32 [32, 128], P('mp'), may hold values from 0.5 to 3
- mlp_bias: float32 [12288], P('mp'), may hold values from -3 to 3
- w_out: bfloat16 [16384, 6144], P('mp', 'dp'), may hold values from -0.046875 to 0.046875
- out_bias: float32 [6144], P('mp'), may hold values from -3 to 3
Outputs:
- mixed: bfloat16 [32, 256, 6144], P('dp', None, 'mp')
All inputs are finite; a program needn't handle non-finite values.
Results may differ from a plain program's by a relative error of at most 0.022.
Values may be sent and summed in bfloat16 or wider, within the bound.
No kernel may reach another device: no remote copies, remote signals or barrier semaphores. Data moves between devices by JAX's collectives and lax.ppermute only.
A program may use at most 64 MiB of HBM per device.

v0:
```python
import jax
import jax.numpy as jnp
from jax import lax
from jax.sharding import PartitionSpec as P

EPS = 1e-06


def normalize(values):
    center = values - jnp.mean(values, axis=-1, keepdims=True)
    spread = jnp.mean(center * center, axis=-1, keepdims=True)
    return center * lax.rsqrt(spread + EPS)


def per_device(patches, norm_gain, w_in, q_gain, k_gain, mlp_bias, w_out, out_bias):
    images, seq_len, local_width = patches.shape
    rows_count = images * seq_len
    flat = patches.reshape(rows_count, local_width)
    whole = lax.all_gather(flat, "mp", axis=1, tiled=True)
    normed = (normalize(whole.astype(jnp.float32)) * norm_gain).astype(jnp.bfloat16)
    project = jnp.dot(normed, w_in, preferred_element_type=jnp.float32)
    heads_local = q_gain.shape[0]
    head_width = q_gain.shape[1]
    width_att = heads_local * head_width
    scale_factor = 1.0 / head_width**0.5
    queries = project[:, :width_att].reshape(images, seq_len, heads_local, head_width)
    keys = project[:, width_att : 2 * width_att].reshape(images, seq_len, heads_local, head_width)
    values = (
        project[:, 2 * width_att : 3 * width_att]
        .astype(jnp.bfloat16)
        .reshape(images, seq_len, heads_local, head_width)
    )
    mlp_pre = project[:, 3 * width_att :]
    qnorm = normalize(queries) * q_gain
    knorm = normalize(keys) * k_gain
    scores = jnp.einsum("bqhd,bkhd->bhqk", qnorm, knorm) * scale_factor
    probs = jax.nn.softmax(scores, axis=-1).astype(jnp.bfloat16)
    attended = jnp.einsum(
        "bhqk,bkhd->bqhd", probs, values, preferred_element_type=jnp.float32
    ).astype(jnp.bfloat16)
    mlp_hidden = jax.nn.gelu(mlp_pre + mlp_bias, approximate=False).astype(jnp.bfloat16)
    hidden = jnp.concatenate([attended.reshape(rows_count, width_att), mlp_hidden], axis=1)
    partial_out = jnp.dot(
        hidden, lax.all_gather(w_out, "dp", axis=1, tiled=True), preferred_element_type=jnp.float32
    )
    summed = lax.psum_scatter(
        partial_out.astype(jnp.bfloat16), "mp", scatter_dimension=1, tiled=True
    ).astype(jnp.float32)
    result = flat.astype(jnp.float32) + summed + out_bias
    return result.astype(jnp.bfloat16).reshape(images, seq_len, local_width)


def solution(mesh):
    in_specs = (
        P("dp", None, "mp"),
        P(),
        P(None, "mp"),
        P("mp", None),
        P("mp", None),
        P("mp"),
        P("mp", "dp"),
        P("mp"),
    )
    out_specs = P("dp", None, "mp")
    return jax.shard_map(
        per_device, mesh=mesh, in_specs=in_specs, out_specs=out_specs, check_vma=False
    )
```

profile of v0, /device:TPU:4, one launch (start us, length us, event | category | flops | bytes accessed | tf_op | source)
XLA Modules:
  0.0 496.2 jit_solution(13679150790880853816)
XLA Ops:
  6.5 0.0 copy-start.6
  6.5 0.0 all-gather.6.cloned.1.call-start
  6.5 0.7 all-gather.6.cloned.1.call-update
  7.3 0.0 all-gather.4.cloned.1.call-start
  7.3 0.7 all-gather.4.cloned.1.call-update
  8.0 0.0 reduce-scatter.2.cloned.1.call-start
  8.1 146.4 %all-gather.6.cloned.1.call-done = bf16[1,256,6144]{1,2,0:T(8,128)(2,1)} async-done(((bf16[1,256,192]{1,2,0:T(8,128)(2,1)}), bf16[1,256,6144]{1,2,0:T(8,128)(2,1)}) %all-gather.6.cloned.1.call-update) | async-done | bytes 3145744 | tf_op jit(solution)/shard_map/all_gather | solution.py:19
  154.4 0.0 copy-start
  154.4 2.9 convert_reduce_fusion
  157.3 2.8 fusion.3
  160.1 0.0 copy-done.6
  160.1 0.0 copy-done
  160.1 0.0 copy-start.4
  160.1 0.0 copy-start.5
  160.1 0.0 copy-start.2
  160.1 7.1 %fusion.6 = f32[256,768]{1,0:T(8,128)S(1)} fusion(bf16[6144,768]{1,0:T(8,128)(2,1)} %param.10, bf16[1,256,6144]{1,2,0:T(8,128)(2,1)S(1)} %copy-done, f32[6144]{0:T(1024)S(1)} %copy-done.6, f32[256]{0:T(256)S(1)} %add_rsqrt_fusion.2, f32[256]{0:T(256)S(1)} %broadcast_multiply_fusion.2), kind=kOutput, calls=%fused_computation.9 | convolution fusion | flops 2423783424 | bytes 13395968 | tf_op jit(solution)/shard_map/dot_general | solution.py:21
  167.2 0.1 slice_reduce_fusion.1
  167.4 0.2 multiply_reduce_fusion.1
  167.6 0.0 copy-done.4
  167.6 0.0 copy-done.5
  167.7 0.3 fusion.40
  168.0 0.1 fusion.25
  168.1 0.2 fusion.11
  168.3 0.0 copy-done.2
  168.3 0.9 fusion.14
  169.2 0.0 copy-start.1
  169.2 0.0 copy-start.3
  169.2 55.3 %all-gather.4.cloned.1.call-done = bf16[512,6144]{0,1:T(8,128)(2,1)} async-done(((bf16[512,192]{0,1:T(8,128)(2,1)}), bf16[512,6144]{0,1:T(8,128)(2,1)}) %all-gather.4.cloned.1.call-update) | async-done | bytes 6291472 | tf_op jit(solution)/shard_map/all_gather | solution.py:44
  224.6 6.3 %convolution_convert_fusion = bf16[256,6144]{0,1:T(8,128)(2,1)} fusion(bf16[512,6144]{0,1:T(8,128)(2,1)} %all-gather.4.cloned.1.call-done, bf16[256,384]{1,0:T(8,128)(2,1)S(1)} %fusion.14, bf16[256,128]{1,0:T(8,128)(2,1)S(1)} %fusion.11), kind=kOutput, calls=%fused_computation.2 | convolution fusion | flops 1612709888 | bytes 9699328 | tf_op jit(solution)/shard_map/dot_general | solution.py:43
  230.9 0.0 reduce-scatter.2.cloned.1.call-update
  230.9 257.1 %reduce-scatter.2.cloned.1.call-done = bf16[256,192]{0,1:T(8,128)(2,1)} async-done(((bf16[256,6144]{0,1:T(8,128)(2,1)}), bf16[256,192]{0,1:T(8,128)(2,1)}) %reduce-scatter.2.cloned.1.call-update) | async-done | bytes 98320 | tf_op jit(solution)/shard_map/reduce_scatter | solution.py:46
  488.0 0.0 copy-done.1
  488.0 0.0 copy-done.3
  488.0 1.6 fusion.32
  (5 shorter events, 0.0 us)
Async XLA Ops:
  6.5 153.5 %copy-start.6 = (f32[6144]{0:T(1024)S(1)}, f32[6144]{0:T(1024)}, u32[]{:S(2)}) copy-start(f32[6144]{0:T(1024)} %param.9) | copy-start | bytes 73732
  6.5 147.9 %all-gather.6.cloned.1.call-start = ((), (), s32[]{:S(2)}) async-start(), calls=%async_computation.3 | async-start | bytes 3244032 | tf_op jit(solution)/shard_map/all_gather | solution.py:19
  7.3 217.3 %all-gather.4.cloned.1.call-start = ((), (), s32[]{:S(2)}) async-start(), calls=%async_computation.1 | async-start | bytes 6488064 | tf_op jit(solution)/shard_map/all_gather | solution.py:44
  8.0 480.0 %reduce-scatter.2.cloned.1.call-start = ((), (), s32[]{:S(2)}) async-start(), calls=%async_computation.2 | async-start | bytes 3244032 | tf_op jit(solution)/shard_map/reduce_scatter | solution.py:46
  154.4 5.7 %copy-start = (bf16[1,256,6144]{1,2,0:T(8,128)(2,1)S(1)}, bf16[1,256,6144]{1,2,0:T(8,128)(2,1)}, u32[]{:S(2)}) copy-start(bf16[1,256,6144]{1,2,0:T(8,128)(2,1)} %all-gather.6.cloned.1.call-done) | copy-start | bytes 9437188
  160.1 7.6 %copy-start.4 = (f32[1,128]{1,0:T(1,128)S(1)}, f32[1,128]{1,0:T(1,128)}, u32[]{:S(2)}) copy-start(f32[1,128]{1,0:T(1,128)} %param.12) | copy-start | bytes 1540
  160.1 7.6 %copy-start.5 = (f32[1,128]{1,0:T(1,128)S(1)}, f32[1,128]{1,0:T(1,128)}, u32[]{:S(2)}) copy-start(f32[1,128]{1,0:T(1,128)} %param.11) | copy-start | bytes 1540
  160.1 8.2 %copy-start.2 = (f32[384]{0:T(512)S(1)}, f32[384]{0:T(512)}, u32[]{:S(2)}) copy-start(f32[384]{0:T(512)} %param.13) | copy-start | bytes 4612
  169.2 318.8 %copy-start.1 = (bf16[1,256,192]{1,2,0:T(8,128)(2,1)S(1)}, bf16[1,256,192]{1,2,0:T(8,128)(2,1)}, u32[]{:S(2)}) copy-start(bf16[1,256,192]{1,2,0:T(8,128)(2,1)} %param.8) | copy-start | bytes 294916
  169.2 318.8 %copy-start.3 = (f32[192]{0:T(256)S(1)}, f32[192]{0:T(256)}, u32[]{:S(2)}) copy-start(f32[192]{0:T(256)} %param.15) | copy-start | bytes 2308
Sparse Core Ops, SparseCore 0:
  11.7 142.6 all-gather.5
  157.1 67.3 all-gather.3
  231.0 256.9 reduce-scatter.1
where the time goes:
time: 496 us
  waiting for transfers between devices  460 us (93%)
  matrix products  14 us (3%)
  between operations  13.2 us (3%)
  other arithmetic  8.63 us (2%)
    reduce_scatter x1, waiting for transfers between devices, per_device(): lax.psum_scatter(partial_out.astype(jnp.bfloat16), 'mp', scatter_dimensio...  257 us
    all_gather x1, waiting for transfers between devices, per_device(): whole = lax.all_gather(flat, 'mp', axis=1, tiled=True)  146 us
    all_gather x1, waiting for transfers between devices, per_device(): lax.all_gather(w_out, 'dp', axis=1, tiled=True)  55.3 us
  transfers between devices with their start and end apart: 3, of which 3 were waited for; matrix products, arithmetic and copies ran while one was open for 3% of the time, Pallas kernels for 0%

commit v1 on v0

v1 whole, which is shorter than its diff:
```python
import jax
import jax.numpy as jnp
from jax import lax
from jax.sharding import Mesh
from jax.sharding import PartitionSpec as P

EPS = 1e-06
NY = 8
NZ = 4


def normalize(values, axis):
    center = values - jnp.mean(values, axis=axis, keepdims=True)
    spread = jnp.mean(center * center, axis=axis, keepdims=True)
    return center * lax.rsqrt(spread + EPS)


def shift(value, axis, count, by):
    return lax.ppermute(value, axis, [(i, (i + by) % count) for i in range(count)])


def gather_y(block):
    y = lax.axis_index("y")
    half = block.shape[0] // 2
    whole = jnp.zeros((NY,) + block.shape, block.dtype)
    put = lambda whole, part, index, row: lax.dynamic_update_slice(
        whole, part[None], (index % NY, row, 0)
    )
    whole = put(whole, block, y, 0)
    up = down = block
    for step in range(1, 4):
        up, down = shift(up, "y", NY, 1), shift(down, "y", NY, -1)
        whole = put(whole, up, y - step + NY, 0)
        whole = put(whole, down, y + step, 0)
    up = shift(up[:half], "y", NY, 1)
    down = shift(down[half:], "y", NY, -1)
    whole = put(whole, up, y + 4, 0)
    whole = put(whole, down, y + 4, half)
    return whole


def per_device(patches, norm_gain, w_in, q_gain, k_gain, mlp_bias, w_out, out_bias):
    images, seq_len, local_width = patches.shape
    mine = patches[0].T
    zgroup = lax.all_gather(mine, "zh", axis=0, tiled=True)
    w_outT = lax.all_gather(w_out.T, ("x", "zl", "c"), axis=0, tiled=True)
    whole = gather_y(zgroup).reshape(-1, seq_len)
    normed = (normalize(whole.astype(jnp.float32), 0) * norm_gain[:, None]).astype(jnp.bfloat16)
    project = lax.dot_general(
        w_in, normed, (((0,), (0,)), ((), ())), preferred_element_type=jnp.float32
    )
    head = q_gain.shape[1]
    queries = normalize(project[:head], 0) * q_gain[0][:, None]
    keys = normalize(project[head : 2 * head], 0) * k_gain[0][:, None]
    values = project[2 * head : 3 * head].astype(jnp.bfloat16)
    scores = lax.dot_general(queries, keys, (((0,), (0,)), ((), ()))) * (1.0 / head**0.5)
    probs = jax.nn.softmax(scores, axis=-1).astype(jnp.bfloat16)
    attended = lax.dot_general(
        values, probs, (((1,), (1,)), ((), ())), preferred_element_type=jnp.float32
    ).astype(jnp.bfloat16)
    mlp_hidden = jax.nn.gelu(project[3 * head :] + mlp_bias[:, None], approximate=False)
    hidden = jnp.concatenate([attended, mlp_hidden.astype(jnp.bfloat16)], axis=0)
    part = jnp.dot(w_outT, hidden, preferred_element_type=jnp.float32).astype(jnp.bfloat16)
    summed = lax.psum_scatter(part, "y", scatter_dimension=0, tiled=True)
    pieces = lax.all_to_all(summed.reshape(NZ, local_width, seq_len), "zh", 0, 0)
    total = jnp.sum(pieces.astype(jnp.float32), axis=0)
    result = mine.astype(jnp.float32) + total + out_bias[:, None]
    return result.astype(jnp.bfloat16).T[None]


def solution(mesh):
    fine = Mesh(mesh.devices.reshape(4, 4, 2, NY, NZ), ("x", "zl", "c", "y", "zh"))
    dp = ("x", "zl", "c")
    mp = ("y", "zh")
    in_specs = (
        P(dp, None, mp),
        P(),
        P(None, mp),
        P(mp, None),
        P(mp, None),
        P(mp),
        P(mp, dp),
        P(mp),
    )
    return jax.shard_map(
        per_device, mesh=fine, in_specs=in_specs, out_specs=P(dp, None, mp), check_vma=False
    )
```

time: 496 us -> 205 us (0.41)
  the two profiles are of different devices: /device:TPU:4 before, /device:TPU:66 now
where the time goes in v1:
time: 205 us; the launch traced here: 204 us
  waiting for transfers between devices  75.2 us (37%)
  blocking collectives  69.8 us (34%)
  starting transfers between devices  29 us (14%)
  between operations  13.9 us (7%)
  matrix products  9.53 us (5%)
  other arithmetic  4.98 us (2%)
    reduce_scatter x1, waiting for transfers between devices, per_device(): summed = lax.psum_scatter(part, 'y', scatter_dimension=0, tiled=True)  58.3 us
    all_to_all x1, blocking collectives, per_device(): lax.all_to_all(summed.reshape(NZ, local_width, seq_len), 'zh', 0, 0)  36.4 us
    all_gather x1, blocking collectives, per_device(): zgroup = lax.all_gather(mine, 'zh', axis=0, tiled=True)  33.4 us
    ppermute x8, starting transfers between devices, shift(): lax.ppermute(value, axis, [(i, (i + by) % count) for i in range(count)])  29 us
    ppermute x8, waiting for transfers between devices, shift(): lax.ppermute(value, axis, [(i, (i + by) % count) for i in range(count)])  16.1 us
    dot_general x1, matrix products, per_device(): jnp.dot(w_outT, hidden, preferred_element_type=jnp.float32)  6.32 us
  transfers between devices with their start and end apart: 10, of which 6 were waited for; matrix products, arithmetic and copies ran while one was open for 4% of the time, Pallas kernels for 0%

profile of v1, /device:TPU:66, one launch (start us, length us, event | category | flops | bytes accessed | tf_op | source)
XLA Modules:
  0.0 204.1 jit_solution(7492156758762512237)
XLA Ops:
  6.5 0.0 all-gather.2.cloned.1.call-start
  6.5 0.7 all-gather.2.cloned.1.call-update
  7.3 0.0 reduce-scatter.2.cloned.1.call-start
  7.3 33.4 %all_gather.6 = bf16[768,256]{1,0:T(8,128)(2,1)S(1)} all-gather(bf16[192,256]{1,0:T(8,128)(2,1)} %bitcast.54), channel_id=1, replica_groups=mesh['x'=4,'zl'=4,'c'=2,'y'=8,'zh'=4] {'zh'}, dimensions={0}, use_global_device_ids=true | all-gather | bytes 491520 | tf_op jit(solution)/shard_map/all_gather | solution.py:45
  40.7 3.6 %collective-permute-start = (bf16[768,256]{1,0:T(8,128)(2,1)S(1)}, bf16[768,256]{1,0:T(8,128)(2,1)S(1)}, u32[]{:S(2)}, u32[]{:S(2)}) collective-permute-start(bf16[768,256]{1,0:T(8,128)(2,1)S(1)} %all_gather.6), channel_id=1, source_target_pairs={{0,4},{4,8},{8,12},{12,16},{16,20},{20,24},{24,28},{28,0},{1,5},{5... | collective-permute-start | bytes 1179656 | tf_op jit(solution)/shard_map/ppermute | solution.py:19
  44.2 4.0 %collective-permute-start.1 = (bf16[768,256]{1,0:T(8,128)(2,1)S(1)}, bf16[768,256]{1,0:T(8,128)(2,1)S(1)}, u32[]{:S(2)}, u32[]{:S(2)}) collective-permute-start(bf16[768,256]{1,0:T(8,128)(2,1)S(1)} %all_gather.6), channel_id=1, source_target_pairs={{0,28},{4,0},{8,4},{12,8},{16,12},{20,16},{24,20},{28,24},{1,29},{... | collective-permute-start | bytes 1179656 | tf_op jit(solution)/shard_map/ppermute | solution.py:19
  48.4 0.0 slice-start
  48.4 0.2 broadcast_in_dim.44
  48.6 5.0 %collective-permute-done = bf16[768,256]{1,0:T(8,128)(2,1)S(1)} collective-permute-done((bf16[768,256]{1,0:T(8,128)(2,1)S(1)}, bf16[768,256]{1,0:T(8,128)(2,1)S(1)}, u32[]{:S(2)}, u32[]{:S(2)}) %collective-permute-start) | collective-permute-done | bytes 393248 | tf_op jit(solution)/shard_map/ppermute | solution.py:19
  53.6 1.9 collective-permute-start.2
  55.5 0.0 collective-permute-done.1
  55.6 5.1 %collective-permute-start.3 = (bf16[768,256]{1,0:T(8,128)(2,1)S(1)}, bf16[768,256]{1,0:T(8,128)(2,1)S(1)}, u32[]{:S(2)}, u32[]{:S(2)}) collective-permute-start(bf16[768,256]{1,0:T(8,128)(2,1)S(1)} %collective-permute-done.1), channel_id=1, source_target_pairs={{0,28},{4,0},{8,4},{12,8},{16,12},{20,16},{24,20},{28,24},{1,29},{... | collective-permute-start | bytes 1179656 | tf_op jit(solution)/shard_map/ppermute | solution.py:19
  60.8 4.4 %collective-permute-done.2 = bf16[768,256]{1,0:T(8,128)(2,1)S(1)} collective-permute-done((bf16[768,256]{1,0:T(8,128)(2,1)S(1)}, bf16[768,256]{1,0:T(8,128)(2,1)S(1)}, u32[]{:S(2)}, u32[]{:S(2)}) %collective-permute-start.2) | collective-permute-done | bytes 393248 | tf_op jit(solution)/shard_map/ppermute | solution.py:19
  65.1 1.9 collective-permute-start.4
  67.0 0.0 collective-permute-done.3
  67.1 5.1 %collective-permute-start.5 = (bf16[768,256]{1,0:T(8,128)(2,1)S(1)}, bf16[768,256]{1,0:T(8,128)(2,1)S(1)}, u32[]{:S(2)}, u32[]{:S(2)}) collective-permute-start(bf16[768,256]{1,0:T(8,128)(2,1)S(1)} %collective-permute-done.3), channel_id=1, source_target_pairs={{0,28},{4,0},{8,4},{12,8},{16,12},{20,16},{24,20},{28,24},{1,29},{... | collective-permute-start | bytes 1179656 | tf_op jit(solution)/shard_map/ppermute | solution.py:19
  72.3 3.7 %collective-permute-done.4 = bf16[768,256]{1,0:T(8,128)(2,1)S(1)} collective-permute-done((bf16[768,256]{1,0:T(8,128)(2,1)S(1)}, bf16[768,256]{1,0:T(8,128)(2,1)S(1)}, u32[]{:S(2)}, u32[]{:S(2)}) %collective-permute-start.4) | collective-permute-done | bytes 393248 | tf_op jit(solution)/shard_map/ppermute | solution.py:19
  76.0 0.0 slice-start.1
  76.0 2.2 %collective-permute-start.6 = (bf16[384,256]{1,0:T(8,128)(2,1)S(1)}, bf16[384,256]{1,0:T(8,128)(2,1)S(1)}, u32[]{:S(2)}, u32[]{:S(2)}) collective-permute-start(bf16[384,256]{1,0:T(8,128)(2,1)S(1)} %slice.25), channel_id=1, source_target_pairs={{0,4},{4,8},{8,12},{12,16},{16,20},{20,24},{24,28},{28,0},{1,5},{5... | collective-permute-start | bytes 589832 | tf_op jit(solution)/shard_map/ppermute | solution.py:19
  78.2 0.0 collective-permute-done.5
  78.3 5.1 %collective-permute-start.7 = (bf16[384,256]{1,0:T(8,128)(2,1)S(1)}, bf16[384,256]{1,0:T(8,128)(2,1)S(1)}, u32[]{:S(2)}, u32[]{:S(2)}) collective-permute-start(bf16[384,256]{1,0:T(8,128)(2,1)S(1)} %slice.26), channel_id=1, source_target_pairs={{0,28},{4,0},{8,4},{12,8},{16,12},{20,16},{24,20},{28,24},{1,29},{... | collective-permute-start | bytes 589832 | tf_op jit(solution)/shard_map/ppermute | solution.py:19
  83.5 1.6 collective-permute-done.6
  85.1 1.5 collective-permute-done.7
  86.6 0.0 copy-start.1
  86.6 0.8 convert_reduce_fusion
  87.4 0.0 slice-start.2
  87.4 0.9 multiply_reduce_fusion
  88.3 0.0 copy-done.1
  88.3 1.1 fusion.3
  89.5 0.0 slice-done
  89.5 0.0 slice-done.1
  89.5 0.0 slice-done.2
  89.5 0.0 copy-start.4
  89.5 0.0 copy-start.5
  89.5 0.0 copy-start.2
  89.5 2.6 %convolution_bitcast_fusion = f32[768,256]{0,1:T(8,128)S(1)} fusion(bf16[6144,256]{1,0:T(8,128)(2,1)S(1)} %fusion.3, bf16[6144,768]{1,0:T(8,128)(2,1)S(1)} %bitcast.52), kind=kOutput, calls=%fused_computation.8 | convolution fusion | flops 2415919104 | bytes 13369344 | tf_op jit(solution)/shard_map/dot_general | solution.py:49
  92.2 0.1 slice_reduce_fusion.1
  92.3 0.2 multiply_reduce_fusion.2
  92.6 0.0 copy-done.4
  92.6 0.0 copy-done.5
  92.6 0.3 fusion.32
  93.0 0.1 fusion.17
  93.0 0.2 convolution_convert_fusion.1
  93.3 0.0 copy-done.2
  93.3 0.9 fusion.6
  94.2 0.0 all-gather.2.cloned.1.call-done
  94.2 6.3 %fusion = bf16[6144,256]{0,1:T(8,128)(2,1)} fusion(bf16[6144,512]{1,0:T(8,128)(2,1)} %all-gather.2.cloned.1.call-done, bf16[384,256]{0,1:T(8,128)(2,1)S(1)} %fusion.6, bf16[128,256]{0,1:T(8,128)(2,1)S(1)} %convolution_convert_fusion.1), kind=kOutput, calls=%fused_computation.1 | convolution fusion | flops 1612709888 | bytes 9699328 | tf_op jit(solution)/shard_map/dot_general | solution.py:63
  100.5 0.0 copy-start
  100.5 0.0 copy-start.3
  100.5 0.0 reduce-scatter.2.cloned.1.call-update
  100.5 58.3 %reduce-scatter.2.cloned.1.call-done = bf16[768,256]{0,1:T(8,128)(2,1)} async-done(((bf16[6144,256]{0,1:T(8,128)(2,1)}), bf16[768,256]{0,1:T(8,128)(2,1)}) %reduce-scatter.2.cloned.1.call-update) | async-done | bytes 393232 | tf_op jit(solution)/shard_map/reduce_scatter | solution.py:64
  158.9 1.2 copy.9
  160.0 36.4 %all_to_all.5 = bf16[4,192,256]{2,1,0:T(8,128)(2,1)S(1)} all-to-all(bf16[4,192,256]{2,1,0:T(8,128)(2,1)S(1)} %bitcast.53), channel_id=1, replica_groups=mesh['x'=4,'zl'=4,'c'=2,'y'=8,'zh'=4] {'zh'}, dimensions={0} | all-to-all | bytes 786432 | tf_op jit(solution)/shard_map/all_to_all | solution.py:65
  196.5 0.0 copy-done
  196.5 0.0 copy-done.3
  196.5 0.7 fusion.24
  (18 shorter events, 0.4 us)
Async XLA Ops:
  6.5 87.7 %all-gather.2.cloned.1.call-start = ((), (), s32[]{:S(2)}) async-start(), calls=%async_computation.2 | async-start | bytes 6488064 | tf_op jit(solution)/shard_map/all_gather | solution.py:46
  7.3 151.6 %reduce-scatter.2.cloned.1.call-start = ((), (), s32[]{:S(2)}) async-start(), calls=%async_computation.3 | async-start | bytes 3538944 | tf_op jit(solution)/shard_map/reduce_scatter | solution.py:64
  40.7 13.0 %collective-permute-start = (bf16[768,256]{1,0:T(8,128)(2,1)S(1)}, bf16[768,256]{1,0:T(8,128)(2,1)S(1)}, u32[]{:S(2)}, u32[]{:S(2)}) collective-permute-start(bf16[768,256]{1,0:T(8,128)(2,1)S(1)} %all_gather.6), channel_id=1, source_target_pairs={{0,4},{4,8},{8,12},{12,16},{16,20},{20,24},{24,28},{28,0},{1,5},{5... | collective-permute-start | bytes 1179656 | tf_op jit(solution)/shard_map/ppermute | solution.py:19
  44.2 11.3 %collective-permute-start.1 = (bf16[768,256]{1,0:T(8,128)(2,1)S(1)}, bf16[768,256]{1,0:T(8,128)(2,1)S(1)}, u32[]{:S(2)}, u32[]{:S(2)}) collective-permute-start(bf16[768,256]{1,0:T(8,128)(2,1)S(1)} %all_gather.6), channel_id=1, source_target_pairs={{0,28},{4,0},{8,4},{12,8},{16,12},{20,16},{24,20},{28,24},{1,29},{... | collective-permute-start | bytes 1179656 | tf_op jit(solution)/shard_map/ppermute | solution.py:19
  48.4 41.1 %slice-start = ((s8[9437184]{0:T(1024)(128)(4,1)}), s8[4194304]{0:T(1024)(128)(4,1)S(1)}, s32[]{:S(2)}) async-start(s8[9437184]{0:T(1024)(128)(4,1)} %bitcast.51), calls=%async_computation.4 | async-start | bytes 8388608
  53.6 11.5 %collective-permute-start.2 = (bf16[768,256]{1,0:T(8,128)(2,1)S(1)}, bf16[768,256]{1,0:T(8,128)(2,1)S(1)}, u32[]{:S(2)}, u32[]{:S(2)}) collective-permute-start(bf16[768,256]{1,0:T(8,128)(2,1)S(1)} %collective-permute-done), channel_id=1, source_target_pairs={{0,4},{4,8},{8,12},{12,16},{16,20},{20,24},{24,28},{28,0},{1,5},{5... | collective-permute-start | bytes 1179656 | tf_op jit(solution)/shard_map/ppermute | solution.py:19
  55.6 11.5 %collective-permute-start.3 = (bf16[768,256]{1,0:T(8,128)(2,1)S(1)}, bf16[768,256]{1,0:T(8,128)(2,1)S(1)}, u32[]{:S(2)}, u32[]{:S(2)}) collective-permute-start(bf16[768,256]{1,0:T(8,128)(2,1)S(1)} %collective-permute-done.1), channel_id=1, source_target_pairs={{0,28},{4,0},{8,4},{12,8},{16,12},{20,16},{24,20},{28,24},{1,29},{... | collective-permute-start | bytes 1179656 | tf_op jit(solution)/shard_map/ppermute | solution.py:19
  65.1 10.9 %collective-permute-start.4 = (bf16[768,256]{1,0:T(8,128)(2,1)S(1)}, bf16[768,256]{1,0:T(8,128)(2,1)S(1)}, u32[]{:S(2)}, u32[]{:S(2)}) collective-permute-start(bf16[768,256]{1,0:T(8,128)(2,1)S(1)} %collective-permute-done.2), channel_id=1, source_target_pairs={{0,4},{4,8},{8,12},{12,16},{16,20},{20,24},{24,28},{28,0},{1,5},{5... | collective-permute-start | bytes 1179656 | tf_op jit(solution)/shard_map/ppermute | solution.py:19
  67.1 11.2 %collective-permute-start.5 = (bf16[768,256]{1,0:T(8,128)(2,1)S(1)}, bf16[768,256]{1,0:T(8,128)(2,1)S(1)}, u32[]{:S(2)}, u32[]{:S(2)}) collective-permute-start(bf16[768,256]{1,0:T(8,128)(2,1)S(1)} %collective-permute-done.3), channel_id=1, source_target_pairs={{0,28},{4,0},{8,4},{12,8},{16,12},{20,16},{24,20},{28,24},{1,29},{... | collective-permute-start | bytes 1179656 | tf_op jit(solution)/shard_map/ppermute | solution.py:19
  76.0 13.4 %slice-start.1 = ((s8[9437184]{0:T(1024)(128)(4,1)}), s8[4194304]{0:T(1024)(128)(4,1)S(1)}, s32[]{:S(2)}) async-start(s8[9437184]{0:T(1024)(128)(4,1)} %bitcast.51), calls=%async_computation.5 | async-start | bytes 8388608
  76.0 9.0 %collective-permute-start.6 = (bf16[384,256]{1,0:T(8,128)(2,1)S(1)}, bf16[384,256]{1,0:T(8,128)(2,1)S(1)}, u32[]{:S(2)}, u32[]{:S(2)}) collective-permute-start(bf16[384,256]{1,0:T(8,128)(2,1)S(1)} %slice.25), channel_id=1, source_target_pairs={{0,4},{4,8},{8,12},{12,16},{16,20},{20,24},{24,28},{28,0},{1,5},{5... | collective-permute-start | bytes 589832 | tf_op jit(solution)/shard_map/ppermute | solution.py:19
  78.3 8.3 %collective-permute-start.7 = (bf16[384,256]{1,0:T(8,128)(2,1)S(1)}, bf16[384,256]{1,0:T(8,128)(2,1)S(1)}, u32[]{:S(2)}, u32[]{:S(2)}) collective-permute-start(bf16[384,256]{1,0:T(8,128)(2,1)S(1)} %slice.26), channel_id=1, source_target_pairs={{0,28},{4,0},{8,4},{12,8},{16,12},{20,16},{24,20},{28,24},{1,29},{... | collective-permute-start | bytes 589832 | tf_op jit(solution)/shard_map/ppermute | solution.py:19
  86.6 1.7 copy-start.1
  87.4 2.0 %slice-start.2 = ((s8[9437184]{0:T(1024)(128)(4,1)}), s8[1048576]{0:T(1024)(128)(4,1)S(1)}, s32[]{:S(2)}) async-start(s8[9437184]{0:T(1024)(128)(4,1)} %bitcast.51), calls=%async_computation.6 | async-start | bytes 2097152
  89.5 3.1 %copy-start.4 = (f32[1,128]{1,0:T(1,128)S(1)}, f32[1,128]{1,0:T(1,128)}, u32[]{:S(2)}) copy-start(f32[1,128]{1,0:T(1,128)} %param.12) | copy-start | bytes 1540
  89.5 3.1 %copy-start.5 = (f32[1,128]{1,0:T(1,128)S(1)}, f32[1,128]{1,0:T(1,128)}, u32[]{:S(2)}) copy-start(f32[1,128]{1,0:T(1,128)} %param.11) | copy-start | bytes 1540
  89.5 3.8 %copy-start.2 = (f32[384]{0:T(512)S(1)}, f32[384]{0:T(512)}, u32[]{:S(2)}) copy-start(f32[384]{0:T(512)} %param.13) | copy-start | bytes 4612
  100.5 96.0 %copy-start = (bf16[1,256,192]{1,2,0:T(8,128)(2,1)S(1)}, bf16[1,256,192]{1,2,0:T(8,128)(2,1)}, u32[]{:S(2)}) copy-start(bf16[1,256,192]{1,2,0:T(8,128)(2,1)} %param.8) | copy-start | bytes 294916
  100.5 96.0 %copy-start.3 = (f32[192]{0:T(256)S(1)}, f32[192]{0:T(256)}, u32[]{:S(2)}) copy-start(f32[192]{0:T(256)} %param.15) | copy-start | bytes 2308
Sparse Core Ops, SparseCore 0:
  10.1 83.4 all-gather.1
  100.7 58.1 reduce-scatter.1

commit v2 on v1

--- a/solution.py
+++ b/solution.py
@@ -5,8 +5,12 @@
 from jax.sharding import PartitionSpec as P
 
 EPS = 1e-06
+NX = 4
 NY = 8
 NZ = 4
+AXES = ("x", "zlh", "zll", "c", "y", "zh")
+DP = ("x", "zlh", "zll", "c")
+MP = ("y", "zh")
 
 
 def normalize(values, axis):
@@ -24,7 +28,7 @@
     half = block.shape[0] // 2
     whole = jnp.zeros((NY,) + block.shape, block.dtype)
     put = lambda whole, part, index, row: lax.dynamic_update_slice(
-        whole, part[None], (index % NY, row, 0)
+        whole, part[None], (index & (NY - 1), row, 0)
     )
     whole = put(whole, block, y, 0)
     up = down = block
@@ -39,11 +43,23 @@
     return whole
 
 
+def gather_out_weights(w_out):
+    depth = w_out.shape[0]
+    pairs = [
+        ((out * 4 + low) * NY + y, (y * 4 + low) * NY + out)
+        for out in range(NY)
+        for low in range(4)
+        for y in range(NY)
+    ]
+    swapped = lax.ppermute(w_out.T, ("x", "zlh", "zll", "c", "y"), pairs)
+    return lax.all_gather(swapped, DP, axis=0, tiled=True).reshape(NY, -1, depth)
+
+
 def per_device(patches, norm_gain, w_in, q_gain, k_gain, mlp_bias, w_out, out_bias):
     images, seq_len, local_width = patches.shape
     mine = patches[0].T
+    w_rows = gather_out_weights(w_out)
     zgroup = lax.all_gather(mine, "zh", axis=0, tiled=True)
-    w_outT = lax.all_gather(w_out.T, ("x", "zl", "c"), axis=0, tiled=True)
     whole = gather_y(zgroup).reshape(-1, seq_len)
     normed = (normalize(whole.astype(jnp.float32), 0) * norm_gain[:, None]).astype(jnp.bfloat16)
     project = lax.dot_general(
@@ -60,28 +76,29 @@
     ).astype(jnp.bfloat16)
     mlp_hidden = jax.nn.gelu(project[3 * head :] + mlp_bias[:, None], approximate=False)
     hidden = jnp.concatenate([attended, mlp_hidden.astype(jnp.bfloat16)], axis=0)
-    part = jnp.dot(w_outT, hidden, preferred_element_type=jnp.float32).astype(jnp.bfloat16)
-    summed = lax.psum_scatter(part, "y", scatter_dimension=0, tiled=True)
-    pieces = lax.all_to_all(summed.reshape(NZ, local_width, seq_len), "zh", 0, 0)
+    hidden_all = gather_y(hidden)
+    part = jnp.zeros((NZ * local_width, seq_len), jnp.float32)
+    for i in range(NY):
+        part = part + jnp.dot(w_rows[i], hidden_all[i], preferred_element_type=jnp.float32)
+    part = part.astype(jnp.bfloat16).reshape(NZ, local_width, seq_len)
+    pieces = lax.all_to_all(part, "zh", 0, 0)
     total = jnp.sum(pieces.astype(jnp.float32), axis=0)
     result = mine.astype(jnp.float32) + total + out_bias[:, None]
     return result.astype(jnp.bfloat16).T[None]
 
 
 def solution(mesh):
-    fine = Mesh(mesh.devices.reshape(4, 4, 2, NY, NZ), ("x", "zl", "c", "y", "zh"))
-    dp = ("x", "zl", "c")
-    mp = ("y", "zh")
+    fine = Mesh(mesh.devices.reshape(NX, 2, 2, 2, NY, NZ), AXES)
     in_specs = (
-        P(dp, None, mp),
+        P(DP, None, MP),
         P(),
-        P(None, mp),
-        P(mp, None),
-        P(mp, None),
-        P(mp),
-        P(mp, dp),
-        P(mp),
+        P(None, MP),
+        P(MP, None),
+        P(MP, None),
+        P(MP),
+        P(MP, DP),
+        P(MP),
     )
     return jax.shard_map(
-        per_device, mesh=fine, in_specs=in_specs, out_specs=P(dp, None, mp), check_vma=False
+        per_device, mesh=fine, in_specs=in_specs, out_specs=P(DP, None, MP), check_vma=False
     )

time: 205 us -> 205 us (level)
  the two profiles are of different devices: /device:TPU:66 before, /device:TPU:88 now
where the time goes in v2:
time: 205 us; the launch traced here: 204 us
  starting transfers between devices  66.8 us (33%)
  blocking collectives  61.3 us (30%)
  waiting for transfers between devices  43.5 us (21%)
  between operations  14 us (7%)
  matrix products  11.5 us (6%)
  other arithmetic  5.05 us (2%)
    ppermute x16, starting transfers between devices, shift(): lax.ppermute(value, axis, [(i, (i + by) % count) for i in range(count)])  60.1 us
    ppermute x16, waiting for transfers between devices, shift(): lax.ppermute(value, axis, [(i, (i + by) % count) for i in range(count)])  32.6 us
    all_to_all x1, blocking collectives, per_device(): pieces = lax.all_to_all(part, 'zh', 0, 0)  31.3 us
    all_gather x1, blocking collectives, per_device(): zgroup = lax.all_gather(mine, 'zh', axis=0, tiled=True)  30 us
    ppermute x1, waiting for transfers between devices, gather_out_weights(): swapped = lax.ppermute(w_out.T, ('x', 'zlh', 'zll', 'c', 'y'), pairs)  10.8 us
    dot_general x8, matrix products, per_device(): jnp.dot(w_rows[i], hidden_all[i], preferred_element_type=jnp.float32)  8.3 us
    ppermute x1, starting transfers between devices, gather_out_weights(): swapped = lax.ppermute(w_out.T, ('x', 'zlh', 'zll', 'c', 'y'), pairs)  6.66 us
  transfers between devices with their start and end apart: 18, of which 14 were waited for; matrix products, arithmetic and copies ran while one was open for 4% of the time, Pallas kernels for 0%

profile of v2, /device:TPU:88, one launch (start us, length us, event | category | flops | bytes accessed | tf_op | source)
XLA Modules:
  0.0 203.9 jit_solution(1727858408532788911)
XLA Ops:
  6.5 6.7 %collective-permute-start.16 = (bf16[192,512]{1,0:T(8,128)(2,1)}, bf16[192,512]{1,0:T(8,128)(2,1)S(1)}, u32[]{:S(2)}, u32[]{:S(2)}) collective-permute-start(bf16[192,512]{1,0:T(8,128)(2,1)} %bitcast.98), channel_id=1, source_target_pairs={{0,0},{4,128},{8,256},{12,384},{16,512},{20,640},{24,768},{28,896}... | collective-permute-start | bytes 589832 | tf_op jit(solution)/shard_map/ppermute | solution.py:54
  13.2 10.8 %collective-permute-done.16 = bf16[192,512]{1,0:T(8,128)(2,1)S(1)} collective-permute-done((bf16[192,512]{1,0:T(8,128)(2,1)}, bf16[192,512]{1,0:T(8,128)(2,1)S(1)}, u32[]{:S(2)}, u32[]{:S(2)}) %collective-permute-start.16) | collective-permute-done | bytes 196640 | tf_op jit(solution)/shard_map/ppermute | solution.py:54
  24.0 0.7 copy-done.2
  24.7 0.0 all-gather.2.cloned.1.call-update
  24.7 30.0 %all_gather.6 = bf16[768,256]{1,0:T(8,128)(2,1)S(1)} all-gather(bf16[192,256]{1,0:T(8,128)(2,1)} %bitcast.95), channel_id=1, replica_groups=mesh['x'=4,'zlh'=2,'zll'=2,'c'=2,'y'=8,'zh'=4] {'zh'}, dimensions={0}, use_global_device_ids=true | all-gather | bytes 491520 | tf_op jit(solution)/shard_map/all_gather | solution.py:62
  54.7 8.7 %collective-permute-start = (bf16[768,256]{1,0:T(8,128)(2,1)S(1)}, bf16[768,256]{1,0:T(8,128)(2,1)S(1)}, u32[]{:S(2)}, u32[]{:S(2)}) collective-permute-start(bf16[768,256]{1,0:T(8,128)(2,1)S(1)} %all_gather.6), channel_id=1, source_target_pairs={{0,4},{4,8},{8,12},{12,16},{16,20},{20,24},{24,28},{28,0},{1,5},{5... | collective-permute-start | bytes 1179656 | tf_op jit(solution)/shard_map/ppermute | solution.py:23
  63.4 1.9 collective-permute-start.1
  65.4 0.0 slice-start
  65.4 0.2 broadcast_in_dim.75
  65.7 3.3 %collective-permute-done = bf16[768,256]{1,0:T(8,128)(2,1)S(1)} collective-permute-done((bf16[768,256]{1,0:T(8,128)(2,1)S(1)}, bf16[768,256]{1,0:T(8,128)(2,1)S(1)}, u32[]{:S(2)}, u32[]{:S(2)}) %collective-permute-start) | collective-permute-done | bytes 393248 | tf_op jit(solution)/shard_map/ppermute | solution.py:23
  69.0 5.6 %collective-permute-start.2 = (bf16[768,256]{1,0:T(8,128)(2,1)S(1)}, bf16[768,256]{1,0:T(8,128)(2,1)S(1)}, u32[]{:S(2)}, u32[]{:S(2)}) collective-permute-start(bf16[768,256]{1,0:T(8,128)(2,1)S(1)} %collective-permute-done), channel_id=1, source_target_pairs={{0,4},{4,8},{8,12},{12,16},{16,20},{20,24},{24,28},{28,0},{1,5},{5... | collective-permute-start | bytes 1179656 | tf_op jit(solution)/shard_map/ppermute | solution.py:23
  74.6 1.9 collective-permute-start.3
  76.6 3.3 %collective-permute-done.2 = bf16[768,256]{1,0:T(8,128)(2,1)S(1)} collective-permute-done((bf16[768,256]{1,0:T(8,128)(2,1)S(1)}, bf16[768,256]{1,0:T(8,128)(2,1)S(1)}, u32[]{:S(2)}, u32[]{:S(2)}) %collective-permute-start.2) | collective-permute-done | bytes 393248 | tf_op jit(solution)/shard_map/ppermute | solution.py:23
  79.8 5.6 %collective-permute-start.4 = (bf16[768,256]{1,0:T(8,128)(2,1)S(1)}, bf16[768,256]{1,0:T(8,128)(2,1)S(1)}, u32[]{:S(2)}, u32[]{:S(2)}) collective-permute-start(bf16[768,256]{1,0:T(8,128)(2,1)S(1)} %collective-permute-done.2), channel_id=1, source_target_pairs={{0,4},{4,8},{8,12},{12,16},{16,20},{20,24},{24,28},{28,0},{1,5},{5... | collective-permute-start | bytes 1179656 | tf_op jit(solution)/shard_map/ppermute | solution.py:23
  85.4 0.0 collective-permute-done.3
  85.5 1.9 collective-permute-start.5
  87.5 3.4 %collective-permute-done.4 = bf16[768,256]{1,0:T(8,128)(2,1)S(1)} collective-permute-done((bf16[768,256]{1,0:T(8,128)(2,1)S(1)}, bf16[768,256]{1,0:T(8,128)(2,1)S(1)}, u32[]{:S(2)}, u32[]{:S(2)}) %collective-permute-start.4) | collective-permute-done | bytes 393248 | tf_op jit(solution)/shard_map/ppermute | solution.py:23
  90.9 0.0 slice-start.1
  90.9 5.9 %collective-permute-start.6 = (bf16[384,256]{1,0:T(8,128)(2,1)S(1)}, bf16[384,256]{1,0:T(8,128)(2,1)S(1)}, u32[]{:S(2)}, u32[]{:S(2)}) collective-permute-start(bf16[384,256]{1,0:T(8,128)(2,1)S(1)} %slice.105), channel_id=1, source_target_pairs={{0,4},{4,8},{8,12},{12,16},{16,20},{20,24},{24,28},{28,0},{1,5},{5... | collective-permute-start | bytes 589832 | tf_op jit(solution)/shard_map/ppermute | solution.py:23
  96.8 1.9 collective-permute-start.7
  98.8 1.1 collective-permute-done.6
  99.9 5.6 %collective-permute-done.7 = bf16[384,256]{1,0:T(8,128)(2,1)S(1)} collective-permute-done((bf16[384,256]{1,0:T(8,128)(2,1)S(1)}, bf16[384,256]{1,0:T(8,128)(2,1)S(1)}, u32[]{:S(2)}, u32[]{:S(2)}) %collective-permute-start.7) | collective-permute-done | bytes 196640 | tf_op jit(solution)/shard_map/ppermute | solution.py:23
  105.6 0.8 convert_reduce_fusion
  106.4 0.9 multiply_reduce_fusion
  107.3 1.1 fusion.2
  108.5 0.0 copy-start.6
  108.5 2.6 %convolution_bitcast_fusion = f32[768,256]{0,1:T(8,128)S(1)} fusion(bf16[6144,256]{1,0:T(8,128)(2,1)S(1)} %fusion.2, bf16[6144,768]{1,0:T(8,128)(2,1)S(1)} %bitcast.93), kind=kOutput, calls=%fused_computation.6 | convolution fusion | flops 2415919104 | bytes 13369344 | tf_op jit(solution)/shard_map/dot_general | solution.py:65
  111.2 0.1 slice_reduce_fusion.1
  111.3 0.3 multiply_reduce_fusion.2
  111.6 0.3 fusion.50
  112.0 0.1 fusion.36
  112.0 0.2 convolution_convert_fusion
  112.3 0.9 fusion.28
  113.2 1.9 collective-permute-start.8
  115.1 3.9 %collective-permute-start.9 = (bf16[512,256]{0,1:T(8,128)(2,1)S(1)}, bf16[512,256]{0,1:T(8,128)(2,1)S(1)}, u32[]{:S(2)}, u32[]{:S(2)}) collective-permute-start(bf16[512,256]{0,1:T(8,128)(2,1)S(1)} %pad_maximum_fusion), channel_id=1, source_target_pairs={{0,28},{4,0},{8,4},{12,8},{16,12},{20,16},{24,20},{28,24},{1,29},{... | collective-permute-start | bytes 786440 | tf_op jit(solution)/shard_map/ppermute | solution.py:23
  119.1 0.2 broadcast_in_dim.74
  119.3 3.8 %collective-permute-done.8 = bf16[512,256]{0,1:T(8,128)(2,1)S(1)} collective-permute-done((bf16[512,256]{0,1:T(8,128)(2,1)S(1)}, bf16[512,256]{0,1:T(8,128)(2,1)S(1)}, u32[]{:S(2)}, u32[]{:S(2)}) %collective-permute-start.8) | collective-permute-done | bytes 262176 | tf_op jit(solution)/shard_map/ppermute | solution.py:23
  123.1 3.9 %collective-permute-start.10 = (bf16[512,256]{0,1:T(8,128)(2,1)S(1)}, bf16[512,256]{0,1:T(8,128)(2,1)S(1)}, u32[]{:S(2)}, u32[]{:S(2)}) collective-permute-start(bf16[512,256]{0,1:T(8,128)(2,1)S(1)} %collective-permute-done.8), channel_id=1, source_target_pairs={{0,4},{4,8},{8,12},{12,16},{16,20},{20,24},{24,28},{28,0},{1,5},{5... | collective-permute-start | bytes 786440 | tf_op jit(solution)/shard_map/ppermute | solution.py:23
  127.1 0.3 collective-permute-done.9
  127.3 1.9 collective-permute-start.11
  129.3 3.6 %collective-permute-done.10 = bf16[512,256]{0,1:T(8,128)(2,1)S(1)} collective-permute-done((bf16[512,256]{0,1:T(8,128)(2,1)S(1)}, bf16[512,256]{0,1:T(8,128)(2,1)S(1)}, u32[]{:S(2)}, u32[]{:S(2)}) %collective-permute-start.10) | collective-permute-done | bytes 262176 | tf_op jit(solution)/shard_map/ppermute | solution.py:23
  132.9 5.6 %collective-permute-start.12 = (bf16[512,256]{0,1:T(8,128)(2,1)S(1)}, bf16[512,256]{0,1:T(8,128)(2,1)S(1)}, u32[]{:S(2)}, u32[]{:S(2)}) collective-permute-start(bf16[512,256]{0,1:T(8,128)(2,1)S(1)} %collective-permute-done.10), channel_id=1, source_target_pairs={{0,4},{4,8},{8,12},{12,16},{16,20},{20,24},{24,28},{28,0},{1,5},{5... | collective-permute-start | bytes 786440 | tf_op jit(solution)/shard_map/ppermute | solution.py:23
  138.5 0.2 collective-permute-done.11
  138.8 1.9 collective-permute-start.13
  140.7 1.6 collective-permute-done.12
  142.4 5.6 %collective-permute-start.14 = (bf16[256,256]{0,1:T(8,128)(2,1)S(1)}, bf16[256,256]{0,1:T(8,128)(2,1)S(1)}, u32[]{:S(2)}, u32[]{:S(2)}) collective-permute-start(bf16[256,256]{0,1:T(8,128)(2,1)S(1)} %slice.111), channel_id=1, source_target_pairs={{0,4},{4,8},{8,12},{12,16},{16,20},{20,24},{24,28},{28,0},{1,5},{5... | collective-permute-start | bytes 393224 | tf_op jit(solution)/shard_map/ppermute | solution.py:23
  148.0 0.2 collective-permute-done.13
  148.2 1.9 collective-permute-start.15
  150.2 0.3 collective-permute-done.14
  150.5 5.8 %collective-permute-done.15 = bf16[256,256]{0,1:T(8,128)(2,1)S(1)} collective-permute-done((bf16[256,256]{0,1:T(8,128)(2,1)S(1)}, bf16[256,256]{0,1:T(8,128)(2,1)S(1)}, u32[]{:S(2)}, u32[]{:S(2)}) %collective-permute-start.15) | collective-permute-done | bytes 131104 | tf_op jit(solution)/shard_map/ppermute | solution.py:23
  156.3 0.0 all-gather.2.cloned.1.call-done
  156.4 1.7 fusion.13
  158.1 1.9 fusion.15
  159.9 1.5 fusion.17
  161.5 1.5 fusion.19
  163.0 0.4 fusion.21
  163.4 0.4 fusion.23
  163.8 0.4 fusion.11
  164.2 0.0 copy-start.1
  164.2 0.0 copy-start.5
  164.3 0.5 fusion.10
  164.8 0.2 copy.11
  164.9 31.3 %all_to_all.5 = bf16[4,192,256]{2,1,0:T(8,128)(2,1)S(1)} all-to-all(bf16[4,192,256]{2,1,0:T(8,128)(2,1)S(1)} %bitcast.94), channel_id=1, replica_groups=mesh['x'=4,'zlh'=2,'zll'=2,'c'=2,'y'=8,'zh'=4] {'zh'}, dimensions={0} | all-to-all | bytes 786432 | tf_op jit(solution)/shard_map/all_to_all | solution.py:84
  196.3 0.7 fusion.43
  (49 shorter events, 0.7 us)
Async XLA Ops:
  6.5 149.8 %all-gather.2.cloned.1.call-start = ((), (), s32[]{:S(2)}) async-start(), calls=%async_computation.1 | async-start | bytes 6488064 | tf_op jit(solution)/shard_map/all_gather | solution.py:55
  6.5 17.5 %collective-permute-start.16 = (bf16[192,512]{1,0:T(8,128)(2,1)}, bf16[192,512]{1,0:T(8,128)(2,1)S(1)}, u32[]{:S(2)}, u32[]{:S(2)}) collective-permute-start(bf16[192,512]{1,0:T(8,128)(2,1)} %bitcast.98), channel_id=1, source_target_pairs={{0,0},{4,128},{8,256},{12,384},{16,512},{20,640},{24,768},{28,896}... | collective-permute-start | bytes 589832 | tf_op jit(solution)/shard_map/ppermute | solution.py:54
  24.0 0.7 copy-start.2
  54.7 14.3 %collective-permute-start = (bf16[768,256]{1,0:T(8,128)(2,1)S(1)}, bf16[768,256]{1,0:T(8,128)(2,1)S(1)}, u32[]{:S(2)}, u32[]{:S(2)}) collective-permute-start(bf16[768,256]{1,0:T(8,128)(2,1)S(1)} %all_gather.6), channel_id=1, source_target_pairs={{0,4},{4,8},{8,12},{12,16},{16,20},{20,24},{24,28},{28,0},{1,5},{5... | collective-permute-start | bytes 1179656 | tf_op jit(solution)/shard_map/ppermute | solution.py:23
  63.4 11.1 %collective-permute-start.1 = (bf16[768,256]{1,0:T(8,128)(2,1)S(1)}, bf16[768,256]{1,0:T(8,128)(2,1)S(1)}, u32[]{:S(2)}, u32[]{:S(2)}) collective-permute-start(bf16[768,256]{1,0:T(8,128)(2,1)S(1)} %all_gather.6), channel_id=1, source_target_pairs={{0,28},{4,0},{8,4},{12,8},{16,12},{20,16},{24,20},{28,24},{1,29},{... | collective-permute-start | bytes 1179656 | tf_op jit(solution)/shard_map/ppermute | solution.py:23
  65.4 43.1 %slice-start = ((s8[9437184]{0:T(1024)(128)(4,1)}), s8[4194304]{0:T(1024)(128)(4,1)S(1)}, s32[]{:S(2)}) async-start(s8[9437184]{0:T(1024)(128)(4,1)} %bitcast.92), calls=%async_computation.2 | async-start | bytes 8388608
  69.0 10.9 %collective-permute-start.2 = (bf16[768,256]{1,0:T(8,128)(2,1)S(1)}, bf16[768,256]{1,0:T(8,128)(2,1)S(1)}, u32[]{:S(2)}, u32[]{:S(2)}) collective-permute-start(bf16[768,256]{1,0:T(8,128)(2,1)S(1)} %collective-permute-done), channel_id=1, source_target_pairs={{0,4},{4,8},{8,12},{12,16},{16,20},{20,24},{24,28},{28,0},{1,5},{5... | collective-permute-start | bytes 1179656 | tf_op jit(solution)/shard_map/ppermute | solution.py:23
  74.6 10.9 %collective-permute-start.3 = (bf16[768,256]{1,0:T(8,128)(2,1)S(1)}, bf16[768,256]{1,0:T(8,128)(2,1)S(1)}, u32[]{:S(2)}, u32[]{:S(2)}) collective-permute-start(bf16[768,256]{1,0:T(8,128)(2,1)S(1)} %collective-permute-done.1), channel_id=1, source_target_pairs={{0,28},{4,0},{8,4},{12,8},{16,12},{20,16},{24,20},{28,24},{1,29},{... | collective-permute-start | bytes 1179656 | tf_op jit(solution)/shard_map/ppermute | solution.py:23
  79.8 11.0 %collective-permute-start.4 = (bf16[768,256]{1,0:T(8,128)(2,1)S(1)}, bf16[768,256]{1,0:T(8,128)(2,1)S(1)}, u32[]{:S(2)}, u32[]{:S(2)}) collective-permute-start(bf16[768,256]{1,0:T(8,128)(2,1)S(1)} %collective-permute-done.2), channel_id=1, source_target_pairs={{0,4},{4,8},{8,12},{12,16},{16,20},{20,24},{24,28},{28,0},{1,5},{5... | collective-permute-start | bytes 1179656 | tf_op jit(solution)/shard_map/ppermute | solution.py:23
  85.5 11.3 %collective-permute-start.5 = (bf16[768,256]{1,0:T(8,128)(2,1)S(1)}, bf16[768,256]{1,0:T(8,128)(2,1)S(1)}, u32[]{:S(2)}, u32[]{:S(2)}) collective-permute-start(bf16[768,256]{1,0:T(8,128)(2,1)S(1)} %collective-permute-done.3), channel_id=1, source_target_pairs={{0,28},{4,0},{8,4},{12,8},{16,12},{20,16},{24,20},{28,24},{1,29},{... | collective-permute-start | bytes 1179656 | tf_op jit(solution)/shard_map/ppermute | solution.py:23
  90.9 17.6 %slice-start.1 = ((s8[9437184]{0:T(1024)(128)(4,1)}), s8[4194304]{0:T(1024)(128)(4,1)S(1)}, s32[]{:S(2)}) async-start(s8[9437184]{0:T(1024)(128)(4,1)} %bitcast.92), calls=%async_computation.3 | async-start | bytes 8388608
  90.9 9.0 %collective-permute-start.6 = (bf16[384,256]{1,0:T(8,128)(2,1)S(1)}, bf16[384,256]{1,0:T(8,128)(2,1)S(1)}, u32[]{:S(2)}, u32[]{:S(2)}) collective-permute-start(bf16[384,256]{1,0:T(8,128)(2,1)S(1)} %slice.105), channel_id=1, source_target_pairs={{0,4},{4,8},{8,12},{12,16},{16,20},{20,24},{24,28},{28,0},{1,5},{5... | collective-permute-start | bytes 589832 | tf_op jit(solution)/shard_map/ppermute | solution.py:23
  96.8 8.8 %collective-permute-start.7 = (bf16[384,256]{1,0:T(8,128)(2,1)S(1)}, bf16[384,256]{1,0:T(8,128)(2,1)S(1)}, u32[]{:S(2)}, u32[]{:S(2)}) collective-permute-start(bf16[384,256]{1,0:T(8,128)(2,1)S(1)} %slice.106), channel_id=1, source_target_pairs={{0,28},{4,0},{8,4},{12,8},{16,12},{20,16},{24,20},{28,24},{1,29},{... | collective-permute-start | bytes 589832 | tf_op jit(solution)/shard_map/ppermute | solution.py:23
  105.6 1.7 copy-start.3
  106.4 2.1 %slice-start.2 = ((s8[9437184]{0:T(1024)(128)(4,1)}), s8[1048576]{0:T(1024)(128)(4,1)S(1)}, s32[]{:S(2)}) async-start(s8[9437184]{0:T(1024)(128)(4,1)} %bitcast.92), calls=%async_computation.4 | async-start | bytes 2097152
  108.5 3.1 %copy-start.6 = (f32[1,128]{1,0:T(1,128)S(1)}, f32[1,128]{1,0:T(1,128)}, u32[]{:S(2)}) copy-start(f32[1,128]{1,0:T(1,128)} %param.12) | copy-start | bytes 1540
  108.5 3.1 %copy-start.7 = (f32[1,128]{1,0:T(1,128)S(1)}, f32[1,128]{1,0:T(1,128)}, u32[]{:S(2)}) copy-start(f32[1,128]{1,0:T(1,128)} %param.11) | copy-start | bytes 1540
  108.5 3.8 %copy-start.4 = (f32[384]{0:T(512)S(1)}, f32[384]{0:T(512)}, u32[]{:S(2)}) copy-start(f32[384]{0:T(512)} %param.13) | copy-start | bytes 4612
  113.2 9.9 %collective-permute-start.8 = (bf16[512,256]{0,1:T(8,128)(2,1)S(1)}, bf16[512,256]{0,1:T(8,128)(2,1)S(1)}, u32[]{:S(2)}, u32[]{:S(2)}) collective-permute-start(bf16[512,256]{0,1:T(8,128)(2,1)S(1)} %pad_maximum_fusion), channel_id=1, source_target_pairs={{0,4},{4,8},{8,12},{12,16},{16,20},{20,24},{24,28},{28,0},{1,5},{5... | collective-permute-start | bytes 786440 | tf_op jit(solution)/shard_map/ppermute | solution.py:23
  115.1 12.2 %collective-permute-start.9 = (bf16[512,256]{0,1:T(8,128)(2,1)S(1)}, bf16[512,256]{0,1:T(8,128)(2,1)S(1)}, u32[]{:S(2)}, u32[]{:S(2)}) collective-permute-start(bf16[512,256]{0,1:T(8,128)(2,1)S(1)} %pad_maximum_fusion), channel_id=1, source_target_pairs={{0,28},{4,0},{8,4},{12,8},{16,12},{20,16},{24,20},{28,24},{1,29},{... | collective-permute-start | bytes 786440 | tf_op jit(solution)/shard_map/ppermute | solution.py:23
  123.1 9.8 %collective-permute-start.10 = (bf16[512,256]{0,1:T(8,128)(2,1)S(1)}, bf16[512,256]{0,1:T(8,128)(2,1)S(1)}, u32[]{:S(2)}, u32[]{:S(2)}) collective-permute-start(bf16[512,256]{0,1:T(8,128)(2,1)S(1)} %collective-permute-done.8), channel_id=1, source_target_pairs={{0,4},{4,8},{8,12},{12,16},{16,20},{20,24},{24,28},{28,0},{1,5},{5... | collective-permute-start | bytes 786440 | tf_op jit(solution)/shard_map/ppermute | solution.py:23
  127.3 11.4 %collective-permute-start.11 = (bf16[512,256]{0,1:T(8,128)(2,1)S(1)}, bf16[512,256]{0,1:T(8,128)(2,1)S(1)}, u32[]{:S(2)}, u32[]{:S(2)}) collective-permute-start(bf16[512,256]{0,1:T(8,128)(2,1)S(1)} %collective-permute-done.9), channel_id=1, source_target_pairs={{0,28},{4,0},{8,4},{12,8},{16,12},{20,16},{24,20},{28,24},{1,29},{... | collective-permute-start | bytes 786440 | tf_op jit(solution)/shard_map/ppermute | solution.py:23
  132.9 9.5 %collective-permute-start.12 = (bf16[512,256]{0,1:T(8,128)(2,1)S(1)}, bf16[512,256]{0,1:T(8,128)(2,1)S(1)}, u32[]{:S(2)}, u32[]{:S(2)}) collective-permute-start(bf16[512,256]{0,1:T(8,128)(2,1)S(1)} %collective-permute-done.10), channel_id=1, source_target_pairs={{0,4},{4,8},{8,12},{12,16},{16,20},{20,24},{24,28},{28,0},{1,5},{5... | collective-permute-start | bytes 786440 | tf_op jit(solution)/shard_map/ppermute | solution.py:23
  138.8 9.5 %collective-permute-start.13 = (bf16[512,256]{0,1:T(8,128)(2,1)S(1)}, bf16[512,256]{0,1:T(8,128)(2,1)S(1)}, u32[]{:S(2)}, u32[]{:S(2)}) collective-permute-start(bf16[512,256]{0,1:T(8,128)(2,1)S(1)} %collective-permute-done.11), channel_id=1, source_target_pairs={{0,28},{4,0},{8,4},{12,8},{16,12},{20,16},{24,20},{28,24},{1,29},{... | collective-permute-start | bytes 786440 | tf_op jit(solution)/shard_map/ppermute | solution.py:23
  142.4 8.1 %collective-permute-start.14 = (bf16[256,256]{0,1:T(8,128)(2,1)S(1)}, bf16[256,256]{0,1:T(8,128)(2,1)S(1)}, u32[]{:S(2)}, u32[]{:S(2)}) collective-permute-start(bf16[256,256]{0,1:T(8,128)(2,1)S(1)} %slice.111), channel_id=1, source_target_pairs={{0,4},{4,8},{8,12},{12,16},{16,20},{20,24},{24,28},{28,0},{1,5},{5... | collective-permute-start | bytes 393224 | tf_op jit(solution)/shard_map/ppermute | solution.py:23
  148.2 8.1 %collective-permute-start.15 = (bf16[256,256]{0,1:T(8,128)(2,1)S(1)}, bf16[256,256]{0,1:T(8,128)(2,1)S(1)}, u32[]{:S(2)}, u32[]{:S(2)}) collective-permute-start(bf16[256,256]{0,1:T(8,128)(2,1)S(1)} %slice.112), channel_id=1, source_target_pairs={{0,28},{4,0},{8,4},{12,8},{16,12},{20,16},{24,20},{28,24},{1,29},{... | collective-permute-start | bytes 393224 | tf_op jit(solution)/shard_map/ppermute | solution.py:23
  156.4 6.7 %copy-start = (bf16[6144,512]{1,0:T(8,128)(2,1)S(1)}, bf16[6144,512]{1,0:T(8,128)(2,1)}, u32[]{:S(2)}) copy-start(bf16[6144,512]{1,0:T(8,128)(2,1)} %all-gather.2.cloned.1.call-done) | copy-start | bytes 18874372
  164.2 32.1 %copy-start.1 = (bf16[1,256,192]{1,2,0:T(8,128)(2,1)S(1)}, bf16[1,256,192]{1,2,0:T(8,128)(2,1)}, u32[]{:S(2)}) copy-start(bf16[1,256,192]{1,2,0:T(8,128)(2,1)} %param.8) | copy-start | bytes 294916
  164.2 32.1 %copy-start.5 = (f32[192]{0:T(256)S(1)}, f32[192]{0:T(256)}, u32[]{:S(2)}) copy-start(f32[192]{0:T(256)} %param.15) | copy-start | bytes 2308
Sparse Core Ops, SparseCore 0:
  24.9 85.5 all-gather.1

commit v3 on v2

--- a/solution.py
+++ b/solution.py
@@ -1,6 +1,8 @@
 import jax
 import jax.numpy as jnp
 from jax import lax
+from jax.experimental import pallas as pl
+from jax.experimental.pallas import tpu as pltpu
 from jax.sharding import Mesh
 from jax.sharding import PartitionSpec as P
 
@@ -55,11 +57,50 @@
     return lax.all_gather(swapped, DP, axis=0, tiled=True).reshape(NY, -1, depth)
 
 
+def multiply_out(weights, hidden):
+    count, rows, depth = weights.shape
+    columns = hidden.shape[2]
+
+    def kernel(w_ref, h_ref, o_ref, total_ref):
+        step = pl.program_id(0)
+        product = jnp.dot(w_ref[0], h_ref[0], preferred_element_type=jnp.float32)
+
+        @pl.when(step == 0)
+        def _():
+            total_ref[...] = product
+
+        @pl.when(step > 0)
+        def _():
+            total_ref[...] += product
+
+        @pl.when(step == count - 1)
+        def _():
+            o_ref[...] = total_ref[...].astype(o_ref.dtype)
+
+    return pl.pallas_call(
+        kernel,
+        grid=(count,),
+        in_specs=[
+            pl.BlockSpec((1, rows, depth), lambda i: (i, 0, 0)),
+            pl.BlockSpec((1, depth, columns), lambda i: (i, 0, 0)),
+        ],
+        out_specs=pl.BlockSpec((rows, columns), lambda i: (0, 0)),
+        out_shape=jax.ShapeDtypeStruct((rows, columns), jnp.bfloat16),
+        scratch_shapes=[pltpu.VMEM((rows, columns), jnp.float32)],
+        compiler_params=pltpu.CompilerParams(vmem_limit_bytes=56 * 1024 * 1024),
+        cost_estimate=pl.CostEstimate(
+            flops=2 * count * rows * depth * columns,
+            bytes_accessed=2 * count * depth * (rows + columns),
+            transcendentals=0,
+        ),
+    )(weights, hidden)
+
+
 def per_device(patches, norm_gain, w_in, q_gain, k_gain, mlp_bias, w_out, out_bias):
     images, seq_len, local_width = patches.shape
     mine = patches[0].T
-    w_rows = gather_out_weights(w_out)
     zgroup = lax.all_gather(mine, "zh", axis=0, tiled=True)
+    w_rows = gather_out_weights(w_out + zgroup[0, 0] * 0)
     whole = gather_y(zgroup).reshape(-1, seq_len)
     normed = (normalize(whole.astype(jnp.float32), 0) * norm_gain[:, None]).astype(jnp.bfloat16)
     project = lax.dot_general(
@@ -77,10 +118,7 @@
     mlp_hidden = jax.nn.gelu(project[3 * head :] + mlp_bias[:, None], approximate=False)
     hidden = jnp.concatenate([attended, mlp_hidden.astype(jnp.bfloat16)], axis=0)
     hidden_all = gather_y(hidden)
-    part = jnp.zeros((NZ * local_width, seq_len), jnp.float32)
-    for i in range(NY):
-        part = part + jnp.dot(w_rows[i], hidden_all[i], preferred_element_type=jnp.float32)
-    part = part.astype(jnp.bfloat16).reshape(NZ, local_width, seq_len)
+    part = multiply_out(w_rows, hidden_all).reshape(NZ, local_width, seq_len)
     pieces = lax.all_to_all(part, "zh", 0, 0)
     total = jnp.sum(pieces.astype(jnp.float32), axis=0)
     result = mine.astype(jnp.float32) + total + out_bias[:, None]

time: 205 us -> 206 us (level)
  the two profiles are of different devices: /device:TPU:88 before, /device:TPU:26 now
where the time goes in v3:
time: 206 us
  starting transfers between devices  65.3 us (32%)
  blocking collectives  61.2 us (30%)
  waiting for transfers between devices  42.8 us (21%)
  between operations  14.6 us (7%)
  Pallas kernels  8.04 us (4%)
  other arithmetic  5.76 us (3%)
  matrix products  4.33 us (2%)
  local copies, waits for them, and re-layouts  3.39 us (2%)
    ppermute x16, starting transfers between devices, shift(): lax.ppermute(value, axis, [(i, (i + by) % count) for i in range(count)])  60.8 us
    ppermute x16, waiting for transfers between devices, shift(): lax.ppermute(value, axis, [(i, (i + by) % count) for i in range(count)])  34.6 us
    all_gather x1, blocking collectives, per_device(): zgroup = lax.all_gather(mine, 'zh', axis=0, tiled=True)  34.2 us
    all_to_all x1, blocking collectives, per_device(): pieces = lax.all_to_all(part, 'zh', 0, 0)  26.9 us
    ppermute x1, waiting for transfers between devices, gather_out_weights(): swapped = lax.ppermute(w_out.T, ('x', 'zlh', 'zll', 'c', 'y'), pairs)  8.19 us
    pallas_call x1, Pallas kernels, multiply_out(): pl.pallas_call(kernel, grid=(count,), in_specs=[pl.BlockSpec((1, rows, de...  8.04 us
    ppermute x1, starting transfers between devices, gather_out_weights(): swapped = lax.ppermute(w_out.T, ('x', 'zlh', 'zll', 'c', 'y'), pairs)  4.58 us
  transfers between devices with their start and end apart: 18, of which 11 were waited for; matrix products, arithmetic and copies ran while one was open for 4% of the time, Pallas kernels for 0%

profile of v3, /device:TPU:26, one launch (start us, length us, event | category | flops | bytes accessed | tf_op | source)
XLA Modules:
  0.0 205.5 jit_solution(13270765399934821012)
XLA Ops:
  6.5 0.0 all-gather.2.cloned.1.call-start
  6.5 34.2 %all_gather.6 = bf16[768,256]{1,0:T(8,128)(2,1)S(1)} all-gather(bf16[192,256]{1,0:T(8,128)(2,1)} %bitcast.71), channel_id=1, replica_groups=mesh['x'=4,'zlh'=2,'zll'=2,'c'=2,'y'=8,'zh'=4] {'zh'}, dimensions={0}, use_global_device_ids=true | all-gather | bytes 491520 | tf_op jit(solution)/shard_map/all_gather | solution.py:102
  40.8 0.5 slice.37
  41.9 0.9 add_bitcast_fusion
  42.9 4.6 %collective-permute-start = (bf16[192,512]{1,0:T(8,128)(2,1)S(1)}, bf16[192,512]{1,0:T(8,128)(2,1)S(1)}, u32[]{:S(2)}, u32[]{:S(2)}) collective-permute-start(bf16[192,512]{1,0:T(8,128)(2,1)S(1)} %add_bitcast_fusion), channel_id=1, source_target_pairs={{0,0},{4,128},{8,256},{12,384},{16,512},{20,640},{24,768},{28,896}... | collective-permute-start | bytes 589832 | tf_op jit(solution)/shard_map/ppermute | solution.py:56
  47.5 8.2 %collective-permute-done = bf16[192,512]{1,0:T(8,128)(2,1)S(1)} collective-permute-done((bf16[192,512]{1,0:T(8,128)(2,1)S(1)}, bf16[192,512]{1,0:T(8,128)(2,1)S(1)}, u32[]{:S(2)}, u32[]{:S(2)}) %collective-permute-start) | collective-permute-done | bytes 196640 | tf_op jit(solution)/shard_map/ppermute | solution.py:56
  55.7 0.7 copy-done.2
  56.4 0.0 all-gather.2.cloned.1.call-update
  56.4 8.5 %collective-permute-start.1 = (bf16[768,256]{1,0:T(8,128)(2,1)S(1)}, bf16[768,256]{1,0:T(8,128)(2,1)S(1)}, u32[]{:S(2)}, u32[]{:S(2)}) collective-permute-start(bf16[768,256]{1,0:T(8,128)(2,1)S(1)} %all_gather.6), channel_id=1, source_target_pairs={{0,4},{4,8},{8,12},{12,16},{16,20},{20,24},{24,28},{28,0},{1,5},{5... | collective-permute-start | bytes 1179656 | tf_op jit(solution)/shard_map/ppermute | solution.py:25
  64.9 1.9 collective-permute-start.2
  66.8 0.0 slice-start
  66.8 0.2 broadcast_in_dim.75
  67.1 4.5 %collective-permute-done.1 = bf16[768,256]{1,0:T(8,128)(2,1)S(1)} collective-permute-done((bf16[768,256]{1,0:T(8,128)(2,1)S(1)}, bf16[768,256]{1,0:T(8,128)(2,1)S(1)}, u32[]{:S(2)}, u32[]{:S(2)}) %collective-permute-start.1) | collective-permute-done | bytes 393248 | tf_op jit(solution)/shard_map/ppermute | solution.py:25
  71.6 5.6 %collective-permute-start.3 = (bf16[768,256]{1,0:T(8,128)(2,1)S(1)}, bf16[768,256]{1,0:T(8,128)(2,1)S(1)}, u32[]{:S(2)}, u32[]{:S(2)}) collective-permute-start(bf16[768,256]{1,0:T(8,128)(2,1)S(1)} %collective-permute-done.1), channel_id=1, source_target_pairs={{0,4},{4,8},{8,12},{12,16},{16,20},{20,24},{24,28},{28,0},{1,5},{5... | collective-permute-start | bytes 1179656 | tf_op jit(solution)/shard_map/ppermute | solution.py:25
  77.2 0.0 collective-permute-done.2
  77.2 1.9 collective-permute-start.4
  79.2 3.7 %collective-permute-done.3 = bf16[768,256]{1,0:T(8,128)(2,1)S(1)} collective-permute-done((bf16[768,256]{1,0:T(8,128)(2,1)S(1)}, bf16[768,256]{1,0:T(8,128)(2,1)S(1)}, u32[]{:S(2)}, u32[]{:S(2)}) %collective-permute-start.3) | collective-permute-done | bytes 393248 | tf_op jit(solution)/shard_map/ppermute | solution.py:25
  82.9 5.6 %collective-permute-start.5 = (bf16[768,256]{1,0:T(8,128)(2,1)S(1)}, bf16[768,256]{1,0:T(8,128)(2,1)S(1)}, u32[]{:S(2)}, u32[]{:S(2)}) collective-permute-start(bf16[768,256]{1,0:T(8,128)(2,1)S(1)} %collective-permute-done.3), channel_id=1, source_target_pairs={{0,4},{4,8},{8,12},{12,16},{16,20},{20,24},{24,28},{28,0},{1,5},{5... | collective-permute-start | bytes 1179656 | tf_op jit(solution)/shard_map/ppermute | solution.py:25
  88.5 0.0 collective-permute-done.4
  88.5 1.9 collective-permute-start.6
  90.5 3.3 %collective-permute-done.5 = bf16[768,256]{1,0:T(8,128)(2,1)S(1)} collective-permute-done((bf16[768,256]{1,0:T(8,128)(2,1)S(1)}, bf16[768,256]{1,0:T(8,128)(2,1)S(1)}, u32[]{:S(2)}, u32[]{:S(2)}) %collective-permute-start.5) | collective-permute-done | bytes 393248 | tf_op jit(solution)/shard_map/ppermute | solution.py:25
  93.8 0.0 slice-start.1
  93.8 5.9 %collective-permute-start.7 = (bf16[384,256]{1,0:T(8,128)(2,1)S(1)}, bf16[384,256]{1,0:T(8,128)(2,1)S(1)}, u32[]{:S(2)}, u32[]{:S(2)}) collective-permute-start(bf16[384,256]{1,0:T(8,128)(2,1)S(1)} %slice.38), channel_id=1, source_target_pairs={{0,4},{4,8},{8,12},{12,16},{16,20},{20,24},{24,28},{28,0},{1,5},{5... | collective-permute-start | bytes 589832 | tf_op jit(solution)/shard_map/ppermute | solution.py:25
  99.7 0.0 collective-permute-done.6
  99.7 1.9 collective-permute-start.8
  101.7 1.1 collective-permute-done.7
  102.9 5.6 %collective-permute-done.8 = bf16[384,256]{1,0:T(8,128)(2,1)S(1)} collective-permute-done((bf16[384,256]{1,0:T(8,128)(2,1)S(1)}, bf16[384,256]{1,0:T(8,128)(2,1)S(1)}, u32[]{:S(2)}, u32[]{:S(2)}) %collective-permute-start.8) | collective-permute-done | bytes 196640 | tf_op jit(solution)/shard_map/ppermute | solution.py:25
  108.5 0.0 copy-start.3
  108.5 0.8 convert_reduce_fusion
  109.4 0.9 multiply_reduce_fusion
  110.3 0.0 copy-done.3
  110.3 1.1 fusion.2
  111.4 0.0 slice-done
  111.4 0.0 copy-start.6
  111.4 0.0 copy-start.7
  111.5 0.0 copy-start.4
  111.5 3.8 %convolution_bitcast_fusion = f32[768,256]{1,0:T(8,128)S(1)} fusion(bf16[6144,256]{1,0:T(8,128)(2,1)S(1)} %fusion.2, bf16[6144,768]{1,0:T(8,128)(2,1)S(1)} %bitcast.75), kind=kOutput, calls=%fused_computation.6 | convolution fusion | flops 2415919104 | bytes 13369344 | tf_op jit(solution)/shard_map/dot_general | solution.py:106
  115.4 0.3 fusion.27
  115.8 0.1 fusion.13
  115.8 0.2 convolution_convert_fusion
  116.0 1.0 fusion.5
  117.0 3.4 %collective-permute-start.9 = (bf16[512,256]{1,0:T(8,128)(2,1)S(1)}, bf16[512,256]{1,0:T(8,128)(2,1)S(1)}, u32[]{:S(2)}, u32[]{:S(2)}) collective-permute-start(bf16[512,256]{1,0:T(8,128)(2,1)S(1)} %pad_maximum_fusion), channel_id=1, source_target_pairs={{0,4},{4,8},{8,12},{12,16},{16,20},{20,24},{24,28},{28,0},{1,5},{5... | collective-permute-start | bytes 786440 | tf_op jit(solution)/shard_map/ppermute | solution.py:25
  120.4 2.5 %collective-permute-start.10 = (bf16[512,256]{1,0:T(8,128)(2,1)S(1)}, bf16[512,256]{1,0:T(8,128)(2,1)S(1)}, u32[]{:S(2)}, u32[]{:S(2)}) collective-permute-start(bf16[512,256]{1,0:T(8,128)(2,1)S(1)} %pad_maximum_fusion), channel_id=1, source_target_pairs={{0,28},{4,0},{8,4},{12,8},{16,12},{20,16},{24,20},{28,24},{1,29},{... | collective-permute-start | bytes 786440 | tf_op jit(solution)/shard_map/ppermute | solution.py:25
  122.9 0.1 broadcast_in_dim.74
  123.1 4.8 %collective-permute-done.9 = bf16[512,256]{1,0:T(8,128)(2,1)S(1)} collective-permute-done((bf16[512,256]{1,0:T(8,128)(2,1)S(1)}, bf16[512,256]{1,0:T(8,128)(2,1)S(1)}, u32[]{:S(2)}, u32[]{:S(2)}) %collective-permute-start.9) | collective-permute-done | bytes 262176 | tf_op jit(solution)/shard_map/ppermute | solution.py:25
  127.8 4.8 %collective-permute-start.11 = (bf16[512,256]{1,0:T(8,128)(2,1)S(1)}, bf16[512,256]{1,0:T(8,128)(2,1)S(1)}, u32[]{:S(2)}, u32[]{:S(2)}) collective-permute-start(bf16[512,256]{1,0:T(8,128)(2,1)S(1)} %collective-permute-done.9), channel_id=1, source_target_pairs={{0,4},{4,8},{8,12},{12,16},{16,20},{20,24},{24,28},{28,0},{1,5},{5... | collective-permute-start | bytes 786440 | tf_op jit(solution)/shard_map/ppermute | solution.py:25
  132.6 0.0 collective-permute-done.10
  132.6 1.9 collective-permute-start.12
  134.6 3.7 %collective-permute-done.11 = bf16[512,256]{1,0:T(8,128)(2,1)S(1)} collective-permute-done((bf16[512,256]{1,0:T(8,128)(2,1)S(1)}, bf16[512,256]{1,0:T(8,128)(2,1)S(1)}, u32[]{:S(2)}, u32[]{:S(2)}) %collective-permute-start.11) | collective-permute-done | bytes 262176 | tf_op jit(solution)/shard_map/ppermute | solution.py:25
  138.4 5.6 %collective-permute-start.13 = (bf16[512,256]{1,0:T(8,128)(2,1)S(1)}, bf16[512,256]{1,0:T(8,128)(2,1)S(1)}, u32[]{:S(2)}, u32[]{:S(2)}) collective-permute-start(bf16[512,256]{1,0:T(8,128)(2,1)S(1)} %collective-permute-done.11), channel_id=1, source_target_pairs={{0,4},{4,8},{8,12},{12,16},{16,20},{20,24},{24,28},{28,0},{1,5},{5... | collective-permute-start | bytes 786440 | tf_op jit(solution)/shard_map/ppermute | solution.py:25
  143.9 0.0 collective-permute-done.12
  144.0 1.9 collective-permute-start.14
  146.0 1.9 collective-permute-done.13
  147.8 5.6 %collective-permute-start.15 = (bf16[256,256]{1,0:T(8,128)(2,1)S(1)}, bf16[256,256]{1,0:T(8,128)(2,1)S(1)}, u32[]{:S(2)}, u32[]{:S(2)}) collective-permute-start(bf16[256,256]{1,0:T(8,128)(2,1)S(1)} %slice.44), channel_id=1, source_target_pairs={{0,4},{4,8},{8,12},{12,16},{16,20},{20,24},{24,28},{28,0},{1,5},{5... | collective-permute-start | bytes 393224 | tf_op jit(solution)/shard_map/ppermute | solution.py:25
  153.4 0.0 collective-permute-done.14
  153.5 1.9 collective-permute-start.16
  155.5 0.5 collective-permute-done.15
  156.0 5.6 %collective-permute-done.16 = bf16[256,256]{1,0:T(8,128)(2,1)S(1)} collective-permute-done((bf16[256,256]{1,0:T(8,128)(2,1)S(1)}, bf16[256,256]{1,0:T(8,128)(2,1)S(1)}, u32[]{:S(2)}, u32[]{:S(2)}) %collective-permute-start.16) | collective-permute-done | bytes 131104 | tf_op jit(solution)/shard_map/ppermute | solution.py:25
  161.6 0.0 copy-start
  161.6 0.0 all-gather.2.cloned.1.call-done
  161.6 1.3 copy-done
  162.9 8.0 %shard_map.82 = bf16[768,256]{1,0:T(8,128)(2,1)} custom-call(bf16[8,768,512]{2,1,0:T(8,128)(2,1)} %bitcast.69, bf16[8,512,256]{2,1,0:T(8,128)(2,1)} %copy-done), custom_call_target="tpu_custom_call" | custom-call | flops 1610612736 | bytes 8388608 | tf_op jit(solution)/shard_map/pallas_call | solution.py:80
  170.9 26.9 %all_to_all.5 = bf16[4,192,256]{2,1,0:T(8,128)(2,1)S(1)} all-to-all(bf16[4,192,256]{2,1,0:T(8,128)(2,1)} %bitcast.70), channel_id=1, replica_groups=mesh['x'=4,'zlh'=2,'zll'=2,'c'=2,'y'=8,'zh'=4] {'zh'}, dimensions={0} | all-to-all | bytes 786432 | tf_op jit(solution)/shard_map/all_to_all | solution.py:122
  198.0 0.7 fusion.20
  (43 shorter events, 0.7 us)
Async XLA Ops:
  6.5 155.1 %all-gather.2.cloned.1.call-start = ((), (), s32[]{:S(2)}) async-start(), calls=%async_computation.1 | async-start | bytes 6488064 | tf_op jit(solution)/shard_map/all_gather | solution.py:57
  42.9 12.8 %collective-permute-start = (bf16[192,512]{1,0:T(8,128)(2,1)S(1)}, bf16[192,512]{1,0:T(8,128)(2,1)S(1)}, u32[]{:S(2)}, u32[]{:S(2)}) collective-permute-start(bf16[192,512]{1,0:T(8,128)(2,1)S(1)} %add_bitcast_fusion), channel_id=1, source_target_pairs={{0,0},{4,128},{8,256},{12,384},{16,512},{20,640},{24,768},{28,896}... | collective-permute-start | bytes 589832 | tf_op jit(solution)/shard_map/ppermute | solution.py:56
  55.7 0.7 copy-start.2
  56.4 15.2 %collective-permute-start.1 = (bf16[768,256]{1,0:T(8,128)(2,1)S(1)}, bf16[768,256]{1,0:T(8,128)(2,1)S(1)}, u32[]{:S(2)}, u32[]{:S(2)}) collective-permute-start(bf16[768,256]{1,0:T(8,128)(2,1)S(1)} %all_gather.6), channel_id=1, source_target_pairs={{0,4},{4,8},{8,12},{12,16},{16,20},{20,24},{24,28},{28,0},{1,5},{5... | collective-permute-start | bytes 1179656 | tf_op jit(solution)/shard_map/ppermute | solution.py:25
  64.9 12.3 %collective-permute-start.2 = (bf16[768,256]{1,0:T(8,128)(2,1)S(1)}, bf16[768,256]{1,0:T(8,128)(2,1)S(1)}, u32[]{:S(2)}, u32[]{:S(2)}) collective-permute-start(bf16[768,256]{1,0:T(8,128)(2,1)S(1)} %all_gather.6), channel_id=1, source_target_pairs={{0,28},{4,0},{8,4},{12,8},{16,12},{20,16},{24,20},{28,24},{1,29},{... | collective-permute-start | bytes 1179656 | tf_op jit(solution)/shard_map/ppermute | solution.py:25
  66.8 44.6 %slice-start = ((s8[9437184]{0:T(1024)(128)(4,1)}), s8[4194304]{0:T(1024)(128)(4,1)S(1)}, s32[]{:S(2)}) async-start(s8[9437184]{0:T(1024)(128)(4,1)} %bitcast.74), calls=%async_computation.2 | async-start | bytes 8388608
  71.6 11.4 %collective-permute-start.3 = (bf16[768,256]{1,0:T(8,128)(2,1)S(1)}, bf16[768,256]{1,0:T(8,128)(2,1)S(1)}, u32[]{:S(2)}, u32[]{:S(2)}) collective-permute-start(bf16[768,256]{1,0:T(8,128)(2,1)S(1)} %collective-permute-done.1), channel_id=1, source_target_pairs={{0,4},{4,8},{8,12},{12,16},{16,20},{20,24},{24,28},{28,0},{1,5},{5... | collective-permute-start | bytes 1179656 | tf_op jit(solution)/shard_map/ppermute | solution.py:25
  77.2 11.4 %collective-permute-start.4 = (bf16[768,256]{1,0:T(8,128)(2,1)S(1)}, bf16[768,256]{1,0:T(8,128)(2,1)S(1)}, u32[]{:S(2)}, u32[]{:S(2)}) collective-permute-start(bf16[768,256]{1,0:T(8,128)(2,1)S(1)} %collective-permute-done.2), channel_id=1, source_target_pairs={{0,28},{4,0},{8,4},{12,8},{16,12},{20,16},{24,20},{28,24},{1,29},{... | collective-permute-start | bytes 1179656 | tf_op jit(solution)/shard_map/ppermute | solution.py:25
  82.9 10.9 %collective-permute-start.5 = (bf16[768,256]{1,0:T(8,128)(2,1)S(1)}, bf16[768,256]{1,0:T(8,128)(2,1)S(1)}, u32[]{:S(2)}, u32[]{:S(2)}) collective-permute-start(bf16[768,256]{1,0:T(8,128)(2,1)S(1)} %collective-permute-done.3), channel_id=1, source_target_pairs={{0,4},{4,8},{8,12},{12,16},{16,20},{20,24},{24,28},{28,0},{1,5},{5... | collective-permute-start | bytes 1179656 | tf_op jit(solution)/shard_map/ppermute | solution.py:25
  88.5 11.2 %collective-permute-start.6 = (bf16[768,256]{1,0:T(8,128)(2,1)S(1)}, bf16[768,256]{1,0:T(8,128)(2,1)S(1)}, u32[]{:S(2)}, u32[]{:S(2)}) collective-permute-start(bf16[768,256]{1,0:T(8,128)(2,1)S(1)} %collective-permute-done.4), channel_id=1, source_target_pairs={{0,28},{4,0},{8,4},{12,8},{16,12},{20,16},{24,20},{28,24},{1,29},{... | collective-permute-start | bytes 1179656 | tf_op jit(solution)/shard_map/ppermute | solution.py:25
  93.8 17.6 %slice-start.1 = ((s8[9437184]{0:T(1024)(128)(4,1)}), s8[4194304]{0:T(1024)(128)(4,1)S(1)}, s32[]{:S(2)}) async-start(s8[9437184]{0:T(1024)(128)(4,1)} %bitcast.74), calls=%async_computation.3 | async-start | bytes 8388608
  93.8 9.0 %collective-permute-start.7 = (bf16[384,256]{1,0:T(8,128)(2,1)S(1)}, bf16[384,256]{1,0:T(8,128)(2,1)S(1)}, u32[]{:S(2)}, u32[]{:S(2)}) collective-permute-start(bf16[384,256]{1,0:T(8,128)(2,1)S(1)} %slice.38), channel_id=1, source_target_pairs={{0,4},{4,8},{8,12},{12,16},{16,20},{20,24},{24,28},{28,0},{1,5},{5... | collective-permute-start | bytes 589832 | tf_op jit(solution)/shard_map/ppermute | solution.py:25
  99.7 8.8 %collective-permute-start.8 = (bf16[384,256]{1,0:T(8,128)(2,1)S(1)}, bf16[384,256]{1,0:T(8,128)(2,1)S(1)}, u32[]{:S(2)}, u32[]{:S(2)}) collective-permute-start(bf16[384,256]{1,0:T(8,128)(2,1)S(1)} %slice.39), channel_id=1, source_target_pairs={{0,28},{4,0},{8,4},{12,8},{16,12},{20,16},{24,20},{28,24},{1,29},{... | collective-permute-start | bytes 589832 | tf_op jit(solution)/shard_map/ppermute | solution.py:25
  108.5 1.7 copy-start.3
  109.4 2.1 slice-start.2
  111.4 4.0 %copy-start.6 = (f32[1,128]{1,0:T(1,128)S(1)}, f32[1,128]{1,0:T(1,128)}, u32[]{:S(2)}) copy-start(f32[1,128]{1,0:T(1,128)} %param.12) | copy-start | bytes 1540
  111.4 4.0 %copy-start.7 = (f32[1,128]{1,0:T(1,128)S(1)}, f32[1,128]{1,0:T(1,128)}, u32[]{:S(2)}) copy-start(f32[1,128]{1,0:T(1,128)} %param.11) | copy-start | bytes 1540
  111.5 4.6 %copy-start.4 = (f32[384]{0:T(512)S(1)}, f32[384]{0:T(512)}, u32[]{:S(2)}) copy-start(f32[384]{0:T(512)} %param.13) | copy-start | bytes 4612
  117.0 10.8 %collective-permute-start.9 = (bf16[512,256]{1,0:T(8,128)(2,1)S(1)}, bf16[512,256]{1,0:T(8,128)(2,1)S(1)}, u32[]{:S(2)}, u32[]{:S(2)}) collective-permute-start(bf16[512,256]{1,0:T(8,128)(2,1)S(1)} %pad_maximum_fusion), channel_id=1, source_target_pairs={{0,4},{4,8},{8,12},{12,16},{16,20},{20,24},{24,28},{28,0},{1,5},{5... | collective-permute-start | bytes 786440 | tf_op jit(solution)/shard_map/ppermute | solution.py:25
  120.4 12.2 %collective-permute-start.10 = (bf16[512,256]{1,0:T(8,128)(2,1)S(1)}, bf16[512,256]{1,0:T(8,128)(2,1)S(1)}, u32[]{:S(2)}, u32[]{:S(2)}) collective-permute-start(bf16[512,256]{1,0:T(8,128)(2,1)S(1)} %pad_maximum_fusion), channel_id=1, source_target_pairs={{0,28},{4,0},{8,4},{12,8},{16,12},{20,16},{24,20},{28,24},{1,29},{... | collective-permute-start | bytes 786440 | tf_op jit(solution)/shard_map/ppermute | solution.py:25
  127.8 10.5 %collective-permute-start.11 = (bf16[512,256]{1,0:T(8,128)(2,1)S(1)}, bf16[512,256]{1,0:T(8,128)(2,1)S(1)}, u32[]{:S(2)}, u32[]{:S(2)}) collective-permute-start(bf16[512,256]{1,0:T(8,128)(2,1)S(1)} %collective-permute-done.9), channel_id=1, source_target_pairs={{0,4},{4,8},{8,12},{12,16},{16,20},{20,24},{24,28},{28,0},{1,5},{5... | collective-permute-start | bytes 786440 | tf_op jit(solution)/shard_map/ppermute | solution.py:25
  132.6 11.3 %collective-permute-start.12 = (bf16[512,256]{1,0:T(8,128)(2,1)S(1)}, bf16[512,256]{1,0:T(8,128)(2,1)S(1)}, u32[]{:S(2)}, u32[]{:S(2)}) collective-permute-start(bf16[512,256]{1,0:T(8,128)(2,1)S(1)} %collective-permute-done.10), channel_id=1, source_target_pairs={{0,28},{4,0},{8,4},{12,8},{16,12},{20,16},{24,20},{28,24},{1,29},{... | collective-permute-start | bytes 786440 | tf_op jit(solution)/shard_map/ppermute | solution.py:25
  138.4 9.5 %collective-permute-start.13 = (bf16[512,256]{1,0:T(8,128)(2,1)S(1)}, bf16[512,256]{1,0:T(8,128)(2,1)S(1)}, u32[]{:S(2)}, u32[]{:S(2)}) collective-permute-start(bf16[512,256]{1,0:T(8,128)(2,1)S(1)} %collective-permute-done.11), channel_id=1, source_target_pairs={{0,4},{4,8},{8,12},{12,16},{16,20},{20,24},{24,28},{28,0},{1,5},{5... | collective-permute-start | bytes 786440 | tf_op jit(solution)/shard_map/ppermute | solution.py:25
  144.0 9.5 %collective-permute-start.14 = (bf16[512,256]{1,0:T(8,128)(2,1)S(1)}, bf16[512,256]{1,0:T(8,128)(2,1)S(1)}, u32[]{:S(2)}, u32[]{:S(2)}) collective-permute-start(bf16[512,256]{1,0:T(8,128)(2,1)S(1)} %collective-permute-done.12), channel_id=1, source_target_pairs={{0,28},{4,0},{8,4},{12,8},{16,12},{20,16},{24,20},{28,24},{1,29},{... | collective-permute-start | bytes 786440 | tf_op jit(solution)/shard_map/ppermute | solution.py:25
  147.8 8.1 %collective-permute-start.15 = (bf16[256,256]{1,0:T(8,128)(2,1)S(1)}, bf16[256,256]{1,0:T(8,128)(2,1)S(1)}, u32[]{:S(2)}, u32[]{:S(2)}) collective-permute-start(bf16[256,256]{1,0:T(8,128)(2,1)S(1)} %slice.44), channel_id=1, source_target_pairs={{0,4},{4,8},{8,12},{12,16},{16,20},{20,24},{24,28},{28,0},{1,5},{5... | collective-permute-start | bytes 393224 | tf_op jit(solution)/shard_map/ppermute | solution.py:25
  153.5 8.1 %collective-permute-start.16 = (bf16[256,256]{1,0:T(8,128)(2,1)S(1)}, bf16[256,256]{1,0:T(8,128)(2,1)S(1)}, u32[]{:S(2)}, u32[]{:S(2)}) collective-permute-start(bf16[256,256]{1,0:T(8,128)(2,1)S(1)} %slice.45), channel_id=1, source_target_pairs={{0,28},{4,0},{8,4},{12,8},{16,12},{20,16},{24,20},{28,24},{1,29},{... | collective-permute-start | bytes 393224 | tf_op jit(solution)/shard_map/ppermute | solution.py:25
  161.6 1.3 copy-start
  162.9 35.0 %copy-start.1 = (bf16[1,256,192]{1,2,0:T(8,128)(2,1)S(1)}, bf16[1,256,192]{1,2,0:T(8,128)(2,1)}, u32[]{:S(2)}) copy-start(bf16[1,256,192]{1,2,0:T(8,128)(2,1)} %param.8) | copy-start | bytes 294916
  162.9 35.0 %copy-start.5 = (f32[192]{0:T(256)S(1)}, f32[192]{0:T(256)}, u32[]{:S(2)}) copy-start(f32[192]{0:T(256)} %param.15) | copy-start | bytes 2308
Sparse Core Ops, SparseCore 0:
  56.5 79.8 all-gather.1

commit v4 on v2

--- a/solution.py
+++ b/solution.py
@@ -1,6 +1,8 @@
 import jax
 import jax.numpy as jnp
 from jax import lax
+from jax.experimental import pallas as pl
+from jax.experimental.pallas import tpu as pltpu
 from jax.sharding import Mesh
 from jax.sharding import PartitionSpec as P
 
@@ -23,7 +25,7 @@
     return lax.ppermute(value, axis, [(i, (i + by) % count) for i in range(count)])
 
 
-def gather_y(block):
+def gather_y(block, early=None):
     y = lax.axis_index("y")
     half = block.shape[0] // 2
     whole = jnp.zeros((NY,) + block.shape, block.dtype)
@@ -36,30 +38,67 @@
         up, down = shift(up, "y", NY, 1), shift(down, "y", NY, -1)
         whole = put(whole, up, y - step + NY, 0)
         whole = put(whole, down, y + step, 0)
-    up = shift(up[:half], "y", NY, 1)
-    down = shift(down[half:], "y", NY, -1)
+    up, down = shift(up[:half], "y", NY, 1), shift(down[half:], "y", NY, -1)
+    if early is not None:
+        return early(whole), jnp.concatenate([up, down], axis=0)
     whole = put(whole, up, y + 4, 0)
-    whole = put(whole, down, y + 4, half)
-    return whole
+    return put(whole, down, y + 4, half)
 
 
-def gather_out_weights(w_out):
-    depth = w_out.shape[0]
+def swap_out_weights(w_out):
     pairs = [
         ((out * 4 + low) * NY + y, (y * 4 + low) * NY + out)
         for out in range(NY)
         for low in range(4)
         for y in range(NY)
     ]
-    swapped = lax.ppermute(w_out.T, ("x", "zlh", "zll", "c", "y"), pairs)
-    return lax.all_gather(swapped, DP, axis=0, tiled=True).reshape(NY, -1, depth)
+    return lax.ppermute(w_out.T, ("x", "zlh", "zll", "c", "y"), pairs)
+
+
+def multiply_out(weights, hidden, first, steps):
+    count, rows, depth = weights.shape
+    columns = hidden.shape[2]
+
+    def kernel(first_ref, w_ref, h_ref, o_ref):
+        product = jnp.dot(w_ref[0], h_ref[0], preferred_element_type=jnp.float32)
+
+        @pl.when(pl.program_id(0) == 0)
+        def _():
+            o_ref[...] = product
+
+        @pl.when(pl.program_id(0) > 0)
+        def _():
+            o_ref[...] += product
+
+    place = lambda i, first_ref: ((first_ref[0] + i) & (count - 1), 0, 0)
+    return pl.pallas_call(
+        kernel,
+        grid_spec=pltpu.PrefetchScalarGridSpec(
+            num_scalar_prefetch=1,
+            grid=(steps,),
+            in_specs=[
+                pl.BlockSpec((1, rows, depth), place),
+                pl.BlockSpec((1, depth, columns), place),
+            ],
+            out_specs=pl.BlockSpec((rows, columns), lambda i, first_ref: (0, 0)),
+        ),
+        out_shape=jax.ShapeDtypeStruct((rows, columns), jnp.float32),
+        compiler_params=pltpu.CompilerParams(vmem_limit_bytes=16 * 1024 * 1024),
+        cost_estimate=pl.CostEstimate(
+            flops=2 * steps * rows * depth * columns,
+            bytes_accessed=2 * steps * depth * (rows + columns) + 4 * rows * columns,
+            transcendentals=0,
+        ),
+    )(first[None], weights, hidden)
 
 
 def per_device(patches, norm_gain, w_in, q_gain, k_gain, mlp_bias, w_out, out_bias):
     images, seq_len, local_width = patches.shape
     mine = patches[0].T
-    w_rows = gather_out_weights(w_out)
+    swapped = swap_out_weights(w_out)
     zgroup = lax.all_gather(mine, "zh", axis=0, tiled=True)
+    w_rows = lax.all_gather(swapped + zgroup[0, 0] * 0, DP, axis=0, tiled=True)
+    w_rows = w_rows.reshape(NY, NZ * local_width, -1)
     whole = gather_y(zgroup).reshape(-1, seq_len)
     normed = (normalize(whole.astype(jnp.float32), 0) * norm_gain[:, None]).astype(jnp.bfloat16)
     project = lax.dot_general(
@@ -76,10 +115,12 @@
     ).astype(jnp.bfloat16)
     mlp_hidden = jax.nn.gelu(project[3 * head :] + mlp_bias[:, None], approximate=False)
     hidden = jnp.concatenate([attended, mlp_hidden.astype(jnp.bfloat16)], axis=0)
-    hidden_all = gather_y(hidden)
-    part = jnp.zeros((NZ * local_width, seq_len), jnp.float32)
-    for i in range(NY):
-        part = part + jnp.dot(w_rows[i], hidden_all[i], preferred_element_type=jnp.float32)
+    far = (lax.axis_index("y") + 4) & (NY - 1)
+    near_part, far_hidden = gather_y(
+        hidden, lambda near: multiply_out(w_rows, near, far + 1, NY - 1)
+    )
+    far_weights = lax.dynamic_index_in_dim(w_rows, far, 0, False)
+    part = near_part + jnp.dot(far_weights, far_hidden, preferred_element_type=jnp.float32)
     part = part.astype(jnp.bfloat16).reshape(NZ, local_width, seq_len)
     pieces = lax.all_to_all(part, "zh", 0, 0)
     total = jnp.sum(pieces.astype(jnp.float32), axis=0)

time: 205 us -> 191 us (0.932)
  the two profiles are of different devices: /device:TPU:88 before, /device:TPU:68 now
where the time goes in v4:
time: 191 us; the launch traced here: 190 us
  starting transfers between devices  73 us (38%)
  blocking collectives  59.2 us (31%)
  waiting for transfers between devices  25.6 us (13%)
  between operations  14.7 us (8%)
  other arithmetic  5.62 us (3%)
  matrix products  4.84 us (3%)
  local copies, waits for them, and re-layouts  4.15 us (2%)
  Pallas kernels  3.14 us (2%)
    ppermute x16, starting transfers between devices, shift(): lax.ppermute(value, axis, [(i, (i + by) % count) for i in range(count)])  65.3 us
    all_gather x1, blocking collectives, per_device(): zgroup = lax.all_gather(mine, 'zh', axis=0, tiled=True)  36.1 us
    ppermute x16, waiting for transfers between devices, shift(): lax.ppermute(value, axis, [(i, (i + by) % count) for i in range(count)])  25.5 us
    all_to_all x1, blocking collectives, per_device(): pieces = lax.all_to_all(part, 'zh', 0, 0)  23.1 us
    ppermute x1, starting transfers between devices, swap_out_weights(): return lax.ppermute(w_out.T, ('x', 'zlh', 'zll', 'c', 'y'), pairs)  7.66 us
    dot_general x1, matrix products, per_device(): lax.dot_general(w_in, normed, (((0,), (0,)), ((), ())), preferred_element...  3.97 us
  transfers between devices with their start and end apart: 18, of which 9 were waited for; matrix products, arithmetic and copies ran while one was open for 5% of the time, Pallas kernels for 2%

profile of v4, /device:TPU:68, one launch (start us, length us, event | category | flops | bytes accessed | tf_op | source)
XLA Modules:
  0.0 190.2 jit_solution(12853564325204843416)
XLA Ops:
  6.5 7.7 %collective-permute-start = (bf16[192,512]{1,0:T(8,128)(2,1)}, bf16[192,512]{1,0:T(8,128)(2,1)S(1)}, u32[]{:S(2)}, u32[]{:S(2)}) collective-permute-start(bf16[192,512]{1,0:T(8,128)(2,1)} %bitcast.76), channel_id=1, source_target_pairs={{0,0},{4,128},{8,256},{12,384},{16,512},{20,640},{24,768},{28,896}... | collective-permute-start | bytes 589832 | tf_op jit(solution)/shard_map/ppermute | solution.py:55
  14.2 36.1 %all_gather.6 = bf16[768,256]{1,0:T(8,128)(2,1)S(1)} all-gather(bf16[192,256]{1,0:T(8,128)(2,1)} %bitcast.71), channel_id=1, replica_groups=mesh['x'=4,'zlh'=2,'zll'=2,'c'=2,'y'=8,'zh'=4] {'zh'}, dimensions={0}, use_global_device_ids=true | all-gather | bytes 491520 | tf_op jit(solution)/shard_map/all_gather | solution.py:99
  50.3 0.5 slice.37
  51.5 0.0 collective-permute-done
  51.5 0.7 broadcast_add_fusion
  52.2 0.0 all-gather.2.cloned.1.call-update
  52.2 11.5 %collective-permute-start.1 = (bf16[768,256]{1,0:T(8,128)(2,1)S(1)}, bf16[768,256]{1,0:T(8,128)(2,1)S(1)}, u32[]{:S(2)}, u32[]{:S(2)}) collective-permute-start(bf16[768,256]{1,0:T(8,128)(2,1)S(1)} %all_gather.6), channel_id=1, source_target_pairs={{0,4},{4,8},{8,12},{12,16},{16,20},{20,24},{24,28},{28,0},{1,5},{5... | collective-permute-start | bytes 1179656 | tf_op jit(solution)/shard_map/ppermute | solution.py:25
  63.7 1.9 %collective-permute-start.2 = (bf16[768,256]{1,0:T(8,128)(2,1)S(1)}, bf16[768,256]{1,0:T(8,128)(2,1)S(1)}, u32[]{:S(2)}, u32[]{:S(2)}) collective-permute-start(bf16[768,256]{1,0:T(8,128)(2,1)S(1)} %all_gather.6), channel_id=1, source_target_pairs={{0,28},{4,0},{8,4},{12,8},{16,12},{20,16},{24,20},{28,24},{1,29},{... | collective-permute-start | bytes 1179656 | tf_op jit(solution)/shard_map/ppermute | solution.py:25
  65.7 0.0 slice-start
  65.7 0.2 broadcast_in_dim.73
  65.9 4.9 %collective-permute-done.1 = bf16[768,256]{1,0:T(8,128)(2,1)S(1)} collective-permute-done((bf16[768,256]{1,0:T(8,128)(2,1)S(1)}, bf16[768,256]{1,0:T(8,128)(2,1)S(1)}, u32[]{:S(2)}, u32[]{:S(2)}) %collective-permute-start.1) | collective-permute-done | bytes 393248 | tf_op jit(solution)/shard_map/ppermute | solution.py:25
  70.9 4.3 %collective-permute-start.3 = (bf16[768,256]{1,0:T(8,128)(2,1)S(1)}, bf16[768,256]{1,0:T(8,128)(2,1)S(1)}, u32[]{:S(2)}, u32[]{:S(2)}) collective-permute-start(bf16[768,256]{1,0:T(8,128)(2,1)S(1)} %collective-permute-done.1), channel_id=1, source_target_pairs={{0,4},{4,8},{8,12},{12,16},{16,20},{20,24},{24,28},{28,0},{1,5},{5... | collective-permute-start | bytes 1179656 | tf_op jit(solution)/shard_map/ppermute | solution.py:25
  75.2 0.0 collective-permute-done.2
  75.2 3.1 %collective-permute-start.4 = (bf16[768,256]{1,0:T(8,128)(2,1)S(1)}, bf16[768,256]{1,0:T(8,128)(2,1)S(1)}, u32[]{:S(2)}, u32[]{:S(2)}) collective-permute-start(bf16[768,256]{1,0:T(8,128)(2,1)S(1)} %collective-permute-done.2), channel_id=1, source_target_pairs={{0,28},{4,0},{8,4},{12,8},{16,12},{20,16},{24,20},{28,24},{1,29},{... | collective-permute-start | bytes 1179656 | tf_op jit(solution)/shard_map/ppermute | solution.py:25
  78.4 4.2 %collective-permute-done.3 = bf16[768,256]{1,0:T(8,128)(2,1)S(1)} collective-permute-done((bf16[768,256]{1,0:T(8,128)(2,1)S(1)}, bf16[768,256]{1,0:T(8,128)(2,1)S(1)}, u32[]{:S(2)}, u32[]{:S(2)}) %collective-permute-start.3) | collective-permute-done | bytes 393248 | tf_op jit(solution)/shard_map/ppermute | solution.py:25
  82.6 3.1 %collective-permute-start.5 = (bf16[768,256]{1,0:T(8,128)(2,1)S(1)}, bf16[768,256]{1,0:T(8,128)(2,1)S(1)}, u32[]{:S(2)}, u32[]{:S(2)}) collective-permute-start(bf16[768,256]{1,0:T(8,128)(2,1)S(1)} %collective-permute-done.3), channel_id=1, source_target_pairs={{0,4},{4,8},{8,12},{12,16},{16,20},{20,24},{24,28},{28,0},{1,5},{5... | collective-permute-start | bytes 1179656 | tf_op jit(solution)/shard_map/ppermute | solution.py:25
  85.8 0.0 collective-permute-done.4
  85.8 4.3 %collective-permute-start.6 = (bf16[768,256]{1,0:T(8,128)(2,1)S(1)}, bf16[768,256]{1,0:T(8,128)(2,1)S(1)}, u32[]{:S(2)}, u32[]{:S(2)}) collective-permute-start(bf16[768,256]{1,0:T(8,128)(2,1)S(1)} %collective-permute-done.4), channel_id=1, source_target_pairs={{0,28},{4,0},{8,4},{12,8},{16,12},{20,16},{24,20},{28,24},{1,29},{... | collective-permute-start | bytes 1179656 | tf_op jit(solution)/shard_map/ppermute | solution.py:25
  90.2 3.3 %collective-permute-done.5 = bf16[768,256]{1,0:T(8,128)(2,1)S(1)} collective-permute-done((bf16[768,256]{1,0:T(8,128)(2,1)S(1)}, bf16[768,256]{1,0:T(8,128)(2,1)S(1)}, u32[]{:S(2)}, u32[]{:S(2)}) %collective-permute-start.5) | collective-permute-done | bytes 393248 | tf_op jit(solution)/shard_map/ppermute | solution.py:25
  93.5 0.0 slice-start.1
  93.5 2.3 %collective-permute-start.7 = (bf16[384,256]{1,0:T(8,128)(2,1)S(1)}, bf16[384,256]{1,0:T(8,128)(2,1)S(1)}, u32[]{:S(2)}, u32[]{:S(2)}) collective-permute-start(bf16[384,256]{1,0:T(8,128)(2,1)S(1)} %slice.38), channel_id=1, source_target_pairs={{0,4},{4,8},{8,12},{12,16},{16,20},{20,24},{24,28},{28,0},{1,5},{5... | collective-permute-start | bytes 589832 | tf_op jit(solution)/shard_map/ppermute | solution.py:25
  95.8 0.0 collective-permute-done.6
  95.8 5.2 %collective-permute-start.8 = (bf16[384,256]{1,0:T(8,128)(2,1)S(1)}, bf16[384,256]{1,0:T(8,128)(2,1)S(1)}, u32[]{:S(2)}, u32[]{:S(2)}) collective-permute-start(bf16[384,256]{1,0:T(8,128)(2,1)S(1)} %slice.39), channel_id=1, source_target_pairs={{0,28},{4,0},{8,4},{12,8},{16,12},{20,16},{24,20},{28,24},{1,29},{... | collective-permute-start | bytes 589832 | tf_op jit(solution)/shard_map/ppermute | solution.py:25
  101.1 1.5 collective-permute-done.7
  102.6 1.6 collective-permute-done.8
  104.2 0.0 copy-start.2
  104.2 0.8 convert_reduce_fusion
  105.0 0.9 multiply_reduce_fusion
  105.9 1.1 fusion.2
  107.1 0.0 copy-start.5
  107.1 0.0 copy-start.6
  107.1 0.0 copy-start.3
  107.1 4.0 %convolution_bitcast_fusion = f32[768,256]{1,0:T(8,128)S(1)} fusion(bf16[6144,256]{1,0:T(8,128)(2,1)S(1)} %fusion.2, bf16[6144,768]{1,0:T(8,128)(2,1)S(1)} %bitcast.75), kind=kOutput, calls=%fused_computation.6 | convolution fusion | flops 2415919104 | bytes 13369344 | tf_op jit(solution)/shard_map/dot_general | solution.py:104
  111.2 0.0 copy-done.5
  111.3 0.3 fusion.35
  111.6 0.1 fusion.19
  111.7 0.2 convolution_convert_fusion
  111.9 1.0 fusion.8
  112.9 2.0 %collective-permute-start.9 = (bf16[512,256]{1,0:T(8,128)(2,1)S(1)}, bf16[512,256]{1,0:T(8,128)(2,1)S(1)}, u32[]{:S(2)}, u32[]{:S(2)}) collective-permute-start(bf16[512,256]{1,0:T(8,128)(2,1)S(1)} %pad_maximum_fusion), channel_id=1, source_target_pairs={{0,4},{4,8},{8,12},{12,16},{16,20},{20,24},{24,28},{28,0},{1,5},{5... | collective-permute-start | bytes 786440 | tf_op jit(solution)/shard_map/ppermute | solution.py:25
  114.9 5.5 %collective-permute-start.10 = (bf16[512,256]{1,0:T(8,128)(2,1)S(1)}, bf16[512,256]{1,0:T(8,128)(2,1)S(1)}, u32[]{:S(2)}, u32[]{:S(2)}) collective-permute-start(bf16[512,256]{1,0:T(8,128)(2,1)S(1)} %pad_maximum_fusion), channel_id=1, source_target_pairs={{0,28},{4,0},{8,4},{12,8},{16,12},{20,16},{24,20},{28,24},{1,29},{... | collective-permute-start | bytes 786440 | tf_op jit(solution)/shard_map/ppermute | solution.py:25
  120.4 0.1 broadcast_in_dim.72
  120.6 2.9 %collective-permute-done.9 = bf16[512,256]{1,0:T(8,128)(2,1)S(1)} collective-permute-done((bf16[512,256]{1,0:T(8,128)(2,1)S(1)}, bf16[512,256]{1,0:T(8,128)(2,1)S(1)}, u32[]{:S(2)}, u32[]{:S(2)}) %collective-permute-start.9) | collective-permute-done | bytes 262176 | tf_op jit(solution)/shard_map/ppermute | solution.py:25
  123.5 1.9 %collective-permute-start.11 = (bf16[512,256]{1,0:T(8,128)(2,1)S(1)}, bf16[512,256]{1,0:T(8,128)(2,1)S(1)}, u32[]{:S(2)}, u32[]{:S(2)}) collective-permute-start(bf16[512,256]{1,0:T(8,128)(2,1)S(1)} %collective-permute-done.9), channel_id=1, source_target_pairs={{0,4},{4,8},{8,12},{12,16},{16,20},{20,24},{24,28},{28,0},{1,5},{5... | collective-permute-start | bytes 786440 | tf_op jit(solution)/shard_map/ppermute | solution.py:25
  125.4 0.0 collective-permute-done.10
  125.4 5.4 %collective-permute-start.12 = (bf16[512,256]{1,0:T(8,128)(2,1)S(1)}, bf16[512,256]{1,0:T(8,128)(2,1)S(1)}, u32[]{:S(2)}, u32[]{:S(2)}) collective-permute-start(bf16[512,256]{1,0:T(8,128)(2,1)S(1)} %collective-permute-done.10), channel_id=1, source_target_pairs={{0,28},{4,0},{8,4},{12,8},{16,12},{20,16},{24,20},{28,24},{1,29},{... | collective-permute-start | bytes 786440 | tf_op jit(solution)/shard_map/ppermute | solution.py:25
  130.9 3.9 %collective-permute-done.11 = bf16[512,256]{1,0:T(8,128)(2,1)S(1)} collective-permute-done((bf16[512,256]{1,0:T(8,128)(2,1)S(1)}, bf16[512,256]{1,0:T(8,128)(2,1)S(1)}, u32[]{:S(2)}, u32[]{:S(2)}) %collective-permute-start.11) | collective-permute-done | bytes 262176 | tf_op jit(solution)/shard_map/ppermute | solution.py:25
  134.8 1.9 %collective-permute-start.13 = (bf16[512,256]{1,0:T(8,128)(2,1)S(1)}, bf16[512,256]{1,0:T(8,128)(2,1)S(1)}, u32[]{:S(2)}, u32[]{:S(2)}) collective-permute-start(bf16[512,256]{1,0:T(8,128)(2,1)S(1)} %collective-permute-done.11), channel_id=1, source_target_pairs={{0,4},{4,8},{8,12},{12,16},{16,20},{20,24},{24,28},{28,0},{1,5},{5... | collective-permute-start | bytes 786440 | tf_op jit(solution)/shard_map/ppermute | solution.py:25
  136.7 0.1 collective-permute-done.12
  136.8 5.6 %collective-permute-start.14 = (bf16[512,256]{1,0:T(8,128)(2,1)S(1)}, bf16[512,256]{1,0:T(8,128)(2,1)S(1)}, u32[]{:S(2)}, u32[]{:S(2)}) collective-permute-start(bf16[512,256]{1,0:T(8,128)(2,1)S(1)} %collective-permute-done.12), channel_id=1, source_target_pairs={{0,28},{4,0},{8,4},{12,8},{16,12},{20,16},{24,20},{28,24},{1,29},{... | collective-permute-start | bytes 786440 | tf_op jit(solution)/shard_map/ppermute | solution.py:25
  142.5 3.0 %collective-permute-done.13 = bf16[512,256]{1,0:T(8,128)(2,1)S(1)} collective-permute-done((bf16[512,256]{1,0:T(8,128)(2,1)S(1)}, bf16[512,256]{1,0:T(8,128)(2,1)S(1)}, u32[]{:S(2)}, u32[]{:S(2)}) %collective-permute-start.13) | collective-permute-done | bytes 262176 | tf_op jit(solution)/shard_map/ppermute | solution.py:25
  145.5 1.9 %collective-permute-start.15 = (bf16[256,256]{1,0:T(8,128)(2,1)S(1)}, bf16[256,256]{1,0:T(8,128)(2,1)S(1)}, u32[]{:S(2)}, u32[]{:S(2)}) collective-permute-start(bf16[256,256]{1,0:T(8,128)(2,1)S(1)} %slice.44), channel_id=1, source_target_pairs={{0,4},{4,8},{8,12},{12,16},{16,20},{20,24},{24,28},{28,0},{1,5},{5... | collective-permute-start | bytes 393224 | tf_op jit(solution)/shard_map/ppermute | solution.py:25
  147.5 0.0 collective-permute-done.14
  147.5 5.4 %collective-permute-start.16 = (bf16[256,256]{1,0:T(8,128)(2,1)S(1)}, bf16[256,256]{1,0:T(8,128)(2,1)S(1)}, u32[]{:S(2)}, u32[]{:S(2)}) collective-permute-start(bf16[256,256]{1,0:T(8,128)(2,1)S(1)} %slice.45), channel_id=1, source_target_pairs={{0,28},{4,0},{8,4},{12,8},{16,12},{20,16},{24,20},{28,24},{1,29},{... | collective-permute-start | bytes 393224 | tf_op jit(solution)/shard_map/ppermute | solution.py:25
  152.9 0.0 all-gather.2.cloned.1.call-done
  153.0 2.8 %copy-done = bf16[6144,512]{1,0:T(8,128)(2,1)S(1)} copy-done((bf16[6144,512]{1,0:T(8,128)(2,1)S(1)}, bf16[6144,512]{1,0:T(8,128)(2,1)}, u32[]{:S(2)}) %copy-start) | copy-done | bytes 6291480
  155.7 3.1 %shard_map.82 = f32[768,256]{1,0:T(8,128)S(1)} custom-call(s32[1]{0:T(128)} %bitcast.1.first_ref, bf16[8,768,512]{2,1,0:T(8,128)(2,1)S(1)} %bitcast.68, bf16[8,512,256]{2,1,0:T(8,128)(2,1)S(1)} %bitcast_dynamic-update-slice_fusion.7.h_ref), custom_call_target="tpu_custom_call" | custom-call | flops 1409286144 | bytes 8126464 | tf_op jit(solution)/shard_map/pallas_call | solution.py:74
  158.9 0.0 copy-start.1
  158.9 0.0 copy-start.4
  158.9 0.0 collective-permute-done.15
  158.9 0.0 collective-permute-done.16
  158.9 0.4 fusion.3
  159.3 0.1 add_convert_fusion
  159.4 23.1 %all_to_all.5 = bf16[4,192,256]{2,1,0:T(8,128)(2,1)S(1)} all-to-all(bf16[4,192,256]{2,1,0:T(8,128)(2,1)S(1)} %bitcast.70), channel_id=1, replica_groups=mesh['x'=4,'zlh'=2,'zll'=2,'c'=2,'y'=8,'zh'=4] {'zh'}, dimensions={0} | all-to-all | bytes 786432 | tf_op jit(solution)/shard_map/all_to_all | solution.py:125
  182.6 0.7 fusion.26
  (41 shorter events, 0.7 us)
Async XLA Ops:
  6.5 146.4 %all-gather.2.cloned.1.call-start = ((), (), s32[]{:S(2)}) async-start(), calls=%async_computation.1 | async-start | bytes 6488064 | tf_op jit(solution)/shard_map/all_gather | solution.py:100
  6.5 44.9 %collective-permute-start = (bf16[192,512]{1,0:T(8,128)(2,1)}, bf16[192,512]{1,0:T(8,128)(2,1)S(1)}, u32[]{:S(2)}, u32[]{:S(2)}) collective-permute-start(bf16[192,512]{1,0:T(8,128)(2,1)} %bitcast.76), channel_id=1, source_target_pairs={{0,0},{4,128},{8,256},{12,384},{16,512},{20,640},{24,768},{28,896}... | collective-permute-start | bytes 589832 | tf_op jit(solution)/shard_map/ppermute | solution.py:55
  52.2 18.7 %collective-permute-start.1 = (bf16[768,256]{1,0:T(8,128)(2,1)S(1)}, bf16[768,256]{1,0:T(8,128)(2,1)S(1)}, u32[]{:S(2)}, u32[]{:S(2)}) collective-permute-start(bf16[768,256]{1,0:T(8,128)(2,1)S(1)} %all_gather.6), channel_id=1, source_target_pairs={{0,4},{4,8},{8,12},{12,16},{16,20},{20,24},{24,28},{28,0},{1,5},{5... | collective-permute-start | bytes 1179656 | tf_op jit(solution)/shard_map/ppermute | solution.py:25
  63.7 11.5 %collective-permute-start.2 = (bf16[768,256]{1,0:T(8,128)(2,1)S(1)}, bf16[768,256]{1,0:T(8,128)(2,1)S(1)}, u32[]{:S(2)}, u32[]{:S(2)}) collective-permute-start(bf16[768,256]{1,0:T(8,128)(2,1)S(1)} %all_gather.6), channel_id=1, source_target_pairs={{0,28},{4,0},{8,4},{12,8},{16,12},{20,16},{24,20},{28,24},{1,29},{... | collective-permute-start | bytes 1179656 | tf_op jit(solution)/shard_map/ppermute | solution.py:25
  65.7 41.4 %slice-start = ((s8[9437184]{0:T(1024)(128)(4,1)}), s8[4194304]{0:T(1024)(128)(4,1)S(1)}, s32[]{:S(2)}) async-start(s8[9437184]{0:T(1024)(128)(4,1)} %bitcast.74), calls=%async_computation.2 | async-start | bytes 8388608
  70.9 11.8 %collective-permute-start.3 = (bf16[768,256]{1,0:T(8,128)(2,1)S(1)}, bf16[768,256]{1,0:T(8,128)(2,1)S(1)}, u32[]{:S(2)}, u32[]{:S(2)}) collective-permute-start(bf16[768,256]{1,0:T(8,128)(2,1)S(1)} %collective-permute-done.1), channel_id=1, source_target_pairs={{0,4},{4,8},{8,12},{12,16},{16,20},{20,24},{24,28},{28,0},{1,5},{5... | collective-permute-start | bytes 1179656 | tf_op jit(solution)/shard_map/ppermute | solution.py:25
  75.2 10.6 %collective-permute-start.4 = (bf16[768,256]{1,0:T(8,128)(2,1)S(1)}, bf16[768,256]{1,0:T(8,128)(2,1)S(1)}, u32[]{:S(2)}, u32[]{:S(2)}) collective-permute-start(bf16[768,256]{1,0:T(8,128)(2,1)S(1)} %collective-permute-done.2), channel_id=1, source_target_pairs={{0,28},{4,0},{8,4},{12,8},{16,12},{20,16},{24,20},{28,24},{1,29},{... | collective-permute-start | bytes 1179656 | tf_op jit(solution)/shard_map/ppermute | solution.py:25
  82.6 10.9 %collective-permute-start.5 = (bf16[768,256]{1,0:T(8,128)(2,1)S(1)}, bf16[768,256]{1,0:T(8,128)(2,1)S(1)}, u32[]{:S(2)}, u32[]{:S(2)}) collective-permute-start(bf16[768,256]{1,0:T(8,128)(2,1)S(1)} %collective-permute-done.3), channel_id=1, source_target_pairs={{0,4},{4,8},{8,12},{12,16},{16,20},{20,24},{24,28},{28,0},{1,5},{5... | collective-permute-start | bytes 1179656 | tf_op jit(solution)/shard_map/ppermute | solution.py:25
  85.8 10.0 %collective-permute-start.6 = (bf16[768,256]{1,0:T(8,128)(2,1)S(1)}, bf16[768,256]{1,0:T(8,128)(2,1)S(1)}, u32[]{:S(2)}, u32[]{:S(2)}) collective-permute-start(bf16[768,256]{1,0:T(8,128)(2,1)S(1)} %collective-permute-done.4), channel_id=1, source_target_pairs={{0,28},{4,0},{8,4},{12,8},{16,12},{20,16},{24,20},{28,24},{1,29},{... | collective-permute-start | bytes 1179656 | tf_op jit(solution)/shard_map/ppermute | solution.py:25
  93.5 13.5 %slice-start.1 = ((s8[9437184]{0:T(1024)(128)(4,1)}), s8[4194304]{0:T(1024)(128)(4,1)S(1)}, s32[]{:S(2)}) async-start(s8[9437184]{0:T(1024)(128)(4,1)} %bitcast.74), calls=%async_computation.3 | async-start | bytes 8388608
  93.5 9.0 %collective-permute-start.7 = (bf16[384,256]{1,0:T(8,128)(2,1)S(1)}, bf16[384,256]{1,0:T(8,128)(2,1)S(1)}, u32[]{:S(2)}, u32[]{:S(2)}) collective-permute-start(bf16[384,256]{1,0:T(8,128)(2,1)S(1)} %slice.38), channel_id=1, source_target_pairs={{0,4},{4,8},{8,12},{12,16},{16,20},{20,24},{24,28},{28,0},{1,5},{5... | collective-permute-start | bytes 589832 | tf_op jit(solution)/shard_map/ppermute | solution.py:25
  95.8 8.3 %collective-permute-start.8 = (bf16[384,256]{1,0:T(8,128)(2,1)S(1)}, bf16[384,256]{1,0:T(8,128)(2,1)S(1)}, u32[]{:S(2)}, u32[]{:S(2)}) collective-permute-start(bf16[384,256]{1,0:T(8,128)(2,1)S(1)} %slice.39), channel_id=1, source_target_pairs={{0,28},{4,0},{8,4},{12,8},{16,12},{20,16},{24,20},{28,24},{1,29},{... | collective-permute-start | bytes 589832 | tf_op jit(solution)/shard_map/ppermute | solution.py:25
  104.2 1.7 copy-start.2
  105.0 2.1 %slice-start.2 = ((s8[9437184]{0:T(1024)(128)(4,1)}), s8[1048576]{0:T(1024)(128)(4,1)S(1)}, s32[]{:S(2)}) async-start(s8[9437184]{0:T(1024)(128)(4,1)} %bitcast.74), calls=%async_computation.4 | async-start | bytes 2097152
  107.1 4.1 %copy-start.5 = (f32[1,128]{1,0:T(1,128)S(1)}, f32[1,128]{1,0:T(1,128)}, u32[]{:S(2)}) copy-start(f32[1,128]{1,0:T(1,128)} %param.12) | copy-start | bytes 1540
  107.1 4.1 %copy-start.6 = (f32[1,128]{1,0:T(1,128)S(1)}, f32[1,128]{1,0:T(1,128)}, u32[]{:S(2)}) copy-start(f32[1,128]{1,0:T(1,128)} %param.11) | copy-start | bytes 1540
  107.1 4.7 %copy-start.3 = (f32[384]{0:T(512)S(1)}, f32[384]{0:T(512)}, u32[]{:S(2)}) copy-start(f32[384]{0:T(512)} %param.13) | copy-start | bytes 4612
  112.9 10.6 %collective-permute-start.9 = (bf16[512,256]{1,0:T(8,128)(2,1)S(1)}, bf16[512,256]{1,0:T(8,128)(2,1)S(1)}, u32[]{:S(2)}, u32[]{:S(2)}) collective-permute-start(bf16[512,256]{1,0:T(8,128)(2,1)S(1)} %pad_maximum_fusion), channel_id=1, source_target_pairs={{0,4},{4,8},{8,12},{12,16},{16,20},{20,24},{24,28},{28,0},{1,5},{5... | collective-permute-start | bytes 786440 | tf_op jit(solution)/shard_map/ppermute | solution.py:25
  114.9 10.5 %collective-permute-start.10 = (bf16[512,256]{1,0:T(8,128)(2,1)S(1)}, bf16[512,256]{1,0:T(8,128)(2,1)S(1)}, u32[]{:S(2)}, u32[]{:S(2)}) collective-permute-start(bf16[512,256]{1,0:T(8,128)(2,1)S(1)} %pad_maximum_fusion), channel_id=1, source_target_pairs={{0,28},{4,0},{8,4},{12,8},{16,12},{20,16},{24,20},{28,24},{1,29},{... | collective-permute-start | bytes 786440 | tf_op jit(solution)/shard_map/ppermute | solution.py:25
  123.5 11.3 %collective-permute-start.11 = (bf16[512,256]{1,0:T(8,128)(2,1)S(1)}, bf16[512,256]{1,0:T(8,128)(2,1)S(1)}, u32[]{:S(2)}, u32[]{:S(2)}) collective-permute-start(bf16[512,256]{1,0:T(8,128)(2,1)S(1)} %collective-permute-done.9), channel_id=1, source_target_pairs={{0,4},{4,8},{8,12},{12,16},{16,20},{20,24},{24,28},{28,0},{1,5},{5... | collective-permute-start | bytes 786440 | tf_op jit(solution)/shard_map/ppermute | solution.py:25
  125.4 11.4 %collective-permute-start.12 = (bf16[512,256]{1,0:T(8,128)(2,1)S(1)}, bf16[512,256]{1,0:T(8,128)(2,1)S(1)}, u32[]{:S(2)}, u32[]{:S(2)}) collective-permute-start(bf16[512,256]{1,0:T(8,128)(2,1)S(1)} %collective-permute-done.10), channel_id=1, source_target_pairs={{0,28},{4,0},{8,4},{12,8},{16,12},{20,16},{24,20},{28,24},{1,29},{... | collective-permute-start | bytes 786440 | tf_op jit(solution)/shard_map/ppermute | solution.py:25
  134.8 10.7 %collective-permute-start.13 = (bf16[512,256]{1,0:T(8,128)(2,1)S(1)}, bf16[512,256]{1,0:T(8,128)(2,1)S(1)}, u32[]{:S(2)}, u32[]{:S(2)}) collective-permute-start(bf16[512,256]{1,0:T(8,128)(2,1)S(1)} %collective-permute-done.11), channel_id=1, source_target_pairs={{0,4},{4,8},{8,12},{12,16},{16,20},{20,24},{24,28},{28,0},{1,5},{5... | collective-permute-start | bytes 786440 | tf_op jit(solution)/shard_map/ppermute | solution.py:25
  136.8 10.6 %collective-permute-start.14 = (bf16[512,256]{1,0:T(8,128)(2,1)S(1)}, bf16[512,256]{1,0:T(8,128)(2,1)S(1)}, u32[]{:S(2)}, u32[]{:S(2)}) collective-permute-start(bf16[512,256]{1,0:T(8,128)(2,1)S(1)} %collective-permute-done.12), channel_id=1, source_target_pairs={{0,28},{4,0},{8,4},{12,8},{16,12},{20,16},{24,20},{28,24},{1,29},{... | collective-permute-start | bytes 786440 | tf_op jit(solution)/shard_map/ppermute | solution.py:25
  145.5 13.4 %collective-permute-start.15 = (bf16[256,256]{1,0:T(8,128)(2,1)S(1)}, bf16[256,256]{1,0:T(8,128)(2,1)S(1)}, u32[]{:S(2)}, u32[]{:S(2)}) collective-permute-start(bf16[256,256]{1,0:T(8,128)(2,1)S(1)} %slice.44), channel_id=1, source_target_pairs={{0,4},{4,8},{8,12},{12,16},{16,20},{20,24},{24,28},{28,0},{1,5},{5... | collective-permute-start | bytes 393224 | tf_op jit(solution)/shard_map/ppermute | solution.py:25
  147.5 11.4 %collective-permute-start.16 = (bf16[256,256]{1,0:T(8,128)(2,1)S(1)}, bf16[256,256]{1,0:T(8,128)(2,1)S(1)}, u32[]{:S(2)}, u32[]{:S(2)}) collective-permute-start(bf16[256,256]{1,0:T(8,128)(2,1)S(1)} %slice.45), channel_id=1, source_target_pairs={{0,28},{4,0},{8,4},{12,8},{16,12},{20,16},{24,20},{28,24},{1,29},{... | collective-permute-start | bytes 393224 | tf_op jit(solution)/shard_map/ppermute | solution.py:25
  153.0 2.8 %copy-start = (bf16[6144,512]{1,0:T(8,128)(2,1)S(1)}, bf16[6144,512]{1,0:T(8,128)(2,1)}, u32[]{:S(2)}) copy-start(bf16[6144,512]{1,0:T(8,128)(2,1)} %all-gather.2.cloned.1.call-done) | copy-start | bytes 18874372
  158.9 23.7 %copy-start.1 = (bf16[1,256,192]{1,2,0:T(8,128)(2,1)S(1)}, bf16[1,256,192]{1,2,0:T(8,128)(2,1)}, u32[]{:S(2)}) copy-start(bf16[1,256,192]{1,2,0:T(8,128)(2,1)} %param.8) | copy-start | bytes 294916
  158.9 23.7 %copy-start.4 = (f32[192]{0:T(256)S(1)}, f32[192]{0:T(256)}, u32[]{:S(2)}) copy-start(f32[192]{0:T(256)} %param.15) | copy-start | bytes 2308
Sparse Core Ops, SparseCore 0:
  52.3 74.3 all-gather.1

commit v5 on v3

--- a/solution.py
+++ b/solution.py
@@ -21,40 +21,18 @@
     return center * lax.rsqrt(spread + EPS)
 
 
-def shift(value, axis, count, by):
-    return lax.ppermute(value, axis, [(i, (i + by) % count) for i in range(count)])
+def gather_direct(block, axis, count):
+    return lax.all_to_all(jnp.broadcast_to(block, (count,) + block.shape), axis, 0, 0)
 
 
-def gather_y(block):
-    y = lax.axis_index("y")
-    half = block.shape[0] // 2
-    whole = jnp.zeros((NY,) + block.shape, block.dtype)
-    put = lambda whole, part, index, row: lax.dynamic_update_slice(
-        whole, part[None], (index & (NY - 1), row, 0)
-    )
-    whole = put(whole, block, y, 0)
-    up = down = block
-    for step in range(1, 4):
-        up, down = shift(up, "y", NY, 1), shift(down, "y", NY, -1)
-        whole = put(whole, up, y - step + NY, 0)
-        whole = put(whole, down, y + step, 0)
-    up = shift(up[:half], "y", NY, 1)
-    down = shift(down[half:], "y", NY, -1)
-    whole = put(whole, up, y + 4, 0)
-    whole = put(whole, down, y + 4, half)
-    return whole
-
-
-def gather_out_weights(w_out):
-    depth = w_out.shape[0]
+def swap_out_weights(w_out):
     pairs = [
         ((out * 4 + low) * NY + y, (y * 4 + low) * NY + out)
         for out in range(NY)
         for low in range(4)
         for y in range(NY)
     ]
-    swapped = lax.ppermute(w_out.T, ("x", "zlh", "zll", "c", "y"), pairs)
-    return lax.all_gather(swapped, DP, axis=0, tiled=True).reshape(NY, -1, depth)
+    return lax.ppermute(w_out.T, ("x", "zlh", "zll", "c", "y"), pairs)
 
 
 def multiply_out(weights, hidden):
@@ -69,13 +47,13 @@
         def _():
             total_ref[...] = product
 
-        @pl.when(step > 0)
+        @pl.when((step > 0) & (step < count - 1))
         def _():
             total_ref[...] += product
 
         @pl.when(step == count - 1)
         def _():
-            o_ref[...] = total_ref[...].astype(o_ref.dtype)
+            o_ref[...] = (total_ref[...] + product).astype(o_ref.dtype)
 
     return pl.pallas_call(
         kernel,
@@ -87,7 +65,7 @@
         out_specs=pl.BlockSpec((rows, columns), lambda i: (0, 0)),
         out_shape=jax.ShapeDtypeStruct((rows, columns), jnp.bfloat16),
         scratch_shapes=[pltpu.VMEM((rows, columns), jnp.float32)],
-        compiler_params=pltpu.CompilerParams(vmem_limit_bytes=56 * 1024 * 1024),
+        compiler_params=pltpu.CompilerParams(vmem_limit_bytes=16 * 1024 * 1024),
         cost_estimate=pl.CostEstimate(
             flops=2 * count * rows * depth * columns,
             bytes_accessed=2 * count * depth * (rows + columns),
@@ -99,9 +77,11 @@
 def per_device(patches, norm_gain, w_in, q_gain, k_gain, mlp_bias, w_out, out_bias):
     images, seq_len, local_width = patches.shape
     mine = patches[0].T
-    zgroup = lax.all_gather(mine, "zh", axis=0, tiled=True)
-    w_rows = gather_out_weights(w_out + zgroup[0, 0] * 0)
-    whole = gather_y(zgroup).reshape(-1, seq_len)
+    swapped = swap_out_weights(w_out)
+    zgroup = gather_direct(mine, "zh", NZ).reshape(NZ * local_width, seq_len)
+    w_rows = lax.all_gather(swapped + zgroup[0, 0] * 0, DP, axis=0, tiled=True)
+    w_rows = w_rows.reshape(NY, NZ * local_width, -1)
+    whole = gather_direct(zgroup, "y", NY).reshape(-1, seq_len)
     normed = (normalize(whole.astype(jnp.float32), 0) * norm_gain[:, None]).astype(jnp.bfloat16)
     project = lax.dot_general(
         w_in, normed, (((0,), (0,)), ((), ())), preferred_element_type=jnp.float32
@@ -117,8 +97,8 @@
     ).astype(jnp.bfloat16)
     mlp_hidden = jax.nn.gelu(project[3 * head :] + mlp_bias[:, None], approximate=False)
     hidden = jnp.concatenate([attended, mlp_hidden.astype(jnp.bfloat16)], axis=0)
-    hidden_all = gather_y(hidden)
-    part = multiply_out(w_rows, hidden_all).reshape(NZ, local_width, seq_len)
+    part = multiply_out(w_rows, gather_direct(hidden, "y", NY))
+    part = part.reshape(NZ, local_width, seq_len)
     pieces = lax.all_to_all(part, "zh", 0, 0)
     total = jnp.sum(pieces.astype(jnp.float32), axis=0)
     result = mine.astype(jnp.float32) + total + out_bias[:, None]

time: 206 us -> 263 us (1.28)
  the two profiles are of different devices: /device:TPU:26 before, /device:TPU:16 now
where the time goes in v5:
time: 263 us
  blocking collectives  127 us (48%)
  waiting for transfers between devices  88.6 us (34%)
  between operations  14.2 us (5%)
  starting transfers between devices  10.3 us (4%)
  matrix products  6.91 us (3%)
  local copies, waits for them, and re-layouts  6.42 us (2%)
  other arithmetic  5.7 us (2%)
  Pallas kernels  3.54 us (1%)
    all_to_all x2, blocking collectives, gather_direct(): lax.all_to_all(jnp.broadcast_to(block, (count,) + block.shape), axis, 0, 0)  89.1 us
    ppermute x1, waiting for transfers between devices, swap_out_weights(): return lax.ppermute(w_out.T, ('x', 'zlh', 'zll', 'c', 'y'), pairs)  75 us
    all_to_all x1, blocking collectives, per_device(): pieces = lax.all_to_all(part, 'zh', 0, 0)  38 us
    all_gather x1, waiting for transfers between devices, per_device(): w_rows = lax.all_gather(swapped + zgroup[0, 0] * 0, DP, axis=0, tiled=True)  13.6 us
    all_to_all x1, starting transfers between devices, gather_direct(): lax.all_to_all(jnp.broadcast_to(block, (count,) + block.shape), axis, 0, 0)  7.43 us
    dot_general x1, matrix products, per_device(): lax.dot_general(w_in, normed, (((0,), (0,)), ((), ())), preferred_element...  6.32 us
  transfers between devices with their start and end apart: 3, of which 2 were waited for; matrix products, arithmetic and copies ran while one was open for 5% of the time, Pallas kernels for 0%

profile of v5, /device:TPU:16, one launch (start us, length us, event | category | flops | bytes accessed | tf_op | source)
XLA Modules:
  0.0 262.9 jit_solution(5808858275242146989)
XLA Ops:
  6.5 0.9 broadcast_in_dim.8
  7.5 38.8 %all_to_all.20 = bf16[4,192,256]{2,1,0:T(8,128)(2,1)S(1)} all-to-all(bf16[4,192,256]{2,1,0:T(8,128)(2,1)S(1)} %broadcast_in_dim.8), channel_id=1, replica_groups=mesh['x'=4,'zlh'=2,'zll'=2,'c'=2,'y'=8,'zh'=4] {'zh'}, dimensions={0} | all-to-all | bytes 786432 | tf_op jit(solution)/shard_map/all_to_all | solution.py:25
  46.3 1.9 broadcast_in_dim.9
  48.2 7.4 %all-to-all-start.1 = ((bf16[8,768,256]{2,1,0:T(8,128)(2,1)}), bf16[8,768,256]{2,1,0:T(8,128)(2,1)S(1)}, u32[]{:S(2)}, u32[]{:S(2)}) async-start(bf16[8,768,256]{2,1,0:T(8,128)(2,1)} %broadcast_in_dim.9), calls=%async_computation.1 | async-start | bytes 6291456 | tf_op jit(solution)/shard_map/all_to_all | solution.py:25
  55.6 0.0 all-gather.2.cloned.1.call-start
  55.6 2.9 %collective-permute-start = (bf16[192,512]{1,0:T(8,128)(2,1)}, bf16[192,512]{1,0:T(8,128)(2,1)S(1)}, u32[]{:S(2)}, u32[]{:S(2)}) collective-permute-start(bf16[192,512]{1,0:T(8,128)(2,1)} %bitcast.40), channel_id=1, source_target_pairs={{0,0},{4,128},{8,256},{12,384},{16,512},{20,640},{24,768},{28,896}... | collective-permute-start | bytes 589832 | tf_op jit(solution)/shard_map/ppermute | solution.py:35
  58.5 0.5 slice.21
  59.0 0.0 copy-start.2
  59.7 75.0 %collective-permute-done = bf16[192,512]{1,0:T(8,128)(2,1)S(1)} collective-permute-done((bf16[192,512]{1,0:T(8,128)(2,1)}, bf16[192,512]{1,0:T(8,128)(2,1)S(1)}, u32[]{:S(2)}, u32[]{:S(2)}) %collective-permute-start) | collective-permute-done | bytes 196640 | tf_op jit(solution)/shard_map/ppermute | solution.py:35
  134.7 0.7 broadcast_add_fusion
  135.4 0.0 all-gather.2.cloned.1.call-update
  135.4 0.0 all-to-all-done.1
  135.4 0.8 convert_reduce_fusion
  136.3 0.9 multiply_reduce_fusion
  137.2 0.0 copy-done.2
  137.2 1.1 fusion.2
  138.3 0.0 copy-start.5
  138.3 0.0 copy-start.6
  138.3 0.0 copy-start.3
  138.3 6.3 %convolution_bitcast_fusion = f32[768,256]{0,1:T(8,128)S(1)} fusion(bf16[6144,256]{1,0:T(8,128)(2,1)S(1)} %fusion.2, bf16[6144,768]{1,0:T(8,128)(2,1)} %param.10), kind=kOutput, calls=%fused_computation.6 | convolution fusion | flops 2415919104 | bytes 13369344 | tf_op jit(solution)/shard_map/dot_general | solution.py:86
  144.6 0.1 slice_reduce_fusion.1
  144.8 0.3 multiply_reduce_fusion.2
  145.1 0.0 copy-done.5
  145.1 0.0 copy-done.6
  145.1 0.3 fusion.27
  145.4 0.1 fusion.13
  145.5 0.2 convolution_convert_fusion
  145.8 0.0 copy-done.3
  145.8 0.9 fusion.5
  146.7 0.1 copy.12
  146.8 0.1 broadcast_in_dim.10
  147.0 0.0 copy-start.1
  147.0 0.0 copy-start.4
  147.0 50.3 %all_to_all.21.h_ref = bf16[8,512,256]{2,1,0:T(8,128)(2,1)S(1)} all-to-all(bf16[8,512,256]{2,1,0:T(8,128)(2,1)S(1)} %broadcast_in_dim.10), channel_id=1, replica_groups=mesh['x'=4,'zlh'=2,'zll'=2,'c'=2,'y'=8,'zh'=4] {'y'}, dimensions={0} | all-to-all | bytes 4194304 | tf_op jit(solution)/shard_map/all_to_all | solution.py:25
  197.3 13.6 %all-gather.2.cloned.1.call-done = bf16[6144,512]{1,0:T(8,128)(2,1)} async-done(((bf16[192,512]{1,0:T(8,128)(2,1)}), bf16[6144,512]{1,0:T(8,128)(2,1)}) %all-gather.2.cloned.1.call-update) | async-done | bytes 6291472 | tf_op jit(solution)/shard_map/all_gather | solution.py:82
  210.9 0.0 copy-start
  210.9 2.8 %copy-done = bf16[6144,512]{1,0:T(8,128)(2,1)S(1)} copy-done((bf16[6144,512]{1,0:T(8,128)(2,1)S(1)}, bf16[6144,512]{1,0:T(8,128)(2,1)}, u32[]{:S(2)}) %copy-start) | copy-done | bytes 6291480
  213.7 3.5 %shard_map.82 = bf16[768,256]{1,0:T(8,128)(2,1)S(1)} custom-call(bf16[8,768,512]{2,1,0:T(8,128)(2,1)S(1)} %bitcast.33, bf16[8,512,256]{2,1,0:T(8,128)(2,1)S(1)} %all_to_all.21.h_ref), custom_call_target="tpu_custom_call" | custom-call | flops 1610612736 | bytes 8388608 | tf_op jit(solution)/shard_map/pallas_call | solution.py:58
  217.2 38.0 %all_to_all.22 = bf16[4,192,256]{2,1,0:T(8,128)(2,1)S(1)} all-to-all(bf16[4,192,256]{2,1,0:T(8,128)(2,1)S(1)} %bitcast.34), channel_id=1, replica_groups=mesh['x'=4,'zlh'=2,'zll'=2,'c'=2,'y'=8,'zh'=4] {'zh'}, dimensions={0} | all-to-all | bytes 786432 | tf_op jit(solution)/shard_map/all_to_all | solution.py:102
  255.3 0.0 copy-done.1
  255.3 0.0 copy-done.4
  255.3 0.7 fusion.20
  (7 shorter events, 0.1 us)
Async XLA Ops:
  48.2 87.3 %all-to-all-start.1 = ((bf16[8,768,256]{2,1,0:T(8,128)(2,1)}), bf16[8,768,256]{2,1,0:T(8,128)(2,1)S(1)}, u32[]{:S(2)}, u32[]{:S(2)}) async-start(bf16[8,768,256]{2,1,0:T(8,128)(2,1)} %broadcast_in_dim.9), calls=%async_computation.1 | async-start | bytes 6291456 | tf_op jit(solution)/shard_map/all_to_all | solution.py:25
  55.6 155.3 %all-gather.2.cloned.1.call-start = ((), (), s32[]{:S(2)}) async-start(), calls=%async_computation.4 | async-start | bytes 6488064 | tf_op jit(solution)/shard_map/all_gather | solution.py:82
  55.6 79.1 %collective-permute-start = (bf16[192,512]{1,0:T(8,128)(2,1)}, bf16[192,512]{1,0:T(8,128)(2,1)S(1)}, u32[]{:S(2)}, u32[]{:S(2)}) collective-permute-start(bf16[192,512]{1,0:T(8,128)(2,1)} %bitcast.40), channel_id=1, source_target_pairs={{0,0},{4,128},{8,256},{12,384},{16,512},{20,640},{24,768},{28,896}... | collective-permute-start | bytes 589832 | tf_op jit(solution)/shard_map/ppermute | solution.py:35
  59.0 78.2 %copy-start.2 = (f32[6144]{0:T(1024)S(1)}, f32[6144]{0:T(1024)}, u32[]{:S(2)}) copy-start(f32[6144]{0:T(1024)} %param.9) | copy-start | bytes 73732
  138.3 6.8 %copy-start.5 = (f32[1,128]{1,0:T(1,128)S(1)}, f32[1,128]{1,0:T(1,128)}, u32[]{:S(2)}) copy-start(f32[1,128]{1,0:T(1,128)} %param.12) | copy-start | bytes 1540
  138.3 6.8 %copy-start.6 = (f32[1,128]{1,0:T(1,128)S(1)}, f32[1,128]{1,0:T(1,128)}, u32[]{:S(2)}) copy-start(f32[1,128]{1,0:T(1,128)} %param.11) | copy-start | bytes 1540
  138.3 7.5 %copy-start.3 = (f32[384]{0:T(512)S(1)}, f32[384]{0:T(512)}, u32[]{:S(2)}) copy-start(f32[384]{0:T(512)} %param.13) | copy-start | bytes 4612
  147.0 108.3 %copy-start.1 = (bf16[1,256,192]{1,2,0:T(8,128)(2,1)S(1)}, bf16[1,256,192]{1,2,0:T(8,128)(2,1)}, u32[]{:S(2)}) copy-start(bf16[1,256,192]{1,2,0:T(8,128)(2,1)} %param.8) | copy-start | bytes 294916
  147.0 108.3 %copy-start.4 = (f32[192]{0:T(256)S(1)}, f32[192]{0:T(256)}, u32[]{:S(2)}) copy-start(f32[192]{0:T(256)} %param.15) | copy-start | bytes 2308
  210.9 2.8 %copy-start = (bf16[6144,512]{1,0:T(8,128)(2,1)S(1)}, bf16[6144,512]{1,0:T(8,128)(2,1)}, u32[]{:S(2)}) copy-start(bf16[6144,512]{1,0:T(8,128)(2,1)} %all-gather.2.cloned.1.call-done) | copy-start | bytes 18874372
Sparse Core Ops, SparseCore 0:
  135.6 75.3 all-gather.1

commit v6 on v5

--- a/solution.py
+++ b/solution.py
@@ -21,8 +21,34 @@
     return center * lax.rsqrt(spread + EPS)
 
 
-def gather_direct(block, axis, count):
-    return lax.all_to_all(jnp.broadcast_to(block, (count,) + block.shape), axis, 0, 0)
+def shift(value, axis, count, by):
+    return lax.ppermute(value, axis, [(i, (i + by) % count) for i in range(count)])
+
+
+def gather_y(block):
+    half = block.shape[0] // 2
+    below2, above2 = shift(block, "y", NY, 2), shift(block, "y", NY, -2)
+    below1, above1 = shift(block, "y", NY, 1), shift(block, "y", NY, -1)
+    below3, above3 = shift(below2, "y", NY, 1), shift(above2, "y", NY, -1)
+    far_top = shift(below2[:half], "y", NY, 2)
+    far_bottom = shift(above2[half:], "y", NY, -2)
+    return (below2, below1, block, above1, above2), (above3, far_top, far_bottom, below3)
+
+
+def gather_in_order(block):
+    y = lax.axis_index("y")
+    half = block.shape[0] // 2
+    near, (above3, far_top, far_bottom, below3) = gather_y(block)
+    whole = jnp.zeros((NY,) + block.shape, block.dtype)
+    put = lambda whole, part, index, row: lax.dynamic_update_slice(
+        whole, part[None], (index & (NY - 1), row, 0)
+    )
+    for i, part in enumerate(near):
+        whole = put(whole, part, y + NY - 2 + i, 0)
+    whole = put(whole, above3, y + 3, 0)
+    whole = put(whole, below3, y + 5, 0)
+    whole = put(whole, far_top, y + 4, 0)
+    return put(whole, far_bottom, y + 4, half)
 
 
 def swap_out_weights(w_out):
@@ -35,11 +61,11 @@
     return lax.ppermute(w_out.T, ("x", "zlh", "zll", "c", "y"), pairs)
 
 
-def multiply_out(weights, hidden):
+def multiply_out(weights, hidden, first):
     count, rows, depth = weights.shape
     columns = hidden.shape[2]
 
-    def kernel(w_ref, h_ref, o_ref, total_ref):
+    def kernel(first_ref, w_ref, h_ref, o_ref, total_ref):
         step = pl.program_id(0)
         product = jnp.dot(w_ref[0], h_ref[0], preferred_element_type=jnp.float32)
 
@@ -57,31 +83,36 @@
 
     return pl.pallas_call(
         kernel,
-        grid=(count,),
-        in_specs=[
-            pl.BlockSpec((1, rows, depth), lambda i: (i, 0, 0)),
-            pl.BlockSpec((1, depth, columns), lambda i: (i, 0, 0)),
-        ],
-        out_specs=pl.BlockSpec((rows, columns), lambda i: (0, 0)),
+        grid_spec=pltpu.PrefetchScalarGridSpec(
+            num_scalar_prefetch=1,
+            grid=(count,),
+            in_specs=[
+                pl.BlockSpec(
+                    (1, rows, depth), lambda i, first_ref: ((first_ref[0] + i) & (count - 1), 0, 0)
+                ),
+                pl.BlockSpec((1, depth, columns), lambda i, first_ref: (i, 0, 0)),
+            ],
+            out_specs=pl.BlockSpec((rows, columns), lambda i, first_ref: (0, 0)),
+            scratch_shapes=[pltpu.VMEM((rows, columns), jnp.float32)],
+        ),
         out_shape=jax.ShapeDtypeStruct((rows, columns), jnp.bfloat16),
-        scratch_shapes=[pltpu.VMEM((rows, columns), jnp.float32)],
         compiler_params=pltpu.CompilerParams(vmem_limit_bytes=16 * 1024 * 1024),
         cost_estimate=pl.CostEstimate(
             flops=2 * count * rows * depth * columns,
             bytes_accessed=2 * count * depth * (rows + columns),
             transcendentals=0,
         ),
-    )(weights, hidden)
+    )(first[None], weights, hidden)
 
 
 def per_device(patches, norm_gain, w_in, q_gain, k_gain, mlp_bias, w_out, out_bias):
     images, seq_len, local_width = patches.shape
     mine = patches[0].T
     swapped = swap_out_weights(w_out)
-    zgroup = gather_direct(mine, "zh", NZ).reshape(NZ * local_width, seq_len)
+    zgroup = lax.all_gather(mine, "zh", axis=0, tiled=True)
     w_rows = lax.all_gather(swapped + zgroup[0, 0] * 0, DP, axis=0, tiled=True)
     w_rows = w_rows.reshape(NY, NZ * local_width, -1)
-    whole = gather_direct(zgroup, "y", NY).reshape(-1, seq_len)
+    whole = gather_in_order(zgroup).reshape(-1, seq_len)
     normed = (normalize(whole.astype(jnp.float32), 0) * norm_gain[:, None]).astype(jnp.bfloat16)
     project = lax.dot_general(
         w_in, normed, (((0,), (0,)), ((), ())), preferred_element_type=jnp.float32
@@ -97,7 +128,10 @@
     ).astype(jnp.bfloat16)
     mlp_hidden = jax.nn.gelu(project[3 * head :] + mlp_bias[:, None], approximate=False)
     hidden = jnp.concatenate([attended, mlp_hidden.astype(jnp.bfloat16)], axis=0)
-    part = multiply_out(w_rows, gather_direct(hidden, "y", NY))
+    near, (above3, far_top, far_bottom, below3) = gather_y(hidden)
+    far = jnp.concatenate([far_top, far_bottom], axis=0)
+    hidden_all = jnp.stack(near + (above3, far, below3))
+    part = multiply_out(w_rows, hidden_all, lax.axis_index("y") + NY - 2)
     part = part.reshape(NZ, local_width, seq_len)
     pieces = lax.all_to_all(part, "zh", 0, 0)
     total = jnp.sum(pieces.astype(jnp.float32), axis=0)

time: 263 us -> 192 us (0.73)
  the two profiles are of different devices: /device:TPU:16 before, /device:TPU:64 now
where the time goes in v6:
time: 192 us; the launch traced here: 191 us
  starting transfers between devices  75.9 us (40%)
  blocking collectives  64.2 us (33%)
  waiting for transfers between devices  18.8 us (10%)
  between operations  14.7 us (8%)
  other arithmetic  5.51 us (3%)
  matrix products  4.33 us (2%)
  local copies, waits for them, and re-layouts  3.98 us (2%)
  Pallas kernels  3.56 us (2%)
    ppermute x16, starting transfers between devices, shift(): lax.ppermute(value, axis, [(i, (i + by) % count) for i in range(count)])  74.3 us
    all_gather x1, blocking collectives, per_device(): zgroup = lax.all_gather(mine, 'zh', axis=0, tiled=True)  32.3 us
    all_to_all x1, blocking collectives, per_device(): pieces = lax.all_to_all(part, 'zh', 0, 0)  32 us
    ppermute x16, waiting for transfers between devices, shift(): lax.ppermute(value, axis, [(i, (i + by) % count) for i in range(count)])  18.7 us
  transfers between devices with their start and end apart: 18, of which 3 were waited for; matrix products, arithmetic and copies ran while one was open for 5% of the time, Pallas kernels for 0%

profile of v6, /device:TPU:64, one launch (start us, length us, event | category | flops | bytes accessed | tf_op | source)
XLA Modules:
  0.0 191.0 jit_solution(4236429857487413181)
XLA Ops:
  6.5 1.6 collective-permute-start
  8.1 32.3 %all_gather.6 = bf16[768,256]{1,0:T(8,128)(2,1)S(1)} all-gather(bf16[192,256]{1,0:T(8,128)(2,1)} %bitcast.71), channel_id=1, replica_groups=mesh['x'=4,'zlh'=2,'zll'=2,'c'=2,'y'=8,'zh'=4] {'zh'}, dimensions={0}, use_global_device_ids=true | all-gather | bytes 491520 | tf_op jit(solution)/shard_map/all_gather | solution.py:112
  40.4 0.5 slice.37
  41.6 0.0 collective-permute-done
  41.6 0.7 broadcast_add_fusion
  42.2 0.0 all-gather.2.cloned.1.call-update
  42.3 7.2 %collective-permute-start.1 = (bf16[768,256]{1,0:T(8,128)(2,1)S(1)}, bf16[768,256]{1,0:T(8,128)(2,1)S(1)}, u32[]{:S(2)}, u32[]{:S(2)}) collective-permute-start(bf16[768,256]{1,0:T(8,128)(2,1)S(1)} %all_gather.6), channel_id=1, source_target_pairs={{0,8},{4,12},{8,16},{12,20},{16,24},{20,28},{24,0},{28,4},{1,9},{5... | collective-permute-start | bytes 1179656 | tf_op jit(solution)/shard_map/ppermute | solution.py:25
  49.4 2.8 %collective-permute-start.4 = (bf16[768,256]{1,0:T(8,128)(2,1)S(1)}, bf16[768,256]{1,0:T(8,128)(2,1)S(1)}, u32[]{:S(2)}, u32[]{:S(2)}) collective-permute-start(bf16[768,256]{1,0:T(8,128)(2,1)S(1)} %all_gather.6), channel_id=1, source_target_pairs={{0,24},{4,28},{8,0},{12,4},{16,8},{20,12},{24,16},{28,20},{1,25},{... | collective-permute-start | bytes 1179656 | tf_op jit(solution)/shard_map/ppermute | solution.py:25
  52.2 15.6 %collective-permute-start.2 = (bf16[768,256]{1,0:T(8,128)(2,1)S(1)}, bf16[768,256]{1,0:T(8,128)(2,1)S(1)}, u32[]{:S(2)}, u32[]{:S(2)}) collective-permute-start(bf16[768,256]{1,0:T(8,128)(2,1)S(1)} %all_gather.6), channel_id=1, source_target_pairs={{0,4},{4,8},{8,12},{12,16},{16,20},{20,24},{24,28},{28,0},{1,5},{5... | collective-permute-start | bytes 1179656 | tf_op jit(solution)/shard_map/ppermute | solution.py:25
  67.9 3.4 %collective-permute-start.3 = (bf16[768,256]{1,0:T(8,128)(2,1)S(1)}, bf16[768,256]{1,0:T(8,128)(2,1)S(1)}, u32[]{:S(2)}, u32[]{:S(2)}) collective-permute-start(bf16[768,256]{1,0:T(8,128)(2,1)S(1)} %all_gather.6), channel_id=1, source_target_pairs={{0,28},{4,0},{8,4},{12,8},{16,12},{20,16},{24,20},{28,24},{1,29},{... | collective-permute-start | bytes 1179656 | tf_op jit(solution)/shard_map/ppermute | solution.py:25
  71.3 0.0 collective-permute-done.1
  71.3 0.0 slice-start
  71.3 2.7 %collective-permute-start.7 = (bf16[384,256]{1,0:T(8,128)(2,1)S(1)}, bf16[384,256]{1,0:T(8,128)(2,1)S(1)}, u32[]{:S(2)}, u32[]{:S(2)}) collective-permute-start(bf16[384,256]{1,0:T(8,128)(2,1)S(1)} %slice.38), channel_id=1, source_target_pairs={{0,8},{4,12},{8,16},{12,20},{16,24},{20,28},{24,0},{28,4},{1,9},{5... | collective-permute-start | bytes 589832 | tf_op jit(solution)/shard_map/ppermute | solution.py:25
  74.0 0.0 collective-permute-done.4
  74.1 5.5 %collective-permute-start.8 = (bf16[384,256]{1,0:T(8,128)(2,1)S(1)}, bf16[384,256]{1,0:T(8,128)(2,1)S(1)}, u32[]{:S(2)}, u32[]{:S(2)}) collective-permute-start(bf16[384,256]{1,0:T(8,128)(2,1)S(1)} %slice.39), channel_id=1, source_target_pairs={{0,24},{4,28},{8,0},{12,4},{16,8},{20,12},{24,16},{28,20},{1,25},{... | collective-permute-start | bytes 589832 | tf_op jit(solution)/shard_map/ppermute | solution.py:25
  79.6 5.1 %collective-permute-start.5 = (bf16[768,256]{1,0:T(8,128)(2,1)S(1)}, bf16[768,256]{1,0:T(8,128)(2,1)S(1)}, u32[]{:S(2)}, u32[]{:S(2)}) collective-permute-start(bf16[768,256]{1,0:T(8,128)(2,1)S(1)} %collective-permute-done.4), channel_id=1, source_target_pairs={{0,28},{4,0},{8,4},{12,8},{16,12},{20,16},{24,20},{28,24},{1,29},{... | collective-permute-start | bytes 1179656 | tf_op jit(solution)/shard_map/ppermute | solution.py:25
  84.7 0.2 broadcast_in_dim.48
  85.0 0.0 collective-permute-done.2
  85.0 2.3 %collective-permute-start.6 = (bf16[768,256]{1,0:T(8,128)(2,1)S(1)}, bf16[768,256]{1,0:T(8,128)(2,1)S(1)}, u32[]{:S(2)}, u32[]{:S(2)}) collective-permute-start(bf16[768,256]{1,0:T(8,128)(2,1)S(1)} %collective-permute-done.1), channel_id=1, source_target_pairs={{0,4},{4,8},{8,12},{12,16},{16,20},{20,24},{24,28},{28,0},{1,5},{5... | collective-permute-start | bytes 1179656 | tf_op jit(solution)/shard_map/ppermute | solution.py:25
  87.4 0.0 collective-permute-done.3
  87.4 0.0 slice-start.1
  87.5 11.2 %collective-permute-done.5 = bf16[768,256]{1,0:T(8,128)(2,1)S(1)} collective-permute-done((bf16[768,256]{1,0:T(8,128)(2,1)S(1)}, bf16[768,256]{1,0:T(8,128)(2,1)S(1)}, u32[]{:S(2)}, u32[]{:S(2)}) %collective-permute-start.5) | collective-permute-done | bytes 393248 | tf_op jit(solution)/shard_map/ppermute | solution.py:25
  98.7 0.0 collective-permute-done.6
  98.8 0.0 collective-permute-done.7
  98.8 0.0 collective-permute-done.8
  98.9 0.0 copy-start.2
  98.9 0.8 convert_reduce_fusion
  99.7 0.9 multiply_reduce_fusion
  100.6 1.1 fusion.2
  101.7 0.0 slice-done
  101.7 0.0 slice-done.1
  101.8 0.0 slice-done.2
  101.8 0.0 copy-start.5
  101.8 0.0 copy-start.6
  101.8 0.0 copy-start.3
  101.8 3.8 %convolution_bitcast_fusion = f32[768,256]{1,0:T(8,128)S(1)} fusion(bf16[6144,256]{1,0:T(8,128)(2,1)S(1)} %fusion.2, bf16[6144,768]{1,0:T(8,128)(2,1)S(1)} %bitcast.75), kind=kOutput, calls=%fused_computation.6 | convolution fusion | flops 2415919104 | bytes 13369344 | tf_op jit(solution)/shard_map/dot_general | solution.py:117
  105.8 0.0 copy-done.5
  105.8 0.0 copy-done.6
  105.8 0.3 fusion.28
  106.1 0.1 fusion.14
  106.2 0.2 convolution_convert_fusion
  106.4 0.0 copy-done.3
  106.4 1.0 fusion.5
  107.4 4.0 %collective-permute-start.9 = (bf16[512,256]{1,0:T(8,128)(2,1)S(1)}, bf16[512,256]{1,0:T(8,128)(2,1)S(1)}, u32[]{:S(2)}, u32[]{:S(2)}) collective-permute-start(bf16[512,256]{1,0:T(8,128)(2,1)S(1)} %pad_maximum_fusion), channel_id=1, source_target_pairs={{0,8},{4,12},{8,16},{12,20},{16,24},{20,28},{24,0},{28,4},{1,9},{5... | collective-permute-start | bytes 786440 | tf_op jit(solution)/shard_map/ppermute | solution.py:25
  111.4 4.0 %collective-permute-start.12 = (bf16[512,256]{1,0:T(8,128)(2,1)S(1)}, bf16[512,256]{1,0:T(8,128)(2,1)S(1)}, u32[]{:S(2)}, u32[]{:S(2)}) collective-permute-start(bf16[512,256]{1,0:T(8,128)(2,1)S(1)} %pad_maximum_fusion), channel_id=1, source_target_pairs={{0,24},{4,28},{8,0},{12,4},{16,8},{20,12},{24,16},{28,20},{1,25},{... | collective-permute-start | bytes 786440 | tf_op jit(solution)/shard_map/ppermute | solution.py:25
  115.4 4.0 %collective-permute-start.10 = (bf16[512,256]{1,0:T(8,128)(2,1)S(1)}, bf16[512,256]{1,0:T(8,128)(2,1)S(1)}, u32[]{:S(2)}, u32[]{:S(2)}) collective-permute-start(bf16[512,256]{1,0:T(8,128)(2,1)S(1)} %pad_maximum_fusion), channel_id=1, source_target_pairs={{0,4},{4,8},{8,12},{12,16},{16,20},{20,24},{24,28},{28,0},{1,5},{5... | collective-permute-start | bytes 786440 | tf_op jit(solution)/shard_map/ppermute | solution.py:25
  119.3 3.1 %collective-permute-start.11 = (bf16[512,256]{1,0:T(8,128)(2,1)S(1)}, bf16[512,256]{1,0:T(8,128)(2,1)S(1)}, u32[]{:S(2)}, u32[]{:S(2)}) collective-permute-start(bf16[512,256]{1,0:T(8,128)(2,1)S(1)} %pad_maximum_fusion), channel_id=1, source_target_pairs={{0,28},{4,0},{8,4},{12,8},{16,12},{20,16},{24,20},{28,24},{1,29},{... | collective-permute-start | bytes 786440 | tf_op jit(solution)/shard_map/ppermute | solution.py:25
  122.4 0.0 collective-permute-done.9
  122.5 5.5 %collective-permute-start.14 = (bf16[256,256]{1,0:T(8,128)(2,1)S(1)}, bf16[256,256]{1,0:T(8,128)(2,1)S(1)}, u32[]{:S(2)}, u32[]{:S(2)}) collective-permute-start(bf16[256,256]{1,0:T(8,128)(2,1)S(1)} %slice.44), channel_id=1, source_target_pairs={{0,8},{4,12},{8,16},{12,20},{16,24},{20,28},{24,0},{28,4},{1,9},{5... | collective-permute-start | bytes 393224 | tf_op jit(solution)/shard_map/ppermute | solution.py:25
  128.0 0.0 collective-permute-done.12
  128.0 2.4 %collective-permute-start.15 = (bf16[256,256]{1,0:T(8,128)(2,1)S(1)}, bf16[256,256]{1,0:T(8,128)(2,1)S(1)}, u32[]{:S(2)}, u32[]{:S(2)}) collective-permute-start(bf16[256,256]{1,0:T(8,128)(2,1)S(1)} %slice.45), channel_id=1, source_target_pairs={{0,24},{4,28},{8,0},{12,4},{16,8},{20,12},{24,16},{28,20},{1,25},{... | collective-permute-start | bytes 393224 | tf_op jit(solution)/shard_map/ppermute | solution.py:25
  130.5 4.0 %collective-permute-start.13 = (bf16[512,256]{1,0:T(8,128)(2,1)S(1)}, bf16[512,256]{1,0:T(8,128)(2,1)S(1)}, u32[]{:S(2)}, u32[]{:S(2)}) collective-permute-start(bf16[512,256]{1,0:T(8,128)(2,1)S(1)} %collective-permute-done.12), channel_id=1, source_target_pairs={{0,28},{4,0},{8,4},{12,8},{16,12},{20,16},{24,20},{28,24},{1,29},{... | collective-permute-start | bytes 786440 | tf_op jit(solution)/shard_map/ppermute | solution.py:25
  134.5 0.0 collective-permute-done.10
  134.5 2.8 %collective-permute-start.16 = (bf16[512,256]{1,0:T(8,128)(2,1)S(1)}, bf16[512,256]{1,0:T(8,128)(2,1)S(1)}, u32[]{:S(2)}, u32[]{:S(2)}) collective-permute-start(bf16[512,256]{1,0:T(8,128)(2,1)S(1)} %collective-permute-done.9), channel_id=1, source_target_pairs={{0,4},{4,8},{8,12},{12,16},{16,20},{20,24},{24,28},{28,0},{1,5},{5... | collective-permute-start | bytes 786440 | tf_op jit(solution)/shard_map/ppermute | solution.py:25
  137.4 0.0 collective-permute-done.11
  137.4 6.8 %collective-permute-done.13 = bf16[512,256]{1,0:T(8,128)(2,1)S(1)} collective-permute-done((bf16[512,256]{1,0:T(8,128)(2,1)S(1)}, bf16[512,256]{1,0:T(8,128)(2,1)S(1)}, u32[]{:S(2)}, u32[]{:S(2)}) %collective-permute-start.13) | collective-permute-done | bytes 262176 | tf_op jit(solution)/shard_map/ppermute | solution.py:25
  144.3 0.0 collective-permute-done.14
  144.3 0.0 collective-permute-done.15
  144.3 0.7 collective-permute-done.16
  145.0 0.0 all-gather.2.cloned.1.call-done
  145.0 2.8 %copy-done = bf16[6144,512]{1,0:T(8,128)(2,1)S(1)} copy-done((bf16[6144,512]{1,0:T(8,128)(2,1)S(1)}, bf16[6144,512]{1,0:T(8,128)(2,1)}, u32[]{:S(2)}) %copy-start) | copy-done | bytes 6291480
  147.8 3.6 %shard_map.82 = bf16[768,256]{1,0:T(8,128)(2,1)S(1)} custom-call(s32[1]{0:T(128)} %bitcast.1.first_ref, bf16[8,768,512]{2,1,0:T(8,128)(2,1)S(1)} %bitcast.69, bf16[8,512,256]{2,1,0:T(8,128)(2,1)S(1)} %bitcast_dynamic-update-slice_fusion.7.h_ref), custom_call_target="tpu_custom_call" | custom-call | flops 1610612736 | bytes 8388608 | tf_op jit(solution)/shard_map/pallas_call | solution.py:84
  151.4 32.0 %all_to_all.5 = bf16[4,192,256]{2,1,0:T(8,128)(2,1)S(1)} all-to-all(bf16[4,192,256]{2,1,0:T(8,128)(2,1)S(1)} %bitcast.70), channel_id=1, replica_groups=mesh['x'=4,'zlh'=2,'zll'=2,'c'=2,'y'=8,'zh'=4] {'zh'}, dimensions={0} | all-to-all | bytes 786432 | tf_op jit(solution)/shard_map/all_to_all | solution.py:136
  183.4 0.7 fusion.21
  (39 shorter events, 0.7 us)
Async XLA Ops:
  6.5 138.5 %all-gather.2.cloned.1.call-start = ((), (), s32[]{:S(2)}) async-start(), calls=%async_computation.1 | async-start | bytes 6488064 | tf_op jit(solution)/shard_map/all_gather | solution.py:113
  6.5 35.0 %collective-permute-start = (bf16[192,512]{1,0:T(8,128)(2,1)}, bf16[192,512]{1,0:T(8,128)(2,1)S(1)}, u32[]{:S(2)}, u32[]{:S(2)}) collective-permute-start(bf16[192,512]{1,0:T(8,128)(2,1)} %bitcast.76), channel_id=1, source_target_pairs={{0,0},{4,128},{8,256},{12,384},{16,512},{20,640},{24,768},{28,896}... | collective-permute-start | bytes 589832 | tf_op jit(solution)/shard_map/ppermute | solution.py:61
  42.3 29.0 %collective-permute-start.1 = (bf16[768,256]{1,0:T(8,128)(2,1)S(1)}, bf16[768,256]{1,0:T(8,128)(2,1)S(1)}, u32[]{:S(2)}, u32[]{:S(2)}) collective-permute-start(bf16[768,256]{1,0:T(8,128)(2,1)S(1)} %all_gather.6), channel_id=1, source_target_pairs={{0,8},{4,12},{8,16},{12,20},{16,24},{20,28},{24,0},{28,4},{1,9},{5... | collective-permute-start | bytes 1179656 | tf_op jit(solution)/shard_map/ppermute | solution.py:25
  49.4 24.6 %collective-permute-start.4 = (bf16[768,256]{1,0:T(8,128)(2,1)S(1)}, bf16[768,256]{1,0:T(8,128)(2,1)S(1)}, u32[]{:S(2)}, u32[]{:S(2)}) collective-permute-start(bf16[768,256]{1,0:T(8,128)(2,1)S(1)} %all_gather.6), channel_id=1, source_target_pairs={{0,24},{4,28},{8,0},{12,4},{16,8},{20,12},{24,16},{28,20},{1,25},{... | collective-permute-start | bytes 1179656 | tf_op jit(solution)/shard_map/ppermute | solution.py:25
  52.2 32.8 %collective-permute-start.2 = (bf16[768,256]{1,0:T(8,128)(2,1)S(1)}, bf16[768,256]{1,0:T(8,128)(2,1)S(1)}, u32[]{:S(2)}, u32[]{:S(2)}) collective-permute-start(bf16[768,256]{1,0:T(8,128)(2,1)S(1)} %all_gather.6), channel_id=1, source_target_pairs={{0,4},{4,8},{8,12},{12,16},{16,20},{20,24},{24,28},{28,0},{1,5},{5... | collective-permute-start | bytes 1179656 | tf_op jit(solution)/shard_map/ppermute | solution.py:25
  67.9 19.5 %collective-permute-start.3 = (bf16[768,256]{1,0:T(8,128)(2,1)S(1)}, bf16[768,256]{1,0:T(8,128)(2,1)S(1)}, u32[]{:S(2)}, u32[]{:S(2)}) collective-permute-start(bf16[768,256]{1,0:T(8,128)(2,1)S(1)} %all_gather.6), channel_id=1, source_target_pairs={{0,28},{4,0},{8,4},{12,8},{16,12},{20,16},{24,20},{28,24},{1,29},{... | collective-permute-start | bytes 1179656 | tf_op jit(solution)/shard_map/ppermute | solution.py:25
  71.3 30.5 %slice-start = ((s8[9437184]{0:T(1024)(128)(4,1)}), s8[4194304]{0:T(1024)(128)(4,1)S(1)}, s32[]{:S(2)}) async-start(s8[9437184]{0:T(1024)(128)(4,1)} %bitcast.74), calls=%async_computation.2 | async-start | bytes 8388608
  71.3 27.5 %collective-permute-start.7 = (bf16[384,256]{1,0:T(8,128)(2,1)S(1)}, bf16[384,256]{1,0:T(8,128)(2,1)S(1)}, u32[]{:S(2)}, u32[]{:S(2)}) collective-permute-start(bf16[384,256]{1,0:T(8,128)(2,1)S(1)} %slice.38), channel_id=1, source_target_pairs={{0,8},{4,12},{8,16},{12,20},{16,24},{20,28},{24,0},{28,4},{1,9},{5... | collective-permute-start | bytes 589832 | tf_op jit(solution)/shard_map/ppermute | solution.py:25
  74.1 24.8 %collective-permute-start.8 = (bf16[384,256]{1,0:T(8,128)(2,1)S(1)}, bf16[384,256]{1,0:T(8,128)(2,1)S(1)}, u32[]{:S(2)}, u32[]{:S(2)}) collective-permute-start(bf16[384,256]{1,0:T(8,128)(2,1)S(1)} %slice.39), channel_id=1, source_target_pairs={{0,24},{4,28},{8,0},{12,4},{16,8},{20,12},{24,16},{28,20},{1,25},{... | collective-permute-start | bytes 589832 | tf_op jit(solution)/shard_map/ppermute | solution.py:25
  79.6 19.1 %collective-permute-start.5 = (bf16[768,256]{1,0:T(8,128)(2,1)S(1)}, bf16[768,256]{1,0:T(8,128)(2,1)S(1)}, u32[]{:S(2)}, u32[]{:S(2)}) collective-permute-start(bf16[768,256]{1,0:T(8,128)(2,1)S(1)} %collective-permute-done.4), channel_id=1, source_target_pairs={{0,28},{4,0},{8,4},{12,8},{16,12},{20,16},{24,20},{28,24},{1,29},{... | collective-permute-start | bytes 1179656 | tf_op jit(solution)/shard_map/ppermute | solution.py:25
  85.0 13.7 %collective-permute-start.6 = (bf16[768,256]{1,0:T(8,128)(2,1)S(1)}, bf16[768,256]{1,0:T(8,128)(2,1)S(1)}, u32[]{:S(2)}, u32[]{:S(2)}) collective-permute-start(bf16[768,256]{1,0:T(8,128)(2,1)S(1)} %collective-permute-done.1), channel_id=1, source_target_pairs={{0,4},{4,8},{8,12},{12,16},{16,20},{20,24},{24,28},{28,0},{1,5},{5... | collective-permute-start | bytes 1179656 | tf_op jit(solution)/shard_map/ppermute | solution.py:25
  87.4 14.3 %slice-start.1 = ((s8[9437184]{0:T(1024)(128)(4,1)}), s8[4194304]{0:T(1024)(128)(4,1)S(1)}, s32[]{:S(2)}) async-start(s8[9437184]{0:T(1024)(128)(4,1)} %bitcast.74), calls=%async_computation.3 | async-start | bytes 8388608
  98.9 1.7 copy-start.2
  99.7 2.1 %slice-start.2 = ((s8[9437184]{0:T(1024)(128)(4,1)}), s8[1048576]{0:T(1024)(128)(4,1)S(1)}, s32[]{:S(2)}) async-start(s8[9437184]{0:T(1024)(128)(4,1)} %bitcast.74), calls=%async_computation.4 | async-start | bytes 2097152
  101.8 4.0 %copy-start.5 = (f32[1,128]{1,0:T(1,128)S(1)}, f32[1,128]{1,0:T(1,128)}, u32[]{:S(2)}) copy-start(f32[1,128]{1,0:T(1,128)} %param.12) | copy-start | bytes 1540
  101.8 4.0 %copy-start.6 = (f32[1,128]{1,0:T(1,128)S(1)}, f32[1,128]{1,0:T(1,128)}, u32[]{:S(2)}) copy-start(f32[1,128]{1,0:T(1,128)} %param.11) | copy-start | bytes 1540
  101.8 4.6 %copy-start.3 = (f32[384]{0:T(512)S(1)}, f32[384]{0:T(512)}, u32[]{:S(2)}) copy-start(f32[384]{0:T(512)} %param.13) | copy-start | bytes 4612
  107.4 15.0 %collective-permute-start.9 = (bf16[512,256]{1,0:T(8,128)(2,1)S(1)}, bf16[512,256]{1,0:T(8,128)(2,1)S(1)}, u32[]{:S(2)}, u32[]{:S(2)}) collective-permute-start(bf16[512,256]{1,0:T(8,128)(2,1)S(1)} %pad_maximum_fusion), channel_id=1, source_target_pairs={{0,8},{4,12},{8,16},{12,20},{16,24},{20,28},{24,0},{28,4},{1,9},{5... | collective-permute-start | bytes 786440 | tf_op jit(solution)/shard_map/ppermute | solution.py:25
  111.4 16.6 %collective-permute-start.12 = (bf16[512,256]{1,0:T(8,128)(2,1)S(1)}, bf16[512,256]{1,0:T(8,128)(2,1)S(1)}, u32[]{:S(2)}, u32[]{:S(2)}) collective-permute-start(bf16[512,256]{1,0:T(8,128)(2,1)S(1)} %pad_maximum_fusion), channel_id=1, source_target_pairs={{0,24},{4,28},{8,0},{12,4},{16,8},{20,12},{24,16},{28,20},{1,25},{... | collective-permute-start | bytes 786440 | tf_op jit(solution)/shard_map/ppermute | solution.py:25
  115.4 19.2 %collective-permute-start.10 = (bf16[512,256]{1,0:T(8,128)(2,1)S(1)}, bf16[512,256]{1,0:T(8,128)(2,1)S(1)}, u32[]{:S(2)}, u32[]{:S(2)}) collective-permute-start(bf16[512,256]{1,0:T(8,128)(2,1)S(1)} %pad_maximum_fusion), channel_id=1, source_target_pairs={{0,4},{4,8},{8,12},{12,16},{16,20},{20,24},{24,28},{28,0},{1,5},{5... | collective-permute-start | bytes 786440 | tf_op jit(solution)/shard_map/ppermute | solution.py:25
  119.3 18.0 %collective-permute-start.11 = (bf16[512,256]{1,0:T(8,128)(2,1)S(1)}, bf16[512,256]{1,0:T(8,128)(2,1)S(1)}, u32[]{:S(2)}, u32[]{:S(2)}) collective-permute-start(bf16[512,256]{1,0:T(8,128)(2,1)S(1)} %pad_maximum_fusion), channel_id=1, source_target_pairs={{0,28},{4,0},{8,4},{12,8},{16,12},{20,16},{24,20},{28,24},{1,29},{... | collective-permute-start | bytes 786440 | tf_op jit(solution)/shard_map/ppermute | solution.py:25
  122.5 21.8 %collective-permute-start.14 = (bf16[256,256]{1,0:T(8,128)(2,1)S(1)}, bf16[256,256]{1,0:T(8,128)(2,1)S(1)}, u32[]{:S(2)}, u32[]{:S(2)}) collective-permute-start(bf16[256,256]{1,0:T(8,128)(2,1)S(1)} %slice.44), channel_id=1, source_target_pairs={{0,8},{4,12},{8,16},{12,20},{16,24},{20,28},{24,0},{28,4},{1,9},{5... | collective-permute-start | bytes 393224 | tf_op jit(solution)/shard_map/ppermute | solution.py:25
  128.0 16.2 %collective-permute-start.15 = (bf16[256,256]{1,0:T(8,128)(2,1)S(1)}, bf16[256,256]{1,0:T(8,128)(2,1)S(1)}, u32[]{:S(2)}, u32[]{:S(2)}) collective-permute-start(bf16[256,256]{1,0:T(8,128)(2,1)S(1)} %slice.45), channel_id=1, source_target_pairs={{0,24},{4,28},{8,0},{12,4},{16,8},{20,12},{24,16},{28,20},{1,25},{... | collective-permute-start | bytes 393224 | tf_op jit(solution)/shard_map/ppermute | solution.py:25
  130.5 13.8 %collective-permute-start.13 = (bf16[512,256]{1,0:T(8,128)(2,1)S(1)}, bf16[512,256]{1,0:T(8,128)(2,1)S(1)}, u32[]{:S(2)}, u32[]{:S(2)}) collective-permute-start(bf16[512,256]{1,0:T(8,128)(2,1)S(1)} %collective-permute-done.12), channel_id=1, source_target_pairs={{0,28},{4,0},{8,4},{12,8},{16,12},{20,16},{24,20},{28,24},{1,29},{... | collective-permute-start | bytes 786440 | tf_op jit(solution)/shard_map/ppermute | solution.py:25
  134.5 10.4 %collective-permute-start.16 = (bf16[512,256]{1,0:T(8,128)(2,1)S(1)}, bf16[512,256]{1,0:T(8,128)(2,1)S(1)}, u32[]{:S(2)}, u32[]{:S(2)}) collective-permute-start(bf16[512,256]{1,0:T(8,128)(2,1)S(1)} %collective-permute-done.9), channel_id=1, source_target_pairs={{0,4},{4,8},{8,12},{12,16},{16,20},{20,24},{24,28},{28,0},{1,5},{5... | collective-permute-start | bytes 786440 | tf_op jit(solution)/shard_map/ppermute | solution.py:25
  145.0 2.8 %copy-start = (bf16[6144,512]{1,0:T(8,128)(2,1)S(1)}, bf16[6144,512]{1,0:T(8,128)(2,1)}, u32[]{:S(2)}) copy-start(bf16[6144,512]{1,0:T(8,128)(2,1)} %all-gather.2.cloned.1.call-done) | copy-start | bytes 18874372
  147.8 35.6 %copy-start.1 = (bf16[1,256,192]{1,2,0:T(8,128)(2,1)S(1)}, bf16[1,256,192]{1,2,0:T(8,128)(2,1)}, u32[]{:S(2)}) copy-start(bf16[1,256,192]{1,2,0:T(8,128)(2,1)} %param.8) | copy-start | bytes 294916
  147.8 35.6 %copy-start.4 = (f32[192]{0:T(256)S(1)}, f32[192]{0:T(256)}, u32[]{:S(2)}) copy-start(f32[192]{0:T(256)} %param.15) | copy-start | bytes 2308
Sparse Core Ops, SparseCore 0:
  42.4 85.3 all-gather.1

commit v7 on v6

--- a/solution.py
+++ b/solution.py
@@ -25,11 +25,12 @@
     return lax.ppermute(value, axis, [(i, (i + by) % count) for i in range(count)])
 
 
-def gather_y(block):
+def gather_y(block, zero=None):
     half = block.shape[0] // 2
     below2, above2 = shift(block, "y", NY, 2), shift(block, "y", NY, -2)
     below1, above1 = shift(block, "y", NY, 1), shift(block, "y", NY, -1)
-    below3, above3 = shift(below2, "y", NY, 1), shift(above2, "y", NY, -1)
+    late = above2 if zero is None else above2 + zero
+    below3, above3 = shift(below2, "y", NY, 1), shift(late, "y", NY, -1)
     far_top = shift(below2[:half], "y", NY, 2)
     far_bottom = shift(above2[half:], "y", NY, -2)
     return (below2, below1, block, above1, above2), (above3, far_top, far_bottom, below3)
@@ -63,29 +64,24 @@
 
 def multiply_out(weights, hidden, first):
     count, rows, depth = weights.shape
-    columns = hidden.shape[2]
+    steps, _, columns = hidden.shape
 
-    def kernel(first_ref, w_ref, h_ref, o_ref, total_ref):
-        step = pl.program_id(0)
+    def kernel(first_ref, w_ref, h_ref, o_ref):
         product = jnp.dot(w_ref[0], h_ref[0], preferred_element_type=jnp.float32)
 
-        @pl.when(step == 0)
+        @pl.when(pl.program_id(0) == 0)
         def _():
-            total_ref[...] = product
+            o_ref[...] = product
 
-        @pl.when((step > 0) & (step < count - 1))
+        @pl.when(pl.program_id(0) > 0)
         def _():
-            total_ref[...] += product
-
-        @pl.when(step == count - 1)
-        def _():
-            o_ref[...] = (total_ref[...] + product).astype(o_ref.dtype)
+            o_ref[...] += product
 
     return pl.pallas_call(
         kernel,
         grid_spec=pltpu.PrefetchScalarGridSpec(
             num_scalar_prefetch=1,
-            grid=(count,),
+            grid=(steps,),
             in_specs=[
                 pl.BlockSpec(
                     (1, rows, depth), lambda i, first_ref: ((first_ref[0] + i) & (count - 1), 0, 0)
@@ -93,13 +89,12 @@
                 pl.BlockSpec((1, depth, columns), lambda i, first_ref: (i, 0, 0)),
             ],
             out_specs=pl.BlockSpec((rows, columns), lambda i, first_ref: (0, 0)),
-            scratch_shapes=[pltpu.VMEM((rows, columns), jnp.float32)],
         ),
-        out_shape=jax.ShapeDtypeStruct((rows, columns), jnp.bfloat16),
+        out_shape=jax.ShapeDtypeStruct((rows, columns), jnp.float32),
         compiler_params=pltpu.CompilerParams(vmem_limit_bytes=16 * 1024 * 1024),
         cost_estimate=pl.CostEstimate(
-            flops=2 * count * rows * depth * columns,
-            bytes_accessed=2 * count * depth * (rows + columns),
+            flops=2 * steps * rows * depth * columns,
+            bytes_accessed=2 * steps * depth * (rows + columns) + 4 * rows * columns,
             transcendentals=0,
         ),
     )(first[None], weights, hidden)
@@ -128,11 +123,12 @@
     ).astype(jnp.bfloat16)
     mlp_hidden = jax.nn.gelu(project[3 * head :] + mlp_bias[:, None], approximate=False)
     hidden = jnp.concatenate([attended, mlp_hidden.astype(jnp.bfloat16)], axis=0)
-    near, (above3, far_top, far_bottom, below3) = gather_y(hidden)
+    near, (above3, far_top, far_bottom, below3) = gather_y(hidden, w_rows[0, 0, 0] * 0)
     far = jnp.concatenate([far_top, far_bottom], axis=0)
-    hidden_all = jnp.stack(near + (above3, far, below3))
-    part = multiply_out(w_rows, hidden_all, lax.axis_index("y") + NY - 2)
-    part = part.reshape(NZ, local_width, seq_len)
+    y = lax.axis_index("y")
+    part = multiply_out(w_rows, jnp.stack(near), y + NY - 2)
+    part = part + multiply_out(w_rows, jnp.stack((above3, far, below3)), y + 3)
+    part = part.astype(jnp.bfloat16).reshape(NZ, local_width, seq_len)
     pieces = lax.all_to_all(part, "zh", 0, 0)
     total = jnp.sum(pieces.astype(jnp.float32), axis=0)
     result = mine.astype(jnp.float32) + total + out_bias[:, None]

time: 192 us -> 188 us (0.979)
  waiting for transfers between devices: 18.8 us -> 13.5 us
    ppermute x16, waiting for transfers between devices: 18.7 us -> 13.5 us  [shift(): lax.ppermute(value, axis, [(i, (i + by) % count) for i in range(count)])]
  transfers between devices with their start and end apart: 18 -> 18, of which waited for: 3 -> 3; matrix products, arithmetic and copies ran while one was open for 5% -> 6% of each run, Pallas kernels for 0% -> 1%
where the time goes in v7:
time: 188 us
  starting transfers between devices  76.2 us (41%)
  blocking collectives  63.9 us (34%)
  between operations  15.4 us (8%)
  waiting for transfers between devices  13.5 us (7%)
  other arithmetic  5.75 us (3%)
  local copies, waits for them, and re-layouts  5.14 us (3%)
  matrix products  4.33 us (2%)
  Pallas kernels  3.52 us (2%)
    ppermute x16, starting transfers between devices, shift(): lax.ppermute(value, axis, [(i, (i + by) % count) for i in range(count)])  74.6 us
    all_gather x1, blocking collectives, per_device(): zgroup = lax.all_gather(mine, 'zh', axis=0, tiled=True)  32.3 us
    all_to_all x1, blocking collectives, per_device(): pieces = lax.all_to_all(part, 'zh', 0, 0)  31.6 us
    ppermute x16, waiting for transfers between devices, shift(): lax.ppermute(value, axis, [(i, (i + by) % count) for i in range(count)])  13.5 us
    dot_general x1, matrix products, per_device(): lax.dot_general(w_in, normed, (((0,), (0,)), ((), ())), preferred_element...  3.83 us
  transfers between devices with their start and end apart: 18, of which 3 were waited for; matrix products, arithmetic and copies ran while one was open for 6% of the time, Pallas kernels for 1%

profile of v7, /device:TPU:64, one launch (start us, length us, event | category | flops | bytes accessed | tf_op | source)
XLA Modules:
  0.0 187.7 jit_solution(12840225251927732918)
XLA Ops:
  6.5 1.6 collective-permute-start
  8.1 32.3 %all_gather.6 = bf16[768,256]{1,0:T(8,128)(2,1)S(1)} all-gather(bf16[192,256]{1,0:T(8,128)(2,1)} %bitcast.71), channel_id=1, replica_groups=mesh['x'=4,'zlh'=2,'zll'=2,'c'=2,'y'=8,'zh'=4] {'zh'}, dimensions={0}, use_global_device_ids=true | all-gather | bytes 491520 | tf_op jit(solution)/shard_map/all_gather | solution.py:107
  40.4 0.5 slice.41
  41.6 0.0 collective-permute-done
  41.6 0.7 broadcast_add_fusion.1
  42.2 0.0 all-gather.2.cloned.1.call-update
  42.3 7.2 %collective-permute-start.1 = (bf16[768,256]{1,0:T(8,128)(2,1)S(1)}, bf16[768,256]{1,0:T(8,128)(2,1)S(1)}, u32[]{:S(2)}, u32[]{:S(2)}) collective-permute-start(bf16[768,256]{1,0:T(8,128)(2,1)S(1)} %all_gather.6), channel_id=1, source_target_pairs={{0,8},{4,12},{8,16},{12,20},{16,24},{20,28},{24,0},{28,4},{1,9},{5... | collective-permute-start | bytes 1179656 | tf_op jit(solution)/shard_map/ppermute | solution.py:25
  49.4 2.8 %collective-permute-start.4 = (bf16[768,256]{1,0:T(8,128)(2,1)S(1)}, bf16[768,256]{1,0:T(8,128)(2,1)S(1)}, u32[]{:S(2)}, u32[]{:S(2)}) collective-permute-start(bf16[768,256]{1,0:T(8,128)(2,1)S(1)} %all_gather.6), channel_id=1, source_target_pairs={{0,24},{4,28},{8,0},{12,4},{16,8},{20,12},{24,16},{28,20},{1,25},{... | collective-permute-start | bytes 1179656 | tf_op jit(solution)/shard_map/ppermute | solution.py:25
  52.2 15.6 %collective-permute-start.2 = (bf16[768,256]{1,0:T(8,128)(2,1)S(1)}, bf16[768,256]{1,0:T(8,128)(2,1)S(1)}, u32[]{:S(2)}, u32[]{:S(2)}) collective-permute-start(bf16[768,256]{1,0:T(8,128)(2,1)S(1)} %all_gather.6), channel_id=1, source_target_pairs={{0,4},{4,8},{8,12},{12,16},{16,20},{20,24},{24,28},{28,0},{1,5},{5... | collective-permute-start | bytes 1179656 | tf_op jit(solution)/shard_map/ppermute | solution.py:25
  67.9 3.4 %collective-permute-start.3 = (bf16[768,256]{1,0:T(8,128)(2,1)S(1)}, bf16[768,256]{1,0:T(8,128)(2,1)S(1)}, u32[]{:S(2)}, u32[]{:S(2)}) collective-permute-start(bf16[768,256]{1,0:T(8,128)(2,1)S(1)} %all_gather.6), channel_id=1, source_target_pairs={{0,28},{4,0},{8,4},{12,8},{16,12},{20,16},{24,20},{28,24},{1,29},{... | collective-permute-start | bytes 1179656 | tf_op jit(solution)/shard_map/ppermute | solution.py:25
  71.3 0.0 collective-permute-done.1
  71.3 0.0 slice-start
  71.3 2.7 %collective-permute-start.7 = (bf16[384,256]{1,0:T(8,128)(2,1)S(1)}, bf16[384,256]{1,0:T(8,128)(2,1)S(1)}, u32[]{:S(2)}, u32[]{:S(2)}) collective-permute-start(bf16[384,256]{1,0:T(8,128)(2,1)S(1)} %slice.42), channel_id=1, source_target_pairs={{0,8},{4,12},{8,16},{12,20},{16,24},{20,28},{24,0},{28,4},{1,9},{5... | collective-permute-start | bytes 589832 | tf_op jit(solution)/shard_map/ppermute | solution.py:25
  74.0 0.0 collective-permute-done.4
  74.1 5.5 %collective-permute-start.8 = (bf16[384,256]{1,0:T(8,128)(2,1)S(1)}, bf16[384,256]{1,0:T(8,128)(2,1)S(1)}, u32[]{:S(2)}, u32[]{:S(2)}) collective-permute-start(bf16[384,256]{1,0:T(8,128)(2,1)S(1)} %slice.43), channel_id=1, source_target_pairs={{0,24},{4,28},{8,0},{12,4},{16,8},{20,12},{24,16},{28,20},{1,25},{... | collective-permute-start | bytes 589832 | tf_op jit(solution)/shard_map/ppermute | solution.py:25
  79.6 5.1 %collective-permute-start.5 = (bf16[768,256]{1,0:T(8,128)(2,1)S(1)}, bf16[768,256]{1,0:T(8,128)(2,1)S(1)}, u32[]{:S(2)}, u32[]{:S(2)}) collective-permute-start(bf16[768,256]{1,0:T(8,128)(2,1)S(1)} %collective-permute-done.4), channel_id=1, source_target_pairs={{0,28},{4,0},{8,4},{12,8},{16,12},{20,16},{24,20},{28,24},{1,29},{... | collective-permute-start | bytes 1179656 | tf_op jit(solution)/shard_map/ppermute | solution.py:25
  84.7 0.2 broadcast_in_dim.51
  85.0 0.0 collective-permute-done.2
  85.0 2.3 %collective-permute-start.6 = (bf16[768,256]{1,0:T(8,128)(2,1)S(1)}, bf16[768,256]{1,0:T(8,128)(2,1)S(1)}, u32[]{:S(2)}, u32[]{:S(2)}) collective-permute-start(bf16[768,256]{1,0:T(8,128)(2,1)S(1)} %collective-permute-done.1), channel_id=1, source_target_pairs={{0,4},{4,8},{8,12},{12,16},{16,20},{20,24},{24,28},{28,0},{1,5},{5... | collective-permute-start | bytes 1179656 | tf_op jit(solution)/shard_map/ppermute | solution.py:25
  87.4 0.0 collective-permute-done.3
  87.4 0.0 slice-start.1
  87.5 11.2 %collective-permute-done.5 = bf16[768,256]{1,0:T(8,128)(2,1)S(1)} collective-permute-done((bf16[768,256]{1,0:T(8,128)(2,1)S(1)}, bf16[768,256]{1,0:T(8,128)(2,1)S(1)}, u32[]{:S(2)}, u32[]{:S(2)}) %collective-permute-start.5) | collective-permute-done | bytes 393248 | tf_op jit(solution)/shard_map/ppermute | solution.py:25
  98.7 0.0 collective-permute-done.6
  98.8 0.0 collective-permute-done.7
  98.8 0.0 collective-permute-done.8
  98.9 0.0 copy-start.2
  98.9 0.8 convert_reduce_fusion
  99.7 0.9 multiply_reduce_fusion
  100.6 1.1 fusion.2
  101.8 0.0 copy-start.5
  101.8 0.0 copy-start.6
  101.8 0.0 copy-start.3
  101.8 3.8 %convolution_bitcast_fusion = f32[768,256]{1,0:T(8,128)S(1)} fusion(bf16[6144,256]{1,0:T(8,128)(2,1)S(1)} %fusion.2, bf16[6144,768]{1,0:T(8,128)(2,1)S(1)} %bitcast.77), kind=kOutput, calls=%fused_computation.6 | convolution fusion | flops 2415919104 | bytes 13369344 | tf_op jit(solution)/shard_map/dot_general | solution.py:112
  105.8 0.3 fusion.27
  106.1 0.1 fusion.13
  106.2 0.2 convolution_convert_fusion
  106.4 1.0 fusion.5
  107.4 4.0 %collective-permute-start.9 = (bf16[512,256]{1,0:T(8,128)(2,1)S(1)}, bf16[512,256]{1,0:T(8,128)(2,1)S(1)}, u32[]{:S(2)}, u32[]{:S(2)}) collective-permute-start(bf16[512,256]{1,0:T(8,128)(2,1)S(1)} %pad_maximum_fusion.1), channel_id=1, source_target_pairs={{0,8},{4,12},{8,16},{12,20},{16,24},{20,28},{24,0},{28,4},{1,9},{5... | collective-permute-start | bytes 786440 | tf_op jit(solution)/shard_map/ppermute | solution.py:25
  111.4 4.0 %collective-permute-start.12 = (bf16[512,256]{1,0:T(8,128)(2,1)S(1)}, bf16[512,256]{1,0:T(8,128)(2,1)S(1)}, u32[]{:S(2)}, u32[]{:S(2)}) collective-permute-start(bf16[512,256]{1,0:T(8,128)(2,1)S(1)} %pad_maximum_fusion.1), channel_id=1, source_target_pairs={{0,24},{4,28},{8,0},{12,4},{16,8},{20,12},{24,16},{28,20},{1,25},{... | collective-permute-start | bytes 786440 | tf_op jit(solution)/shard_map/ppermute | solution.py:25
  115.4 4.0 %collective-permute-start.10 = (bf16[512,256]{1,0:T(8,128)(2,1)S(1)}, bf16[512,256]{1,0:T(8,128)(2,1)S(1)}, u32[]{:S(2)}, u32[]{:S(2)}) collective-permute-start(bf16[512,256]{1,0:T(8,128)(2,1)S(1)} %pad_maximum_fusion.1), channel_id=1, source_target_pairs={{0,4},{4,8},{8,12},{12,16},{16,20},{20,24},{24,28},{28,0},{1,5},{5... | collective-permute-start | bytes 786440 | tf_op jit(solution)/shard_map/ppermute | solution.py:25
  119.3 3.1 %collective-permute-start.11 = (bf16[512,256]{1,0:T(8,128)(2,1)S(1)}, bf16[512,256]{1,0:T(8,128)(2,1)S(1)}, u32[]{:S(2)}, u32[]{:S(2)}) collective-permute-start(bf16[512,256]{1,0:T(8,128)(2,1)S(1)} %pad_maximum_fusion.1), channel_id=1, source_target_pairs={{0,28},{4,0},{8,4},{12,8},{16,12},{20,16},{24,20},{28,24},{1,29},{... | collective-permute-start | bytes 786440 | tf_op jit(solution)/shard_map/ppermute | solution.py:25
  122.4 0.0 collective-permute-done.9
  122.5 5.5 %collective-permute-start.14 = (bf16[256,256]{1,0:T(8,128)(2,1)S(1)}, bf16[256,256]{1,0:T(8,128)(2,1)S(1)}, u32[]{:S(2)}, u32[]{:S(2)}) collective-permute-start(bf16[256,256]{1,0:T(8,128)(2,1)S(1)} %slice.49), channel_id=1, source_target_pairs={{0,8},{4,12},{8,16},{12,20},{16,24},{20,28},{24,0},{28,4},{1,9},{5... | collective-permute-start | bytes 393224 | tf_op jit(solution)/shard_map/ppermute | solution.py:25
  128.0 0.0 collective-permute-done.12
  128.0 2.4 %collective-permute-start.15 = (bf16[256,256]{1,0:T(8,128)(2,1)S(1)}, bf16[256,256]{1,0:T(8,128)(2,1)S(1)}, u32[]{:S(2)}, u32[]{:S(2)}) collective-permute-start(bf16[256,256]{1,0:T(8,128)(2,1)S(1)} %slice.50), channel_id=1, source_target_pairs={{0,24},{4,28},{8,0},{12,4},{16,8},{20,12},{24,16},{28,20},{1,25},{... | collective-permute-start | bytes 393224 | tf_op jit(solution)/shard_map/ppermute | solution.py:25
  130.5 4.9 %collective-permute-start.16 = (bf16[512,256]{1,0:T(8,128)(2,1)S(1)}, bf16[512,256]{1,0:T(8,128)(2,1)S(1)}, u32[]{:S(2)}, u32[]{:S(2)}) collective-permute-start(bf16[512,256]{1,0:T(8,128)(2,1)S(1)} %collective-permute-done.9), channel_id=1, source_target_pairs={{0,4},{4,8},{8,12},{12,16},{16,20},{20,24},{24,28},{28,0},{1,5},{5... | collective-permute-start | bytes 786440 | tf_op jit(solution)/shard_map/ppermute | solution.py:25
  135.4 0.0 collective-permute-done.10
  135.4 0.0 collective-permute-done.11
  135.5 0.0 all-gather.2.cloned.1.call-done
  135.5 1.2 slice.48
  137.4 2.2 %collective-permute-start.13 = (bf16[512,256]{1,0:T(8,128)(2,1)S(1)}, bf16[512,256]{1,0:T(8,128)(2,1)S(1)}, u32[]{:S(2)}, u32[]{:S(2)}) collective-permute-start(bf16[512,256]{1,0:T(8,128)(2,1)S(1)} %broadcast_add_fusion), channel_id=1, source_target_pairs={{0,28},{4,0},{8,4},{12,8},{16,12},{20,16},{24,20},{28,24},{1,29},{... | collective-permute-start | bytes 786440 | tf_op jit(solution)/shard_map/ppermute | solution.py:25
  139.6 0.0 collective-permute-done.14
  139.6 0.2 collective-permute-done.15
  139.8 2.8 %copy-done = bf16[6144,512]{1,0:T(8,128)(2,1)S(1)} copy-done((bf16[6144,512]{1,0:T(8,128)(2,1)S(1)}, bf16[6144,512]{1,0:T(8,128)(2,1)}, u32[]{:S(2)}) %copy-start) | copy-done | bytes 6291480
  142.6 2.2 %shard_map.82 = f32[768,256]{1,0:T(8,128)S(1)} custom-call(s32[1]{0:T(128)} %bitcast.1.first_ref, bf16[8,768,512]{2,1,0:T(8,128)(2,1)S(1)} %bitcast.68, bf16[5,512,256]{2,1,0:T(8,128)(2,1)S(1)} %bitcast_dynamic-update-slice_fusion.7.h_ref), custom_call_target="tpu_custom_call" | custom-call | flops 1006632960 | bytes 6029312 | tf_op jit(solution)/shard_map/pallas_call | solution.py:80
  144.8 0.0 collective-permute-done.16
  144.8 2.0 %collective-permute-done.13 = bf16[512,256]{1,0:T(8,128)(2,1)S(1)} collective-permute-done((bf16[512,256]{1,0:T(8,128)(2,1)S(1)}, bf16[512,256]{1,0:T(8,128)(2,1)S(1)}, u32[]{:S(2)}, u32[]{:S(2)}) %collective-permute-start.13) | collective-permute-done | bytes 262176 | tf_op jit(solution)/shard_map/ppermute | solution.py:25
  146.8 0.1 pad_maximum_fusion.h_ref
  146.9 1.3 shard_map.83
  148.2 0.0 copy-start.1
  148.3 0.0 copy-start.4
  148.3 0.1 add_convert_fusion
  148.4 31.6 %all_to_all.5 = bf16[4,192,256]{2,1,0:T(8,128)(2,1)S(1)} all-to-all(bf16[4,192,256]{2,1,0:T(8,128)(2,1)S(1)} %bitcast.70), channel_id=1, replica_groups=mesh['x'=4,'zlh'=2,'zll'=2,'c'=2,'y'=8,'zh'=4] {'zh'}, dimensions={0} | all-to-all | bytes 786432 | tf_op jit(solution)/shard_map/all_to_all | solution.py:132
  180.1 0.7 fusion.20
  (42 shorter events, 0.7 us)
Async XLA Ops:
  6.5 129.0 %all-gather.2.cloned.1.call-start = ((), (), s32[]{:S(2)}) async-start(), calls=%async_computation.1 | async-start | bytes 6488064 | tf_op jit(solution)/shard_map/all_gather | solution.py:108
  6.5 35.0 %collective-permute-start = (bf16[192,512]{1,0:T(8,128)(2,1)}, bf16[192,512]{1,0:T(8,128)(2,1)S(1)}, u32[]{:S(2)}, u32[]{:S(2)}) collective-permute-start(bf16[192,512]{1,0:T(8,128)(2,1)} %bitcast.78), channel_id=1, source_target_pairs={{0,0},{4,128},{8,256},{12,384},{16,512},{20,640},{24,768},{28,896}... | collective-permute-start | bytes 589832 | tf_op jit(solution)/shard_map/ppermute | solution.py:62
  42.3 29.0 %collective-permute-start.1 = (bf16[768,256]{1,0:T(8,128)(2,1)S(1)}, bf16[768,256]{1,0:T(8,128)(2,1)S(1)}, u32[]{:S(2)}, u32[]{:S(2)}) collective-permute-start(bf16[768,256]{1,0:T(8,128)(2,1)S(1)} %all_gather.6), channel_id=1, source_target_pairs={{0,8},{4,12},{8,16},{12,20},{16,24},{20,28},{24,0},{28,4},{1,9},{5... | collective-permute-start | bytes 1179656 | tf_op jit(solution)/shard_map/ppermute | solution.py:25
  49.4 24.6 %collective-permute-start.4 = (bf16[768,256]{1,0:T(8,128)(2,1)S(1)}, bf16[768,256]{1,0:T(8,128)(2,1)S(1)}, u32[]{:S(2)}, u32[]{:S(2)}) collective-permute-start(bf16[768,256]{1,0:T(8,128)(2,1)S(1)} %all_gather.6), channel_id=1, source_target_pairs={{0,24},{4,28},{8,0},{12,4},{16,8},{20,12},{24,16},{28,20},{1,25},{... | collective-permute-start | bytes 1179656 | tf_op jit(solution)/shard_map/ppermute | solution.py:25
  52.2 32.8 %collective-permute-start.2 = (bf16[768,256]{1,0:T(8,128)(2,1)S(1)}, bf16[768,256]{1,0:T(8,128)(2,1)S(1)}, u32[]{:S(2)}, u32[]{:S(2)}) collective-permute-start(bf16[768,256]{1,0:T(8,128)(2,1)S(1)} %all_gather.6), channel_id=1, source_target_pairs={{0,4},{4,8},{8,12},{12,16},{16,20},{20,24},{24,28},{28,0},{1,5},{5... | collective-permute-start | bytes 1179656 | tf_op jit(solution)/shard_map/ppermute | solution.py:25
  67.9 19.5 %collective-permute-start.3 = (bf16[768,256]{1,0:T(8,128)(2,1)S(1)}, bf16[768,256]{1,0:T(8,128)(2,1)S(1)}, u32[]{:S(2)}, u32[]{:S(2)}) collective-permute-start(bf16[768,256]{1,0:T(8,128)(2,1)S(1)} %all_gather.6), channel_id=1, source_target_pairs={{0,28},{4,0},{8,4},{12,8},{16,12},{20,16},{24,20},{28,24},{1,29},{... | collective-permute-start | bytes 1179656 | tf_op jit(solution)/shard_map/ppermute | solution.py:25
  71.3 30.5 %slice-start = ((s8[9437184]{0:T(1024)(128)(4,1)}), s8[4194304]{0:T(1024)(128)(4,1)S(1)}, s32[]{:S(2)}) async-start(s8[9437184]{0:T(1024)(128)(4,1)} %bitcast.76), calls=%async_computation.2 | async-start | bytes 8388608
  71.3 27.5 %collective-permute-start.7 = (bf16[384,256]{1,0:T(8,128)(2,1)S(1)}, bf16[384,256]{1,0:T(8,128)(2,1)S(1)}, u32[]{:S(2)}, u32[]{:S(2)}) collective-permute-start(bf16[384,256]{1,0:T(8,128)(2,1)S(1)} %slice.42), channel_id=1, source_target_pairs={{0,8},{4,12},{8,16},{12,20},{16,24},{20,28},{24,0},{28,4},{1,9},{5... | collective-permute-start | bytes 589832 | tf_op jit(solution)/shard_map/ppermute | solution.py:25
  74.1 24.8 %collective-permute-start.8 = (bf16[384,256]{1,0:T(8,128)(2,1)S(1)}, bf16[384,256]{1,0:T(8,128)(2,1)S(1)}, u32[]{:S(2)}, u32[]{:S(2)}) collective-permute-start(bf16[384,256]{1,0:T(8,128)(2,1)S(1)} %slice.43), channel_id=1, source_target_pairs={{0,24},{4,28},{8,0},{12,4},{16,8},{20,12},{24,16},{28,20},{1,25},{... | collective-permute-start | bytes 589832 | tf_op jit(solution)/shard_map/ppermute | solution.py:25
  79.6 19.1 %collective-permute-start.5 = (bf16[768,256]{1,0:T(8,128)(2,1)S(1)}, bf16[768,256]{1,0:T(8,128)(2,1)S(1)}, u32[]{:S(2)}, u32[]{:S(2)}) collective-permute-start(bf16[768,256]{1,0:T(8,128)(2,1)S(1)} %collective-permute-done.4), channel_id=1, source_target_pairs={{0,28},{4,0},{8,4},{12,8},{16,12},{20,16},{24,20},{28,24},{1,29},{... | collective-permute-start | bytes 1179656 | tf_op jit(solution)/shard_map/ppermute | solution.py:25
  85.0 13.7 %collective-permute-start.6 = (bf16[768,256]{1,0:T(8,128)(2,1)S(1)}, bf16[768,256]{1,0:T(8,128)(2,1)S(1)}, u32[]{:S(2)}, u32[]{:S(2)}) collective-permute-start(bf16[768,256]{1,0:T(8,128)(2,1)S(1)} %collective-permute-done.1), channel_id=1, source_target_pairs={{0,4},{4,8},{8,12},{12,16},{16,20},{20,24},{24,28},{28,0},{1,5},{5... | collective-permute-start | bytes 1179656 | tf_op jit(solution)/shard_map/ppermute | solution.py:25
  87.4 14.3 %slice-start.1 = ((s8[9437184]{0:T(1024)(128)(4,1)}), s8[4194304]{0:T(1024)(128)(4,1)S(1)}, s32[]{:S(2)}) async-start(s8[9437184]{0:T(1024)(128)(4,1)} %bitcast.76), calls=%async_computation.3 | async-start | bytes 8388608
  98.9 1.7 copy-start.2
  99.7 2.1 %slice-start.2 = ((s8[9437184]{0:T(1024)(128)(4,1)}), s8[1048576]{0:T(1024)(128)(4,1)S(1)}, s32[]{:S(2)}) async-start(s8[9437184]{0:T(1024)(128)(4,1)} %bitcast.76), calls=%async_computation.4 | async-start | bytes 2097152
  101.8 4.0 %copy-start.5 = (f32[1,128]{1,0:T(1,128)S(1)}, f32[1,128]{1,0:T(1,128)}, u32[]{:S(2)}) copy-start(f32[1,128]{1,0:T(1,128)} %param.12) | copy-start | bytes 1540
  101.8 4.0 %copy-start.6 = (f32[1,128]{1,0:T(1,128)S(1)}, f32[1,128]{1,0:T(1,128)}, u32[]{:S(2)}) copy-start(f32[1,128]{1,0:T(1,128)} %param.11) | copy-start | bytes 1540
  101.8 4.6 %copy-start.3 = (f32[384]{0:T(512)S(1)}, f32[384]{0:T(512)}, u32[]{:S(2)}) copy-start(f32[384]{0:T(512)} %param.13) | copy-start | bytes 4612
  107.4 15.0 %collective-permute-start.9 = (bf16[512,256]{1,0:T(8,128)(2,1)S(1)}, bf16[512,256]{1,0:T(8,128)(2,1)S(1)}, u32[]{:S(2)}, u32[]{:S(2)}) collective-permute-start(bf16[512,256]{1,0:T(8,128)(2,1)S(1)} %pad_maximum_fusion.1), channel_id=1, source_target_pairs={{0,8},{4,12},{8,16},{12,20},{16,24},{20,28},{24,0},{28,4},{1,9},{5... | collective-permute-start | bytes 786440 | tf_op jit(solution)/shard_map/ppermute | solution.py:25
  111.4 16.6 %collective-permute-start.12 = (bf16[512,256]{1,0:T(8,128)(2,1)S(1)}, bf16[512,256]{1,0:T(8,128)(2,1)S(1)}, u32[]{:S(2)}, u32[]{:S(2)}) collective-permute-start(bf16[512,256]{1,0:T(8,128)(2,1)S(1)} %pad_maximum_fusion.1), channel_id=1, source_target_pairs={{0,24},{4,28},{8,0},{12,4},{16,8},{20,12},{24,16},{28,20},{1,25},{... | collective-permute-start | bytes 786440 | tf_op jit(solution)/shard_map/ppermute | solution.py:25
  115.4 20.0 %collective-permute-start.10 = (bf16[512,256]{1,0:T(8,128)(2,1)S(1)}, bf16[512,256]{1,0:T(8,128)(2,1)S(1)}, u32[]{:S(2)}, u32[]{:S(2)}) collective-permute-start(bf16[512,256]{1,0:T(8,128)(2,1)S(1)} %pad_maximum_fusion.1), channel_id=1, source_target_pairs={{0,4},{4,8},{8,12},{12,16},{16,20},{20,24},{24,28},{28,0},{1,5},{5... | collective-permute-start | bytes 786440 | tf_op jit(solution)/shard_map/ppermute | solution.py:25
  119.3 16.1 %collective-permute-start.11 = (bf16[512,256]{1,0:T(8,128)(2,1)S(1)}, bf16[512,256]{1,0:T(8,128)(2,1)S(1)}, u32[]{:S(2)}, u32[]{:S(2)}) collective-permute-start(bf16[512,256]{1,0:T(8,128)(2,1)S(1)} %pad_maximum_fusion.1), channel_id=1, source_target_pairs={{0,28},{4,0},{8,4},{12,8},{16,12},{20,16},{24,20},{28,24},{1,29},{... | collective-permute-start | bytes 786440 | tf_op jit(solution)/shard_map/ppermute | solution.py:25
  122.5 17.1 %collective-permute-start.14 = (bf16[256,256]{1,0:T(8,128)(2,1)S(1)}, bf16[256,256]{1,0:T(8,128)(2,1)S(1)}, u32[]{:S(2)}, u32[]{:S(2)}) collective-permute-start(bf16[256,256]{1,0:T(8,128)(2,1)S(1)} %slice.49), channel_id=1, source_target_pairs={{0,8},{4,12},{8,16},{12,20},{16,24},{20,28},{24,0},{28,4},{1,9},{5... | collective-permute-start | bytes 393224 | tf_op jit(solution)/shard_map/ppermute | solution.py:25
  128.0 11.8 %collective-permute-start.15 = (bf16[256,256]{1,0:T(8,128)(2,1)S(1)}, bf16[256,256]{1,0:T(8,128)(2,1)S(1)}, u32[]{:S(2)}, u32[]{:S(2)}) collective-permute-start(bf16[256,256]{1,0:T(8,128)(2,1)S(1)} %slice.50), channel_id=1, source_target_pairs={{0,24},{4,28},{8,0},{12,4},{16,8},{20,12},{24,16},{28,20},{1,25},{... | collective-permute-start | bytes 393224 | tf_op jit(solution)/shard_map/ppermute | solution.py:25
  130.5 14.3 %collective-permute-start.16 = (bf16[512,256]{1,0:T(8,128)(2,1)S(1)}, bf16[512,256]{1,0:T(8,128)(2,1)S(1)}, u32[]{:S(2)}, u32[]{:S(2)}) collective-permute-start(bf16[512,256]{1,0:T(8,128)(2,1)S(1)} %collective-permute-done.9), channel_id=1, source_target_pairs={{0,4},{4,8},{8,12},{12,16},{16,20},{20,24},{24,28},{28,0},{1,5},{5... | collective-permute-start | bytes 786440 | tf_op jit(solution)/shard_map/ppermute | solution.py:25
  137.4 9.5 %collective-permute-start.13 = (bf16[512,256]{1,0:T(8,128)(2,1)S(1)}, bf16[512,256]{1,0:T(8,128)(2,1)S(1)}, u32[]{:S(2)}, u32[]{:S(2)}) collective-permute-start(bf16[512,256]{1,0:T(8,128)(2,1)S(1)} %broadcast_add_fusion), channel_id=1, source_target_pairs={{0,28},{4,0},{8,4},{12,8},{16,12},{20,16},{24,20},{28,24},{1,29},{... | collective-permute-start | bytes 786440 | tf_op jit(solution)/shard_map/ppermute | solution.py:25
  139.8 2.8 %copy-start = (bf16[6144,512]{1,0:T(8,128)(2,1)S(1)}, bf16[6144,512]{1,0:T(8,128)(2,1)}, u32[]{:S(2)}) copy-start(bf16[6144,512]{1,0:T(8,128)(2,1)} %all-gather.2.cloned.1.call-done) | copy-start | bytes 18874372
  148.2 31.8 %copy-start.1 = (bf16[1,256,192]{1,2,0:T(8,128)(2,1)S(1)}, bf16[1,256,192]{1,2,0:T(8,128)(2,1)}, u32[]{:S(2)}) copy-start(bf16[1,256,192]{1,2,0:T(8,128)(2,1)} %param.8) | copy-start | bytes 294916
  148.3 31.8 %copy-start.4 = (f32[192]{0:T(256)S(1)}, f32[192]{0:T(256)}, u32[]{:S(2)}) copy-start(f32[192]{0:T(256)} %param.15) | copy-start | bytes 2308
Sparse Core Ops, SparseCore 0:
  42.4 85.3 all-gather.1

commit v8 on v7

--- a/solution.py
+++ b/solution.py
@@ -105,10 +105,16 @@
     mine = patches[0].T
     swapped = swap_out_weights(w_out)
     zgroup = lax.all_gather(mine, "zh", axis=0, tiled=True)
-    w_rows = lax.all_gather(swapped + zgroup[0, 0] * 0, DP, axis=0, tiled=True)
+    zeros = jnp.concatenate([zgroup[:local_width]] * (w_out.shape[0] // seq_len), axis=1) * 0
+    w_rows = lax.all_gather(swapped + zeros, DP, axis=0, tiled=True)
     w_rows = w_rows.reshape(NY, NZ * local_width, -1)
-    whole = gather_in_order(zgroup).reshape(-1, seq_len)
-    normed = (normalize(whole.astype(jnp.float32), 0) * norm_gain[:, None]).astype(jnp.bfloat16)
+    guess = jnp.mean(zgroup.astype(jnp.float32), axis=0, keepdims=True)
+    whole = gather_in_order(zgroup).reshape(-1, seq_len).astype(jnp.float32)
+    offset = whole - guess
+    first = jnp.mean(offset, axis=0, keepdims=True)
+    second = jnp.mean(offset * offset, axis=0, keepdims=True)
+    scale = lax.rsqrt(jnp.maximum(second - first * first, 0.0) + EPS)
+    normed = ((whole - (guess + first)) * scale * norm_gain[:, None]).astype(jnp.bfloat16)
     project = lax.dot_general(
         w_in, normed, (((0,), (0,)), ((), ())), preferred_element_type=jnp.float32
     )
@@ -123,7 +129,9 @@
     ).astype(jnp.bfloat16)
     mlp_hidden = jax.nn.gelu(project[3 * head :] + mlp_bias[:, None], approximate=False)
     hidden = jnp.concatenate([attended, mlp_hidden.astype(jnp.bfloat16)], axis=0)
-    near, (above3, far_top, far_bottom, below3) = gather_y(hidden, w_rows[0, 0, 0] * 0)
+    near, (above3, far_top, far_bottom, below3) = gather_y(
+        hidden, w_rows[0, : hidden.shape[0], :seq_len] * 0
+    )
     far = jnp.concatenate([far_top, far_bottom], axis=0)
     y = lax.axis_index("y")
     part = multiply_out(w_rows, jnp.stack(near), y + NY - 2)

time: 188 us -> 188 us (level)
  the two profiles are of different devices: /device:TPU:64 before, /device:TPU:73 now
where the time goes in v8:
time: 188 us; the launch traced here: 187 us
  blocking collectives  73.5 us (39%)
  starting transfers between devices  56.4 us (30%)
  waiting for transfers between devices  23.8 us (13%)
  between operations  14 us (7%)
  other arithmetic  6.28 us (3%)
  local copies, waits for them, and re-layouts  4.98 us (3%)
  matrix products  4.33 us (2%)
  Pallas kernels  3.53 us (2%)
    ppermute x16, starting transfers between devices, shift(): lax.ppermute(value, axis, [(i, (i + by) % count) for i in range(count)])  50.7 us
    all_gather x1, blocking collectives, per_device(): zgroup = lax.all_gather(mine, 'zh', axis=0, tiled=True)  40.2 us
    all_to_all x1, blocking collectives, per_device(): pieces = lax.all_to_all(part, 'zh', 0, 0)  33.3 us
    ppermute x16, waiting for transfers between devices, shift(): lax.ppermute(value, axis, [(i, (i + by) % count) for i in range(count)])  23.8 us
    ppermute x1, starting transfers between devices, swap_out_weights(): return lax.ppermute(w_out.T, ('x', 'zlh', 'zll', 'c', 'y'), pairs)  5.68 us
    unnamed x19, local copies, waits for them, and re-layouts  4.43 us
    dot_general x1, matrix products, per_device(): lax.dot_general(w_in, normed, (((0,), (0,)), ((), ())), preferred_element...  3.83 us
  transfers between devices with their start and end apart: 18, of which 6 were waited for; matrix products, arithmetic and copies ran while one was open for 5% of the time, Pallas kernels for 1%

profile of v8, /device:TPU:73, one launch (start us, length us, event | category | flops | bytes accessed | tf_op | source)
XLA Modules:
  0.0 186.8 jit_solution(8830999128812333005)
XLA Ops:
  6.5 0.0 all-gather.2.cloned.1.call-start
  6.5 5.7 %collective-permute-start = (bf16[192,512]{1,0:T(8,128)(2,1)}, bf16[192,512]{1,0:T(8,128)(2,1)S(1)}, u32[]{:S(2)}, u32[]{:S(2)}) collective-permute-start(bf16[192,512]{1,0:T(8,128)(2,1)} %bitcast.78), channel_id=1, source_target_pairs={{0,0},{4,128},{8,256},{12,384},{16,512},{20,640},{24,768},{28,896}... | collective-permute-start | bytes 589832 | tf_op jit(solution)/shard_map/ppermute | solution.py:62
  12.2 40.2 %all_gather.6 = bf16[768,256]{1,0:T(8,128)(2,1)S(1)} all-gather(bf16[192,256]{1,0:T(8,128)(2,1)} %bitcast.73), channel_id=1, replica_groups=mesh['x'=4,'zlh'=2,'zll'=2,'c'=2,'y'=8,'zh'=4] {'zh'}, dimensions={0}, use_global_device_ids=true | all-gather | bytes 491520 | tf_op jit(solution)/shard_map/all_gather | solution.py:107
  52.4 0.0 collective-permute-done
  52.4 0.7 fusion.16
  53.2 0.0 all-gather.2.cloned.1.call-update
  53.2 5.4 %collective-permute-start.1 = (bf16[768,256]{1,0:T(8,128)(2,1)S(1)}, bf16[768,256]{1,0:T(8,128)(2,1)S(1)}, u32[]{:S(2)}, u32[]{:S(2)}) collective-permute-start(bf16[768,256]{1,0:T(8,128)(2,1)S(1)} %all_gather.6), channel_id=1, source_target_pairs={{0,8},{4,12},{8,16},{12,20},{16,24},{20,28},{24,0},{28,4},{1,9},{5... | collective-permute-start | bytes 1179656 | tf_op jit(solution)/shard_map/ppermute | solution.py:25
  58.6 3.1 %collective-permute-start.4 = (bf16[768,256]{1,0:T(8,128)(2,1)S(1)}, bf16[768,256]{1,0:T(8,128)(2,1)S(1)}, u32[]{:S(2)}, u32[]{:S(2)}) collective-permute-start(bf16[768,256]{1,0:T(8,128)(2,1)S(1)} %all_gather.6), channel_id=1, source_target_pairs={{0,24},{4,28},{8,0},{12,4},{16,8},{20,12},{24,16},{28,20},{1,25},{... | collective-permute-start | bytes 1179656 | tf_op jit(solution)/shard_map/ppermute | solution.py:25
  61.7 1.9 %collective-permute-start.2 = (bf16[768,256]{1,0:T(8,128)(2,1)S(1)}, bf16[768,256]{1,0:T(8,128)(2,1)S(1)}, u32[]{:S(2)}, u32[]{:S(2)}) collective-permute-start(bf16[768,256]{1,0:T(8,128)(2,1)S(1)} %all_gather.6), channel_id=1, source_target_pairs={{0,4},{4,8},{8,12},{12,16},{16,20},{20,24},{24,28},{28,0},{1,5},{5... | collective-permute-start | bytes 1179656 | tf_op jit(solution)/shard_map/ppermute | solution.py:25
  63.6 3.4 %collective-permute-start.3 = (bf16[768,256]{1,0:T(8,128)(2,1)S(1)}, bf16[768,256]{1,0:T(8,128)(2,1)S(1)}, u32[]{:S(2)}, u32[]{:S(2)}) collective-permute-start(bf16[768,256]{1,0:T(8,128)(2,1)S(1)} %all_gather.6), channel_id=1, source_target_pairs={{0,28},{4,0},{8,4},{12,8},{16,12},{20,16},{24,20},{28,24},{1,29},{... | collective-permute-start | bytes 1179656 | tf_op jit(solution)/shard_map/ppermute | solution.py:25
  67.0 0.1 convert_reduce_fusion.1
  67.1 0.0 collective-permute-done.1
  67.1 3.7 %collective-permute-start.7 = (bf16[384,256]{1,0:T(8,128)(2,1)S(1)}, bf16[384,256]{1,0:T(8,128)(2,1)S(1)}, u32[]{:S(2)}, u32[]{:S(2)}) collective-permute-start(bf16[384,256]{1,0:T(8,128)(2,1)S(1)} %slice.42), channel_id=1, source_target_pairs={{0,8},{4,12},{8,16},{12,20},{16,24},{20,28},{24,0},{28,4},{1,9},{5... | collective-permute-start | bytes 589832 | tf_op jit(solution)/shard_map/ppermute | solution.py:25
  70.8 0.0 collective-permute-done.4
  70.9 3.7 %collective-permute-start.8 = (bf16[384,256]{1,0:T(8,128)(2,1)S(1)}, bf16[384,256]{1,0:T(8,128)(2,1)S(1)}, u32[]{:S(2)}, u32[]{:S(2)}) collective-permute-start(bf16[384,256]{1,0:T(8,128)(2,1)S(1)} %slice.43), channel_id=1, source_target_pairs={{0,24},{4,28},{8,0},{12,4},{16,8},{20,12},{24,16},{28,20},{1,25},{... | collective-permute-start | bytes 589832 | tf_op jit(solution)/shard_map/ppermute | solution.py:25
  74.6 3.1 %collective-permute-start.5 = (bf16[768,256]{1,0:T(8,128)(2,1)S(1)}, bf16[768,256]{1,0:T(8,128)(2,1)S(1)}, u32[]{:S(2)}, u32[]{:S(2)}) collective-permute-start(bf16[768,256]{1,0:T(8,128)(2,1)S(1)} %collective-permute-done.4), channel_id=1, source_target_pairs={{0,28},{4,0},{8,4},{12,8},{16,12},{20,16},{24,20},{28,24},{1,29},{... | collective-permute-start | bytes 1179656 | tf_op jit(solution)/shard_map/ppermute | solution.py:25
  77.7 0.2 broadcast_in_dim.52
  77.9 0.2 collective-permute-done.2
  78.2 2.0 %collective-permute-start.6 = (bf16[768,256]{1,0:T(8,128)(2,1)S(1)}, bf16[768,256]{1,0:T(8,128)(2,1)S(1)}, u32[]{:S(2)}, u32[]{:S(2)}) collective-permute-start(bf16[768,256]{1,0:T(8,128)(2,1)S(1)} %collective-permute-done.1), channel_id=1, source_target_pairs={{0,4},{4,8},{8,12},{12,16},{16,20},{20,24},{24,28},{28,0},{1,5},{5... | collective-permute-start | bytes 1179656 | tf_op jit(solution)/shard_map/ppermute | solution.py:25
  80.2 2.8 %collective-permute-done.3 = bf16[768,256]{1,0:T(8,128)(2,1)S(1)} collective-permute-done((bf16[768,256]{1,0:T(8,128)(2,1)S(1)}, bf16[768,256]{1,0:T(8,128)(2,1)S(1)}, u32[]{:S(2)}, u32[]{:S(2)}) %collective-permute-start.3) | collective-permute-done | bytes 393248 | tf_op jit(solution)/shard_map/ppermute | solution.py:25
  83.0 0.0 copy-start.2
  83.1 14.9 %collective-permute-done.5 = bf16[768,256]{1,0:T(8,128)(2,1)S(1)} collective-permute-done((bf16[768,256]{1,0:T(8,128)(2,1)S(1)}, bf16[768,256]{1,0:T(8,128)(2,1)S(1)}, u32[]{:S(2)}, u32[]{:S(2)}) %collective-permute-start.5) | collective-permute-done | bytes 393248 | tf_op jit(solution)/shard_map/ppermute | solution.py:25
  98.0 0.0 collective-permute-done.6
  98.0 0.0 collective-permute-done.7
  98.1 0.0 collective-permute-done.8
  98.1 0.0 copy-start.7
  98.1 1.1 subtract_reduce_fusion
  99.2 0.0 copy-done.2
  99.2 1.1 fusion.2
  100.4 1.6 copy-done.7
  101.9 3.8 %convolution_bitcast_fusion = f32[768,256]{1,0:T(8,128)S(1)} fusion(bf16[6144,256]{1,0:T(8,128)(2,1)S(1)} %fusion.2, bf16[6144,768]{1,0:T(8,128)(2,1)S(1)} %copy-done.7), kind=kOutput, calls=%fused_computation.6 | convolution fusion | flops 2415919104 | bytes 13369344 | tf_op jit(solution)/shard_map/dot_general | solution.py:118
  105.9 0.0 copy-done.5
  105.9 0.0 copy-done.6
  105.9 0.3 fusion.30
  106.2 0.1 fusion.15
  106.3 0.2 convolution_convert_fusion
  106.5 1.0 fusion.5
  107.5 5.2 %collective-permute-start.9 = (bf16[512,256]{1,0:T(8,128)(2,1)S(1)}, bf16[512,256]{1,0:T(8,128)(2,1)S(1)}, u32[]{:S(2)}, u32[]{:S(2)}) collective-permute-start(bf16[512,256]{1,0:T(8,128)(2,1)S(1)} %pad_maximum_fusion.1), channel_id=1, source_target_pairs={{0,8},{4,12},{8,16},{12,20},{16,24},{20,28},{24,0},{28,4},{1,9},{5... | collective-permute-start | bytes 786440 | tf_op jit(solution)/shard_map/ppermute | solution.py:25
  112.7 2.2 %collective-permute-start.12 = (bf16[512,256]{1,0:T(8,128)(2,1)S(1)}, bf16[512,256]{1,0:T(8,128)(2,1)S(1)}, u32[]{:S(2)}, u32[]{:S(2)}) collective-permute-start(bf16[512,256]{1,0:T(8,128)(2,1)S(1)} %pad_maximum_fusion.1), channel_id=1, source_target_pairs={{0,24},{4,28},{8,0},{12,4},{16,8},{20,12},{24,16},{28,20},{1,25},{... | collective-permute-start | bytes 786440 | tf_op jit(solution)/shard_map/ppermute | solution.py:25
  114.9 1.9 %collective-permute-start.10 = (bf16[512,256]{1,0:T(8,128)(2,1)S(1)}, bf16[512,256]{1,0:T(8,128)(2,1)S(1)}, u32[]{:S(2)}, u32[]{:S(2)}) collective-permute-start(bf16[512,256]{1,0:T(8,128)(2,1)S(1)} %pad_maximum_fusion.1), channel_id=1, source_target_pairs={{0,4},{4,8},{8,12},{12,16},{16,20},{20,24},{24,28},{28,0},{1,5},{5... | collective-permute-start | bytes 786440 | tf_op jit(solution)/shard_map/ppermute | solution.py:25
  116.8 3.4 %collective-permute-start.11 = (bf16[512,256]{1,0:T(8,128)(2,1)S(1)}, bf16[512,256]{1,0:T(8,128)(2,1)S(1)}, u32[]{:S(2)}, u32[]{:S(2)}) collective-permute-start(bf16[512,256]{1,0:T(8,128)(2,1)S(1)} %pad_maximum_fusion.1), channel_id=1, source_target_pairs={{0,28},{4,0},{8,4},{12,8},{16,12},{20,16},{24,20},{28,24},{1,29},{... | collective-permute-start | bytes 786440 | tf_op jit(solution)/shard_map/ppermute | solution.py:25
  120.2 2.9 %collective-permute-done.9 = bf16[512,256]{1,0:T(8,128)(2,1)S(1)} collective-permute-done((bf16[512,256]{1,0:T(8,128)(2,1)S(1)}, bf16[512,256]{1,0:T(8,128)(2,1)S(1)}, u32[]{:S(2)}, u32[]{:S(2)}) %collective-permute-start.9) | collective-permute-done | bytes 262176 | tf_op jit(solution)/shard_map/ppermute | solution.py:25
  123.1 3.0 %collective-permute-start.14 = (bf16[256,256]{1,0:T(8,128)(2,1)S(1)}, bf16[256,256]{1,0:T(8,128)(2,1)S(1)}, u32[]{:S(2)}, u32[]{:S(2)}) collective-permute-start(bf16[256,256]{1,0:T(8,128)(2,1)S(1)} %slice.49), channel_id=1, source_target_pairs={{0,8},{4,12},{8,16},{12,20},{16,24},{20,28},{24,0},{28,4},{1,9},{5... | collective-permute-start | bytes 393224 | tf_op jit(solution)/shard_map/ppermute | solution.py:25
  126.2 1.7 collective-permute-done.12
  127.9 3.5 %collective-permute-start.15 = (bf16[256,256]{1,0:T(8,128)(2,1)S(1)}, bf16[256,256]{1,0:T(8,128)(2,1)S(1)}, u32[]{:S(2)}, u32[]{:S(2)}) collective-permute-start(bf16[256,256]{1,0:T(8,128)(2,1)S(1)} %slice.50), channel_id=1, source_target_pairs={{0,24},{4,28},{8,0},{12,4},{16,8},{20,12},{24,16},{28,20},{1,25},{... | collective-permute-start | bytes 393224 | tf_op jit(solution)/shard_map/ppermute | solution.py:25
  131.4 1.9 %collective-permute-start.16 = (bf16[512,256]{1,0:T(8,128)(2,1)S(1)}, bf16[512,256]{1,0:T(8,128)(2,1)S(1)}, u32[]{:S(2)}, u32[]{:S(2)}) collective-permute-start(bf16[512,256]{1,0:T(8,128)(2,1)S(1)} %collective-permute-done.9), channel_id=1, source_target_pairs={{0,4},{4,8},{8,12},{12,16},{16,20},{20,24},{24,28},{28,0},{1,5},{5... | collective-permute-start | bytes 786440 | tf_op jit(solution)/shard_map/ppermute | solution.py:25
  133.4 0.0 collective-permute-done.10
  133.5 0.0 collective-permute-done.11
  133.5 0.0 all-gather.2.cloned.1.call-done
  133.5 1.0 fusion.14
  134.5 3.4 %collective-permute-start.13 = (bf16[512,256]{1,0:T(8,128)(2,1)S(1)}, bf16[512,256]{1,0:T(8,128)(2,1)S(1)}, u32[]{:S(2)}, u32[]{:S(2)}) collective-permute-start(bf16[512,256]{1,0:T(8,128)(2,1)S(1)} %fusion.14), channel_id=1, source_target_pairs={{0,28},{4,0},{8,4},{12,8},{16,12},{20,16},{24,20},{28,24},{1,29},{... | collective-permute-start | bytes 786440 | tf_op jit(solution)/shard_map/ppermute | solution.py:25
  137.9 0.0 collective-permute-done.14
  137.9 1.2 collective-permute-done.15
  139.2 2.8 %copy-done = bf16[6144,512]{1,0:T(8,128)(2,1)S(1)} copy-done((bf16[6144,512]{1,0:T(8,128)(2,1)S(1)}, bf16[6144,512]{1,0:T(8,128)(2,1)}, u32[]{:S(2)}) %copy-start) | copy-done | bytes 6291480
  142.0 2.2 %shard_map.82 = f32[768,256]{1,0:T(8,128)S(1)} custom-call(s32[1]{0:T(128)} %bitcast.1.first_ref, bf16[8,768,512]{2,1,0:T(8,128)(2,1)S(1)} %bitcast.70, bf16[5,512,256]{2,1,0:T(8,128)(2,1)S(1)} %bitcast_dynamic-update-slice_fusion.7.h_ref), custom_call_target="tpu_custom_call" | custom-call | flops 1006632960 | bytes 6029312 | tf_op jit(solution)/shard_map/pallas_call | solution.py:80
  144.2 0.0 collective-permute-done.16
  144.2 0.0 collective-permute-done.13
  144.2 0.1 pad_maximum_fusion.h_ref
  144.3 1.3 shard_map.83
  145.6 0.0 copy-start.1
  145.6 0.0 copy-start.4
  145.6 0.1 add_convert_fusion
  145.8 33.3 %all_to_all.5 = bf16[4,192,256]{2,1,0:T(8,128)(2,1)S(1)} all-to-all(bf16[4,192,256]{2,1,0:T(8,128)(2,1)S(1)} %bitcast.72), channel_id=1, replica_groups=mesh['x'=4,'zlh'=2,'zll'=2,'c'=2,'y'=8,'zh'=4] {'zh'}, dimensions={0} | all-to-all | bytes 786432 | tf_op jit(solution)/shard_map/all_to_all | solution.py:140
  179.2 0.7 fusion.23
  (36 shorter events, 0.6 us)
Async XLA Ops:
  6.5 127.0 %all-gather.2.cloned.1.call-start = ((), (), s32[]{:S(2)}) async-start(), calls=%async_computation.1 | async-start | bytes 6488064 | tf_op jit(solution)/shard_map/all_gather | solution.py:109
  6.5 45.9 %collective-permute-start = (bf16[192,512]{1,0:T(8,128)(2,1)}, bf16[192,512]{1,0:T(8,128)(2,1)S(1)}, u32[]{:S(2)}, u32[]{:S(2)}) collective-permute-start(bf16[192,512]{1,0:T(8,128)(2,1)} %bitcast.78), channel_id=1, source_target_pairs={{0,0},{4,128},{8,256},{12,384},{16,512},{20,640},{24,768},{28,896}... | collective-permute-start | bytes 589832 | tf_op jit(solution)/shard_map/ppermute | solution.py:62
  53.2 13.9 %collective-permute-start.1 = (bf16[768,256]{1,0:T(8,128)(2,1)S(1)}, bf16[768,256]{1,0:T(8,128)(2,1)S(1)}, u32[]{:S(2)}, u32[]{:S(2)}) collective-permute-start(bf16[768,256]{1,0:T(8,128)(2,1)S(1)} %all_gather.6), channel_id=1, source_target_pairs={{0,8},{4,12},{8,16},{12,20},{16,24},{20,28},{24,0},{28,4},{1,9},{5... | collective-permute-start | bytes 1179656 | tf_op jit(solution)/shard_map/ppermute | solution.py:25
  58.6 12.2 %collective-permute-start.4 = (bf16[768,256]{1,0:T(8,128)(2,1)S(1)}, bf16[768,256]{1,0:T(8,128)(2,1)S(1)}, u32[]{:S(2)}, u32[]{:S(2)}) collective-permute-start(bf16[768,256]{1,0:T(8,128)(2,1)S(1)} %all_gather.6), channel_id=1, source_target_pairs={{0,24},{4,28},{8,0},{12,4},{16,8},{20,12},{24,16},{28,20},{1,25},{... | collective-permute-start | bytes 1179656 | tf_op jit(solution)/shard_map/ppermute | solution.py:25
  61.7 16.5 %collective-permute-start.2 = (bf16[768,256]{1,0:T(8,128)(2,1)S(1)}, bf16[768,256]{1,0:T(8,128)(2,1)S(1)}, u32[]{:S(2)}, u32[]{:S(2)}) collective-permute-start(bf16[768,256]{1,0:T(8,128)(2,1)S(1)} %all_gather.6), channel_id=1, source_target_pairs={{0,4},{4,8},{8,12},{12,16},{16,20},{20,24},{24,28},{28,0},{1,5},{5... | collective-permute-start | bytes 1179656 | tf_op jit(solution)/shard_map/ppermute | solution.py:25
  63.6 19.4 %collective-permute-start.3 = (bf16[768,256]{1,0:T(8,128)(2,1)S(1)}, bf16[768,256]{1,0:T(8,128)(2,1)S(1)}, u32[]{:S(2)}, u32[]{:S(2)}) collective-permute-start(bf16[768,256]{1,0:T(8,128)(2,1)S(1)} %all_gather.6), channel_id=1, source_target_pairs={{0,28},{4,0},{8,4},{12,8},{16,12},{20,16},{24,20},{28,24},{1,29},{... | collective-permute-start | bytes 1179656 | tf_op jit(solution)/shard_map/ppermute | solution.py:25
  67.1 30.9 %collective-permute-start.7 = (bf16[384,256]{1,0:T(8,128)(2,1)S(1)}, bf16[384,256]{1,0:T(8,128)(2,1)S(1)}, u32[]{:S(2)}, u32[]{:S(2)}) collective-permute-start(bf16[384,256]{1,0:T(8,128)(2,1)S(1)} %slice.42), channel_id=1, source_target_pairs={{0,8},{4,12},{8,16},{12,20},{16,24},{20,28},{24,0},{28,4},{1,9},{5... | collective-permute-start | bytes 589832 | tf_op jit(solution)/shard_map/ppermute | solution.py:25
  70.9 27.2 %collective-permute-start.8 = (bf16[384,256]{1,0:T(8,128)(2,1)S(1)}, bf16[384,256]{1,0:T(8,128)(2,1)S(1)}, u32[]{:S(2)}, u32[]{:S(2)}) collective-permute-start(bf16[384,256]{1,0:T(8,128)(2,1)S(1)} %slice.43), channel_id=1, source_target_pairs={{0,24},{4,28},{8,0},{12,4},{16,8},{20,12},{24,16},{28,20},{1,25},{... | collective-permute-start | bytes 589832 | tf_op jit(solution)/shard_map/ppermute | solution.py:25
  74.6 23.4 %collective-permute-start.5 = (bf16[768,256]{1,0:T(8,128)(2,1)S(1)}, bf16[768,256]{1,0:T(8,128)(2,1)S(1)}, u32[]{:S(2)}, u32[]{:S(2)}) collective-permute-start(bf16[768,256]{1,0:T(8,128)(2,1)S(1)} %collective-permute-done.4), channel_id=1, source_target_pairs={{0,28},{4,0},{8,4},{12,8},{16,12},{20,16},{24,20},{28,24},{1,29},{... | collective-permute-start | bytes 1179656 | tf_op jit(solution)/shard_map/ppermute | solution.py:25
  78.2 19.8 %collective-permute-start.6 = (bf16[768,256]{1,0:T(8,128)(2,1)S(1)}, bf16[768,256]{1,0:T(8,128)(2,1)S(1)}, u32[]{:S(2)}, u32[]{:S(2)}) collective-permute-start(bf16[768,256]{1,0:T(8,128)(2,1)S(1)} %collective-permute-done.1), channel_id=1, source_target_pairs={{0,4},{4,8},{8,12},{12,16},{16,20},{20,24},{24,28},{28,0},{1,5},{5... | collective-permute-start | bytes 1179656 | tf_op jit(solution)/shard_map/ppermute | solution.py:25
  83.0 16.2 %copy-start.2 = (f32[6144]{0:T(1024)S(1)}, f32[6144]{0:T(1024)}, u32[]{:S(2)}) copy-start(f32[6144]{0:T(1024)} %param.9) | copy-start | bytes 73732
  98.1 3.8 %copy-start.7 = (bf16[6144,768]{1,0:T(8,128)(2,1)S(1)}, bf16[6144,768]{1,0:T(8,128)(2,1)}, u32[]{:S(2)}) copy-start(bf16[6144,768]{1,0:T(8,128)(2,1)} %param.10) | copy-start | bytes 28311556
  101.9 4.0 %copy-start.5 = (f32[1,128]{1,0:T(1,128)S(1)}, f32[1,128]{1,0:T(1,128)}, u32[]{:S(2)}) copy-start(f32[1,128]{1,0:T(1,128)} %param.12) | copy-start | bytes 1540
  101.9 4.0 %copy-start.6 = (f32[1,128]{1,0:T(1,128)S(1)}, f32[1,128]{1,0:T(1,128)}, u32[]{:S(2)}) copy-start(f32[1,128]{1,0:T(1,128)} %param.11) | copy-start | bytes 1540
  101.9 4.6 %copy-start.3 = (f32[384]{0:T(512)S(1)}, f32[384]{0:T(512)}, u32[]{:S(2)}) copy-start(f32[384]{0:T(512)} %param.13) | copy-start | bytes 4612
  107.5 15.6 %collective-permute-start.9 = (bf16[512,256]{1,0:T(8,128)(2,1)S(1)}, bf16[512,256]{1,0:T(8,128)(2,1)S(1)}, u32[]{:S(2)}, u32[]{:S(2)}) collective-permute-start(bf16[512,256]{1,0:T(8,128)(2,1)S(1)} %pad_maximum_fusion.1), channel_id=1, source_target_pairs={{0,8},{4,12},{8,16},{12,20},{16,24},{20,28},{24,0},{28,4},{1,9},{5... | collective-permute-start | bytes 786440 | tf_op jit(solution)/shard_map/ppermute | solution.py:25
  112.7 15.2 %collective-permute-start.12 = (bf16[512,256]{1,0:T(8,128)(2,1)S(1)}, bf16[512,256]{1,0:T(8,128)(2,1)S(1)}, u32[]{:S(2)}, u32[]{:S(2)}) collective-permute-start(bf16[512,256]{1,0:T(8,128)(2,1)S(1)} %pad_maximum_fusion.1), channel_id=1, source_target_pairs={{0,24},{4,28},{8,0},{12,4},{16,8},{20,12},{24,16},{28,20},{1,25},{... | collective-permute-start | bytes 786440 | tf_op jit(solution)/shard_map/ppermute | solution.py:25
  114.9 18.5 %collective-permute-start.10 = (bf16[512,256]{1,0:T(8,128)(2,1)S(1)}, bf16[512,256]{1,0:T(8,128)(2,1)S(1)}, u32[]{:S(2)}, u32[]{:S(2)}) collective-permute-start(bf16[512,256]{1,0:T(8,128)(2,1)S(1)} %pad_maximum_fusion.1), channel_id=1, source_target_pairs={{0,4},{4,8},{8,12},{12,16},{16,20},{20,24},{24,28},{28,0},{1,5},{5... | collective-permute-start | bytes 786440 | tf_op jit(solution)/shard_map/ppermute | solution.py:25
  116.8 16.6 %collective-permute-start.11 = (bf16[512,256]{1,0:T(8,128)(2,1)S(1)}, bf16[512,256]{1,0:T(8,128)(2,1)S(1)}, u32[]{:S(2)}, u32[]{:S(2)}) collective-permute-start(bf16[512,256]{1,0:T(8,128)(2,1)S(1)} %pad_maximum_fusion.1), channel_id=1, source_target_pairs={{0,28},{4,0},{8,4},{12,8},{16,12},{20,16},{24,20},{28,24},{1,29},{... | collective-permute-start | bytes 786440 | tf_op jit(solution)/shard_map/ppermute | solution.py:25
  123.1 14.8 %collective-permute-start.14 = (bf16[256,256]{1,0:T(8,128)(2,1)S(1)}, bf16[256,256]{1,0:T(8,128)(2,1)S(1)}, u32[]{:S(2)}, u32[]{:S(2)}) collective-permute-start(bf16[256,256]{1,0:T(8,128)(2,1)S(1)} %slice.49), channel_id=1, source_target_pairs={{0,8},{4,12},{8,16},{12,20},{16,24},{20,28},{24,0},{28,4},{1,9},{5... | collective-permute-start | bytes 393224 | tf_op jit(solution)/shard_map/ppermute | solution.py:25
  127.9 11.2 %collective-permute-start.15 = (bf16[256,256]{1,0:T(8,128)(2,1)S(1)}, bf16[256,256]{1,0:T(8,128)(2,1)S(1)}, u32[]{:S(2)}, u32[]{:S(2)}) collective-permute-start(bf16[256,256]{1,0:T(8,128)(2,1)S(1)} %slice.50), channel_id=1, source_target_pairs={{0,24},{4,28},{8,0},{12,4},{16,8},{20,12},{24,16},{28,20},{1,25},{... | collective-permute-start | bytes 393224 | tf_op jit(solution)/shard_map/ppermute | solution.py:25
  131.4 12.7 %collective-permute-start.16 = (bf16[512,256]{1,0:T(8,128)(2,1)S(1)}, bf16[512,256]{1,0:T(8,128)(2,1)S(1)}, u32[]{:S(2)}, u32[]{:S(2)}) collective-permute-start(bf16[512,256]{1,0:T(8,128)(2,1)S(1)} %collective-permute-done.9), channel_id=1, source_target_pairs={{0,4},{4,8},{8,12},{12,16},{16,20},{20,24},{24,28},{28,0},{1,5},{5... | collective-permute-start | bytes 786440 | tf_op jit(solution)/shard_map/ppermute | solution.py:25
  134.5 9.7 %collective-permute-start.13 = (bf16[512,256]{1,0:T(8,128)(2,1)S(1)}, bf16[512,256]{1,0:T(8,128)(2,1)S(1)}, u32[]{:S(2)}, u32[]{:S(2)}) collective-permute-start(bf16[512,256]{1,0:T(8,128)(2,1)S(1)} %fusion.14), channel_id=1, source_target_pairs={{0,28},{4,0},{8,4},{12,8},{16,12},{20,16},{24,20},{28,24},{1,29},{... | collective-permute-start | bytes 786440 | tf_op jit(solution)/shard_map/ppermute | solution.py:25
  139.2 2.8 %copy-start = (bf16[6144,512]{1,0:T(8,128)(2,1)S(1)}, bf16[6144,512]{1,0:T(8,128)(2,1)}, u32[]{:S(2)}) copy-start(bf16[6144,512]{1,0:T(8,128)(2,1)} %all-gather.2.cloned.1.call-done) | copy-start | bytes 18874372
  145.6 33.5 %copy-start.1 = (bf16[1,256,192]{1,2,0:T(8,128)(2,1)S(1)}, bf16[1,256,192]{1,2,0:T(8,128)(2,1)}, u32[]{:S(2)}) copy-start(bf16[1,256,192]{1,2,0:T(8,128)(2,1)} %param.8) | copy-start | bytes 294916
  145.6 33.5 %copy-start.4 = (f32[192]{0:T(256)S(1)}, f32[192]{0:T(256)}, u32[]{:S(2)}) copy-start(f32[192]{0:T(256)} %param.15) | copy-start | bytes 2308
Sparse Core Ops, SparseCore 0:
  53.3 73.2 all-gather.1

commit v9 on v7

--- a/solution.py
+++ b/solution.py
@@ -39,17 +39,19 @@
 def gather_in_order(block):
     y = lax.axis_index("y")
     half = block.shape[0] // 2
-    near, (above3, far_top, far_bottom, below3) = gather_y(block)
     whole = jnp.zeros((NY,) + block.shape, block.dtype)
     put = lambda whole, part, index, row: lax.dynamic_update_slice(
         whole, part[None], (index & (NY - 1), row, 0)
     )
-    for i, part in enumerate(near):
-        whole = put(whole, part, y + NY - 2 + i, 0)
-    whole = put(whole, above3, y + 3, 0)
-    whole = put(whole, below3, y + 5, 0)
-    whole = put(whole, far_top, y + 4, 0)
-    return put(whole, far_bottom, y + 4, half)
+    whole = put(whole, block, y, 0)
+    up = down = block
+    for step in range(1, 4):
+        up, down = shift(up, "y", NY, 1), shift(down, "y", NY, -1)
+        whole = put(whole, up, y - step + NY, 0)
+        whole = put(whole, down, y + step, 0)
+    up, down = shift(up[:half], "y", NY, 1), shift(down[half:], "y", NY, -1)
+    whole = put(whole, up, y + 4, 0)
+    return put(whole, down, y + 4, half)
 
 
 def swap_out_weights(w_out):
@@ -105,7 +107,8 @@
     mine = patches[0].T
     swapped = swap_out_weights(w_out)
     zgroup = lax.all_gather(mine, "zh", axis=0, tiled=True)
-    w_rows = lax.all_gather(swapped + zgroup[0, 0] * 0, DP, axis=0, tiled=True)
+    zeros = jnp.concatenate([zgroup[:local_width]] * (w_out.shape[0] // seq_len), axis=1) * 0
+    w_rows = lax.all_gather(swapped + zeros, DP, axis=0, tiled=True)
     w_rows = w_rows.reshape(NY, NZ * local_width, -1)
     whole = gather_in_order(zgroup).reshape(-1, seq_len)
     normed = (normalize(whole.astype(jnp.float32), 0) * norm_gain[:, None]).astype(jnp.bfloat16)
@@ -123,7 +126,9 @@
     ).astype(jnp.bfloat16)
     mlp_hidden = jax.nn.gelu(project[3 * head :] + mlp_bias[:, None], approximate=False)
     hidden = jnp.concatenate([attended, mlp_hidden.astype(jnp.bfloat16)], axis=0)
-    near, (above3, far_top, far_bottom, below3) = gather_y(hidden, w_rows[0, 0, 0] * 0)
+    near, (above3, far_top, far_bottom, below3) = gather_y(
+        hidden, w_rows[0, : hidden.shape[0], :seq_len] * 0
+    )
     far = jnp.concatenate([far_top, far_bottom], axis=0)
     y = lax.axis_index("y")
     part = multiply_out(w_rows, jnp.stack(near), y + NY - 2)

time: 188 us -> 186 us (0.989)
  the two profiles are of different devices: /device:TPU:64 before, /device:TPU:120 now
where the time goes in v9:
time: 186 us; the launch traced here: 185 us
  blocking collectives  68.5 us (37%)
  starting transfers between devices  59.5 us (32%)
  waiting for transfers between devices  24.9 us (13%)
  between operations  14 us (8%)
  other arithmetic  6.75 us (4%)
  matrix products  4.33 us (2%)
  Pallas kernels  3.56 us (2%)
  local copies, waits for them, and re-layouts  3.44 us (2%)
    ppermute x16, starting transfers between devices, shift(): lax.ppermute(value, axis, [(i, (i + by) % count) for i in range(count)])  52 us
    all_gather x1, blocking collectives, per_device(): zgroup = lax.all_gather(mine, 'zh', axis=0, tiled=True)  41.3 us
    all_to_all x1, blocking collectives, per_device(): pieces = lax.all_to_all(part, 'zh', 0, 0)  27.2 us
    ppermute x16, waiting for transfers between devices, shift(): lax.ppermute(value, axis, [(i, (i + by) % count) for i in range(count)])  24.8 us
    ppermute x1, starting transfers between devices, swap_out_weights(): return lax.ppermute(w_out.T, ('x', 'zlh', 'zll', 'c', 'y'), pairs)  7.48 us
    dot_general x1, matrix products, per_device(): lax.dot_general(w_in, normed, (((0,), (0,)), ((), ())), preferred_element...  3.83 us
  transfers between devices with their start and end apart: 18, of which 8 were waited for; matrix products, arithmetic and copies ran while one was open for 5% of the time, Pallas kernels for 1%

profile of v9, /device:TPU:120, one launch (start us, length us, event | category | flops | bytes accessed | tf_op | source)
XLA Modules:
  0.0 184.9 jit_solution(15190376358169752682)
XLA Ops:
  6.5 7.5 %collective-permute-start = (bf16[192,512]{1,0:T(8,128)(2,1)}, bf16[192,512]{1,0:T(8,128)(2,1)S(1)}, u32[]{:S(2)}, u32[]{:S(2)}) collective-permute-start(bf16[192,512]{1,0:T(8,128)(2,1)} %bitcast.80), channel_id=1, source_target_pairs={{0,0},{4,128},{8,256},{12,384},{16,512},{20,640},{24,768},{28,896}... | collective-permute-start | bytes 589832 | tf_op jit(solution)/shard_map/ppermute | solution.py:64
  14.0 41.3 %all_gather.6 = bf16[768,256]{1,0:T(8,128)(2,1)S(1)} all-gather(bf16[192,256]{1,0:T(8,128)(2,1)} %bitcast.73), channel_id=1, replica_groups=mesh['x'=4,'zlh'=2,'zll'=2,'c'=2,'y'=8,'zh'=4] {'zh'}, dimensions={0}, use_global_device_ids=true | all-gather | bytes 491520 | tf_op jit(solution)/shard_map/all_gather | solution.py:109
  55.3 0.0 collective-permute-done
  55.3 0.7 fusion.16
  56.0 0.0 all-gather.2.cloned.1.call-update
  56.0 1.9 %collective-permute-start.1 = (bf16[768,256]{1,0:T(8,128)(2,1)S(1)}, bf16[768,256]{1,0:T(8,128)(2,1)S(1)}, u32[]{:S(2)}, u32[]{:S(2)}) collective-permute-start(bf16[768,256]{1,0:T(8,128)(2,1)S(1)} %all_gather.6), channel_id=1, source_target_pairs={{0,4},{4,8},{8,12},{12,16},{16,20},{20,24},{24,28},{28,0},{1,5},{5... | collective-permute-start | bytes 1179656 | tf_op jit(solution)/shard_map/ppermute | solution.py:25
  58.0 3.9 %collective-permute-start.2 = (bf16[768,256]{1,0:T(8,128)(2,1)S(1)}, bf16[768,256]{1,0:T(8,128)(2,1)S(1)}, u32[]{:S(2)}, u32[]{:S(2)}) collective-permute-start(bf16[768,256]{1,0:T(8,128)(2,1)S(1)} %all_gather.6), channel_id=1, source_target_pairs={{0,28},{4,0},{8,4},{12,8},{16,12},{20,16},{24,20},{28,24},{1,29},{... | collective-permute-start | bytes 1179656 | tf_op jit(solution)/shard_map/ppermute | solution.py:25
  61.9 0.0 slice-start
  62.0 0.2 broadcast_in_dim.51
  62.2 5.3 %collective-permute-done.1 = bf16[768,256]{1,0:T(8,128)(2,1)S(1)} collective-permute-done((bf16[768,256]{1,0:T(8,128)(2,1)S(1)}, bf16[768,256]{1,0:T(8,128)(2,1)S(1)}, u32[]{:S(2)}, u32[]{:S(2)}) %collective-permute-start.1) | collective-permute-done | bytes 393248 | tf_op jit(solution)/shard_map/ppermute | solution.py:25
  67.5 3.4 %collective-permute-start.3 = (bf16[768,256]{1,0:T(8,128)(2,1)S(1)}, bf16[768,256]{1,0:T(8,128)(2,1)S(1)}, u32[]{:S(2)}, u32[]{:S(2)}) collective-permute-start(bf16[768,256]{1,0:T(8,128)(2,1)S(1)} %collective-permute-done.1), channel_id=1, source_target_pairs={{0,4},{4,8},{8,12},{12,16},{16,20},{20,24},{24,28},{28,0},{1,5},{5... | collective-permute-start | bytes 1179656 | tf_op jit(solution)/shard_map/ppermute | solution.py:25
  70.9 0.0 collective-permute-done.2
  70.9 2.4 %collective-permute-start.4 = (bf16[768,256]{1,0:T(8,128)(2,1)S(1)}, bf16[768,256]{1,0:T(8,128)(2,1)S(1)}, u32[]{:S(2)}, u32[]{:S(2)}) collective-permute-start(bf16[768,256]{1,0:T(8,128)(2,1)S(1)} %collective-permute-done.2), channel_id=1, source_target_pairs={{0,28},{4,0},{8,4},{12,8},{16,12},{20,16},{24,20},{28,24},{1,29},{... | collective-permute-start | bytes 1179656 | tf_op jit(solution)/shard_map/ppermute | solution.py:25
  73.4 4.5 %collective-permute-done.3 = bf16[768,256]{1,0:T(8,128)(2,1)S(1)} collective-permute-done((bf16[768,256]{1,0:T(8,128)(2,1)S(1)}, bf16[768,256]{1,0:T(8,128)(2,1)S(1)}, u32[]{:S(2)}, u32[]{:S(2)}) %collective-permute-start.3) | collective-permute-done | bytes 393248 | tf_op jit(solution)/shard_map/ppermute | solution.py:25
  77.9 4.9 %collective-permute-start.5 = (bf16[768,256]{1,0:T(8,128)(2,1)S(1)}, bf16[768,256]{1,0:T(8,128)(2,1)S(1)}, u32[]{:S(2)}, u32[]{:S(2)}) collective-permute-start(bf16[768,256]{1,0:T(8,128)(2,1)S(1)} %collective-permute-done.3), channel_id=1, source_target_pairs={{0,4},{4,8},{8,12},{12,16},{16,20},{20,24},{24,28},{28,0},{1,5},{5... | collective-permute-start | bytes 1179656 | tf_op jit(solution)/shard_map/ppermute | solution.py:25
  82.8 0.0 collective-permute-done.4
  82.8 1.9 %collective-permute-start.6 = (bf16[768,256]{1,0:T(8,128)(2,1)S(1)}, bf16[768,256]{1,0:T(8,128)(2,1)S(1)}, u32[]{:S(2)}, u32[]{:S(2)}) collective-permute-start(bf16[768,256]{1,0:T(8,128)(2,1)S(1)} %collective-permute-done.4), channel_id=1, source_target_pairs={{0,28},{4,0},{8,4},{12,8},{16,12},{20,16},{24,20},{28,24},{1,29},{... | collective-permute-start | bytes 1179656 | tf_op jit(solution)/shard_map/ppermute | solution.py:25
  84.9 3.4 %collective-permute-done.5 = bf16[768,256]{1,0:T(8,128)(2,1)S(1)} collective-permute-done((bf16[768,256]{1,0:T(8,128)(2,1)S(1)}, bf16[768,256]{1,0:T(8,128)(2,1)S(1)}, u32[]{:S(2)}, u32[]{:S(2)}) %collective-permute-start.5) | collective-permute-done | bytes 393248 | tf_op jit(solution)/shard_map/ppermute | solution.py:25
  88.3 0.0 slice-start.1
  88.3 5.9 %collective-permute-start.7 = (bf16[384,256]{1,0:T(8,128)(2,1)S(1)}, bf16[384,256]{1,0:T(8,128)(2,1)S(1)}, u32[]{:S(2)}, u32[]{:S(2)}) collective-permute-start(bf16[384,256]{1,0:T(8,128)(2,1)S(1)} %slice.42), channel_id=1, source_target_pairs={{0,4},{4,8},{8,12},{12,16},{16,20},{20,24},{24,28},{28,0},{1,5},{5... | collective-permute-start | bytes 589832 | tf_op jit(solution)/shard_map/ppermute | solution.py:25
  94.2 0.0 collective-permute-done.6
  94.2 1.9 %collective-permute-start.8 = (bf16[384,256]{1,0:T(8,128)(2,1)S(1)}, bf16[384,256]{1,0:T(8,128)(2,1)S(1)}, u32[]{:S(2)}, u32[]{:S(2)}) collective-permute-start(bf16[384,256]{1,0:T(8,128)(2,1)S(1)} %slice.43), channel_id=1, source_target_pairs={{0,28},{4,0},{8,4},{12,8},{16,12},{20,16},{24,20},{28,24},{1,29},{... | collective-permute-start | bytes 589832 | tf_op jit(solution)/shard_map/ppermute | solution.py:25
  96.2 1.1 collective-permute-done.7
  97.4 5.6 %collective-permute-done.8 = bf16[384,256]{1,0:T(8,128)(2,1)S(1)} collective-permute-done((bf16[384,256]{1,0:T(8,128)(2,1)S(1)}, bf16[384,256]{1,0:T(8,128)(2,1)S(1)}, u32[]{:S(2)}, u32[]{:S(2)}) %collective-permute-start.8) | collective-permute-done | bytes 196640 | tf_op jit(solution)/shard_map/ppermute | solution.py:25
  103.0 0.0 copy-start.2
  103.0 0.8 convert_reduce_fusion
  103.9 0.9 multiply_reduce_fusion
  104.8 1.1 fusion.2
  105.9 0.0 copy-start.5
  105.9 0.0 copy-start.6
  106.0 0.0 copy-start.3
  106.0 3.8 %convolution_bitcast_fusion = f32[768,256]{1,0:T(8,128)S(1)} fusion(bf16[6144,256]{1,0:T(8,128)(2,1)S(1)} %fusion.2, bf16[6144,768]{1,0:T(8,128)(2,1)S(1)} %bitcast.79), kind=kOutput, calls=%fused_computation.6 | convolution fusion | flops 2415919104 | bytes 13369344 | tf_op jit(solution)/shard_map/dot_general | solution.py:115
  109.9 0.0 copy-done.5
  109.9 0.3 fusion.30
  110.3 0.1 fusion.15
  110.4 0.2 convolution_convert_fusion
  110.5 1.0 fusion.5
  111.6 1.9 %collective-permute-start.9 = (bf16[512,256]{1,0:T(8,128)(2,1)S(1)}, bf16[512,256]{1,0:T(8,128)(2,1)S(1)}, u32[]{:S(2)}, u32[]{:S(2)}) collective-permute-start(bf16[512,256]{1,0:T(8,128)(2,1)S(1)} %pad_maximum_fusion.1), channel_id=1, source_target_pairs={{0,8},{4,12},{8,16},{12,20},{16,24},{20,28},{24,0},{28,4},{1,9},{5... | collective-permute-start | bytes 786440 | tf_op jit(solution)/shard_map/ppermute | solution.py:25
  113.5 4.8 %collective-permute-start.12 = (bf16[512,256]{1,0:T(8,128)(2,1)S(1)}, bf16[512,256]{1,0:T(8,128)(2,1)S(1)}, u32[]{:S(2)}, u32[]{:S(2)}) collective-permute-start(bf16[512,256]{1,0:T(8,128)(2,1)S(1)} %pad_maximum_fusion.1), channel_id=1, source_target_pairs={{0,24},{4,28},{8,0},{12,4},{16,8},{20,12},{24,16},{28,20},{1,25},{... | collective-permute-start | bytes 786440 | tf_op jit(solution)/shard_map/ppermute | solution.py:25
  118.3 2.7 %collective-permute-start.10 = (bf16[512,256]{1,0:T(8,128)(2,1)S(1)}, bf16[512,256]{1,0:T(8,128)(2,1)S(1)}, u32[]{:S(2)}, u32[]{:S(2)}) collective-permute-start(bf16[512,256]{1,0:T(8,128)(2,1)S(1)} %pad_maximum_fusion.1), channel_id=1, source_target_pairs={{0,4},{4,8},{8,12},{12,16},{16,20},{20,24},{24,28},{28,0},{1,5},{5... | collective-permute-start | bytes 786440 | tf_op jit(solution)/shard_map/ppermute | solution.py:25
  121.0 3.2 %collective-permute-start.11 = (bf16[512,256]{1,0:T(8,128)(2,1)S(1)}, bf16[512,256]{1,0:T(8,128)(2,1)S(1)}, u32[]{:S(2)}, u32[]{:S(2)}) collective-permute-start(bf16[512,256]{1,0:T(8,128)(2,1)S(1)} %pad_maximum_fusion.1), channel_id=1, source_target_pairs={{0,28},{4,0},{8,4},{12,8},{16,12},{20,16},{24,20},{28,24},{1,29},{... | collective-permute-start | bytes 786440 | tf_op jit(solution)/shard_map/ppermute | solution.py:25
  124.2 2.3 %collective-permute-done.9 = bf16[512,256]{1,0:T(8,128)(2,1)S(1)} collective-permute-done((bf16[512,256]{1,0:T(8,128)(2,1)S(1)}, bf16[512,256]{1,0:T(8,128)(2,1)S(1)}, u32[]{:S(2)}, u32[]{:S(2)}) %collective-permute-start.9) | collective-permute-done | bytes 262176 | tf_op jit(solution)/shard_map/ppermute | solution.py:25
  126.4 2.0 %collective-permute-start.14 = (bf16[256,256]{1,0:T(8,128)(2,1)S(1)}, bf16[256,256]{1,0:T(8,128)(2,1)S(1)}, u32[]{:S(2)}, u32[]{:S(2)}) collective-permute-start(bf16[256,256]{1,0:T(8,128)(2,1)S(1)} %slice.49), channel_id=1, source_target_pairs={{0,8},{4,12},{8,16},{12,20},{16,24},{20,28},{24,0},{28,4},{1,9},{5... | collective-permute-start | bytes 393224 | tf_op jit(solution)/shard_map/ppermute | solution.py:25
  128.5 0.2 collective-permute-done.12
  128.7 4.6 %collective-permute-start.15 = (bf16[256,256]{1,0:T(8,128)(2,1)S(1)}, bf16[256,256]{1,0:T(8,128)(2,1)S(1)}, u32[]{:S(2)}, u32[]{:S(2)}) collective-permute-start(bf16[256,256]{1,0:T(8,128)(2,1)S(1)} %slice.50), channel_id=1, source_target_pairs={{0,24},{4,28},{8,0},{12,4},{16,8},{20,12},{24,16},{28,20},{1,25},{... | collective-permute-start | bytes 393224 | tf_op jit(solution)/shard_map/ppermute | solution.py:25
  133.2 4.6 %collective-permute-start.16 = (bf16[512,256]{1,0:T(8,128)(2,1)S(1)}, bf16[512,256]{1,0:T(8,128)(2,1)S(1)}, u32[]{:S(2)}, u32[]{:S(2)}) collective-permute-start(bf16[512,256]{1,0:T(8,128)(2,1)S(1)} %collective-permute-done.9), channel_id=1, source_target_pairs={{0,4},{4,8},{8,12},{12,16},{16,20},{20,24},{24,28},{28,0},{1,5},{5... | collective-permute-start | bytes 786440 | tf_op jit(solution)/shard_map/ppermute | solution.py:25
  137.9 0.0 collective-permute-done.10
  138.0 0.0 collective-permute-done.11
  138.0 0.0 all-gather.2.cloned.1.call-done
  138.0 1.0 fusion.14
  139.0 1.9 %collective-permute-start.13 = (bf16[512,256]{1,0:T(8,128)(2,1)S(1)}, bf16[512,256]{1,0:T(8,128)(2,1)S(1)}, u32[]{:S(2)}, u32[]{:S(2)}) collective-permute-start(bf16[512,256]{1,0:T(8,128)(2,1)S(1)} %fusion.14), channel_id=1, source_target_pairs={{0,28},{4,0},{8,4},{12,8},{16,12},{20,16},{24,20},{28,24},{1,29},{... | collective-permute-start | bytes 786440 | tf_op jit(solution)/shard_map/ppermute | solution.py:25
  141.0 0.0 collective-permute-done.14
  141.0 0.0 collective-permute-done.15
  141.0 2.8 %copy-done = bf16[6144,512]{1,0:T(8,128)(2,1)S(1)} copy-done((bf16[6144,512]{1,0:T(8,128)(2,1)S(1)}, bf16[6144,512]{1,0:T(8,128)(2,1)}, u32[]{:S(2)}) %copy-start) | copy-done | bytes 6291480
  143.8 2.2 %shard_map.82 = f32[768,256]{1,0:T(8,128)S(1)} custom-call(s32[1]{0:T(128)} %bitcast.1.first_ref, bf16[8,768,512]{2,1,0:T(8,128)(2,1)S(1)} %bitcast.70, bf16[5,512,256]{2,1,0:T(8,128)(2,1)S(1)} %bitcast_dynamic-update-slice_fusion.7.h_ref), custom_call_target="tpu_custom_call" | custom-call | flops 1006632960 | bytes 6029312 | tf_op jit(solution)/shard_map/pallas_call | solution.py:82
  146.0 0.0 collective-permute-done.16
  146.0 2.4 %collective-permute-done.13 = bf16[512,256]{1,0:T(8,128)(2,1)S(1)} collective-permute-done((bf16[512,256]{1,0:T(8,128)(2,1)S(1)}, bf16[512,256]{1,0:T(8,128)(2,1)S(1)}, u32[]{:S(2)}, u32[]{:S(2)}) %collective-permute-start.13) | collective-permute-done | bytes 262176 | tf_op jit(solution)/shard_map/ppermute | solution.py:25
  148.5 0.1 pad_maximum_fusion.h_ref
  148.6 1.3 shard_map.83
  149.9 0.0 copy-start.1
  149.9 0.0 copy-start.4
  149.9 0.1 add_convert_fusion
  150.1 27.2 %all_to_all.5 = bf16[4,192,256]{2,1,0:T(8,128)(2,1)S(1)} all-to-all(bf16[4,192,256]{2,1,0:T(8,128)(2,1)S(1)} %bitcast.72), channel_id=1, replica_groups=mesh['x'=4,'zlh'=2,'zll'=2,'c'=2,'y'=8,'zh'=4] {'zh'}, dimensions={0} | all-to-all | bytes 786432 | tf_op jit(solution)/shard_map/all_to_all | solution.py:137
  177.4 0.7 fusion.23
  (41 shorter events, 0.6 us)
Async XLA Ops:
  6.5 131.5 %all-gather.2.cloned.1.call-start = ((), (), s32[]{:S(2)}) async-start(), calls=%async_computation.1 | async-start | bytes 6488064 | tf_op jit(solution)/shard_map/all_gather | solution.py:111
  6.5 48.8 %collective-permute-start = (bf16[192,512]{1,0:T(8,128)(2,1)}, bf16[192,512]{1,0:T(8,128)(2,1)S(1)}, u32[]{:S(2)}, u32[]{:S(2)}) collective-permute-start(bf16[192,512]{1,0:T(8,128)(2,1)} %bitcast.80), channel_id=1, source_target_pairs={{0,0},{4,128},{8,256},{12,384},{16,512},{20,640},{24,768},{28,896}... | collective-permute-start | bytes 589832 | tf_op jit(solution)/shard_map/ppermute | solution.py:64
  56.0 11.4 %collective-permute-start.1 = (bf16[768,256]{1,0:T(8,128)(2,1)S(1)}, bf16[768,256]{1,0:T(8,128)(2,1)S(1)}, u32[]{:S(2)}, u32[]{:S(2)}) collective-permute-start(bf16[768,256]{1,0:T(8,128)(2,1)S(1)} %all_gather.6), channel_id=1, source_target_pairs={{0,4},{4,8},{8,12},{12,16},{16,20},{20,24},{24,28},{28,0},{1,5},{5... | collective-permute-start | bytes 1179656 | tf_op jit(solution)/shard_map/ppermute | solution.py:25
  58.0 12.9 %collective-permute-start.2 = (bf16[768,256]{1,0:T(8,128)(2,1)S(1)}, bf16[768,256]{1,0:T(8,128)(2,1)S(1)}, u32[]{:S(2)}, u32[]{:S(2)}) collective-permute-start(bf16[768,256]{1,0:T(8,128)(2,1)S(1)} %all_gather.6), channel_id=1, source_target_pairs={{0,28},{4,0},{8,4},{12,8},{16,12},{20,16},{24,20},{28,24},{1,29},{... | collective-permute-start | bytes 1179656 | tf_op jit(solution)/shard_map/ppermute | solution.py:25
  61.9 44.0 %slice-start = ((s8[9437184]{0:T(1024)(128)(4,1)}), s8[4194304]{0:T(1024)(128)(4,1)S(1)}, s32[]{:S(2)}) async-start(s8[9437184]{0:T(1024)(128)(4,1)} %bitcast.78), calls=%async_computation.2 | async-start | bytes 8388608
  67.5 10.5 %collective-permute-start.3 = (bf16[768,256]{1,0:T(8,128)(2,1)S(1)}, bf16[768,256]{1,0:T(8,128)(2,1)S(1)}, u32[]{:S(2)}, u32[]{:S(2)}) collective-permute-start(bf16[768,256]{1,0:T(8,128)(2,1)S(1)} %collective-permute-done.1), channel_id=1, source_target_pairs={{0,4},{4,8},{8,12},{12,16},{16,20},{20,24},{24,28},{28,0},{1,5},{5... | collective-permute-start | bytes 1179656 | tf_op jit(solution)/shard_map/ppermute | solution.py:25
  70.9 12.0 %collective-permute-start.4 = (bf16[768,256]{1,0:T(8,128)(2,1)S(1)}, bf16[768,256]{1,0:T(8,128)(2,1)S(1)}, u32[]{:S(2)}, u32[]{:S(2)}) collective-permute-start(bf16[768,256]{1,0:T(8,128)(2,1)S(1)} %collective-permute-done.2), channel_id=1, source_target_pairs={{0,28},{4,0},{8,4},{12,8},{16,12},{20,16},{24,20},{28,24},{1,29},{... | collective-permute-start | bytes 1179656 | tf_op jit(solution)/shard_map/ppermute | solution.py:25
  77.9 10.3 %collective-permute-start.5 = (bf16[768,256]{1,0:T(8,128)(2,1)S(1)}, bf16[768,256]{1,0:T(8,128)(2,1)S(1)}, u32[]{:S(2)}, u32[]{:S(2)}) collective-permute-start(bf16[768,256]{1,0:T(8,128)(2,1)S(1)} %collective-permute-done.3), channel_id=1, source_target_pairs={{0,4},{4,8},{8,12},{12,16},{16,20},{20,24},{24,28},{28,0},{1,5},{5... | collective-permute-start | bytes 1179656 | tf_op jit(solution)/shard_map/ppermute | solution.py:25
  82.8 11.3 %collective-permute-start.6 = (bf16[768,256]{1,0:T(8,128)(2,1)S(1)}, bf16[768,256]{1,0:T(8,128)(2,1)S(1)}, u32[]{:S(2)}, u32[]{:S(2)}) collective-permute-start(bf16[768,256]{1,0:T(8,128)(2,1)S(1)} %collective-permute-done.4), channel_id=1, source_target_pairs={{0,28},{4,0},{8,4},{12,8},{16,12},{20,16},{24,20},{28,24},{1,29},{... | collective-permute-start | bytes 1179656 | tf_op jit(solution)/shard_map/ppermute | solution.py:25
  88.3 17.6 %slice-start.1 = ((s8[9437184]{0:T(1024)(128)(4,1)}), s8[4194304]{0:T(1024)(128)(4,1)S(1)}, s32[]{:S(2)}) async-start(s8[9437184]{0:T(1024)(128)(4,1)} %bitcast.78), calls=%async_computation.3 | async-start | bytes 8388608
  88.3 9.0 %collective-permute-start.7 = (bf16[384,256]{1,0:T(8,128)(2,1)S(1)}, bf16[384,256]{1,0:T(8,128)(2,1)S(1)}, u32[]{:S(2)}, u32[]{:S(2)}) collective-permute-start(bf16[384,256]{1,0:T(8,128)(2,1)S(1)} %slice.42), channel_id=1, source_target_pairs={{0,4},{4,8},{8,12},{12,16},{16,20},{20,24},{24,28},{28,0},{1,5},{5... | collective-permute-start | bytes 589832 | tf_op jit(solution)/shard_map/ppermute | solution.py:25
  94.2 8.8 %collective-permute-start.8 = (bf16[384,256]{1,0:T(8,128)(2,1)S(1)}, bf16[384,256]{1,0:T(8,128)(2,1)S(1)}, u32[]{:S(2)}, u32[]{:S(2)}) collective-permute-start(bf16[384,256]{1,0:T(8,128)(2,1)S(1)} %slice.43), channel_id=1, source_target_pairs={{0,28},{4,0},{8,4},{12,8},{16,12},{20,16},{24,20},{28,24},{1,29},{... | collective-permute-start | bytes 589832 | tf_op jit(solution)/shard_map/ppermute | solution.py:25
  103.0 1.7 copy-start.2
  103.9 2.1 %slice-start.2 = ((s8[9437184]{0:T(1024)(128)(4,1)}), s8[1048576]{0:T(1024)(128)(4,1)S(1)}, s32[]{:S(2)}) async-start(s8[9437184]{0:T(1024)(128)(4,1)} %bitcast.78), calls=%async_computation.4 | async-start | bytes 2097152
  105.9 4.0 %copy-start.5 = (f32[1,128]{1,0:T(1,128)S(1)}, f32[1,128]{1,0:T(1,128)}, u32[]{:S(2)}) copy-start(f32[1,128]{1,0:T(1,128)} %param.12) | copy-start | bytes 1540
  105.9 4.0 %copy-start.6 = (f32[1,128]{1,0:T(1,128)S(1)}, f32[1,128]{1,0:T(1,128)}, u32[]{:S(2)}) copy-start(f32[1,128]{1,0:T(1,128)} %param.11) | copy-start | bytes 1540
  106.0 4.6 %copy-start.3 = (f32[384]{0:T(512)S(1)}, f32[384]{0:T(512)}, u32[]{:S(2)}) copy-start(f32[384]{0:T(512)} %param.13) | copy-start | bytes 4612
  111.6 14.9 %collective-permute-start.9 = (bf16[512,256]{1,0:T(8,128)(2,1)S(1)}, bf16[512,256]{1,0:T(8,128)(2,1)S(1)}, u32[]{:S(2)}, u32[]{:S(2)}) collective-permute-start(bf16[512,256]{1,0:T(8,128)(2,1)S(1)} %pad_maximum_fusion.1), channel_id=1, source_target_pairs={{0,8},{4,12},{8,16},{12,20},{16,24},{20,28},{24,0},{28,4},{1,9},{5... | collective-permute-start | bytes 786440 | tf_op jit(solution)/shard_map/ppermute | solution.py:25
  113.5 15.2 %collective-permute-start.12 = (bf16[512,256]{1,0:T(8,128)(2,1)S(1)}, bf16[512,256]{1,0:T(8,128)(2,1)S(1)}, u32[]{:S(2)}, u32[]{:S(2)}) collective-permute-start(bf16[512,256]{1,0:T(8,128)(2,1)S(1)} %pad_maximum_fusion.1), channel_id=1, source_target_pairs={{0,24},{4,28},{8,0},{12,4},{16,8},{20,12},{24,16},{28,20},{1,25},{... | collective-permute-start | bytes 786440 | tf_op jit(solution)/shard_map/ppermute | solution.py:25
  118.3 19.6 %collective-permute-start.10 = (bf16[512,256]{1,0:T(8,128)(2,1)S(1)}, bf16[512,256]{1,0:T(8,128)(2,1)S(1)}, u32[]{:S(2)}, u32[]{:S(2)}) collective-permute-start(bf16[512,256]{1,0:T(8,128)(2,1)S(1)} %pad_maximum_fusion.1), channel_id=1, source_target_pairs={{0,4},{4,8},{8,12},{12,16},{16,20},{20,24},{24,28},{28,0},{1,5},{5... | collective-permute-start | bytes 786440 | tf_op jit(solution)/shard_map/ppermute | solution.py:25
  121.0 17.0 %collective-permute-start.11 = (bf16[512,256]{1,0:T(8,128)(2,1)S(1)}, bf16[512,256]{1,0:T(8,128)(2,1)S(1)}, u32[]{:S(2)}, u32[]{:S(2)}) collective-permute-start(bf16[512,256]{1,0:T(8,128)(2,1)S(1)} %pad_maximum_fusion.1), channel_id=1, source_target_pairs={{0,28},{4,0},{8,4},{12,8},{16,12},{20,16},{24,20},{28,24},{1,29},{... | collective-permute-start | bytes 786440 | tf_op jit(solution)/shard_map/ppermute | solution.py:25
  126.4 14.5 %collective-permute-start.14 = (bf16[256,256]{1,0:T(8,128)(2,1)S(1)}, bf16[256,256]{1,0:T(8,128)(2,1)S(1)}, u32[]{:S(2)}, u32[]{:S(2)}) collective-permute-start(bf16[256,256]{1,0:T(8,128)(2,1)S(1)} %slice.49), channel_id=1, source_target_pairs={{0,8},{4,12},{8,16},{12,20},{16,24},{20,28},{24,0},{28,4},{1,9},{5... | collective-permute-start | bytes 393224 | tf_op jit(solution)/shard_map/ppermute | solution.py:25
  128.7 12.3 %collective-permute-start.15 = (bf16[256,256]{1,0:T(8,128)(2,1)S(1)}, bf16[256,256]{1,0:T(8,128)(2,1)S(1)}, u32[]{:S(2)}, u32[]{:S(2)}) collective-permute-start(bf16[256,256]{1,0:T(8,128)(2,1)S(1)} %slice.50), channel_id=1, source_target_pairs={{0,24},{4,28},{8,0},{12,4},{16,8},{20,12},{24,16},{28,20},{1,25},{... | collective-permute-start | bytes 393224 | tf_op jit(solution)/shard_map/ppermute | solution.py:25
  133.2 12.8 %collective-permute-start.16 = (bf16[512,256]{1,0:T(8,128)(2,1)S(1)}, bf16[512,256]{1,0:T(8,128)(2,1)S(1)}, u32[]{:S(2)}, u32[]{:S(2)}) collective-permute-start(bf16[512,256]{1,0:T(8,128)(2,1)S(1)} %collective-permute-done.9), channel_id=1, source_target_pairs={{0,4},{4,8},{8,12},{12,16},{16,20},{20,24},{24,28},{28,0},{1,5},{5... | collective-permute-start | bytes 786440 | tf_op jit(solution)/shard_map/ppermute | solution.py:25
  139.0 9.5 %collective-permute-start.13 = (bf16[512,256]{1,0:T(8,128)(2,1)S(1)}, bf16[512,256]{1,0:T(8,128)(2,1)S(1)}, u32[]{:S(2)}, u32[]{:S(2)}) collective-permute-start(bf16[512,256]{1,0:T(8,128)(2,1)S(1)} %fusion.14), channel_id=1, source_target_pairs={{0,28},{4,0},{8,4},{12,8},{16,12},{20,16},{24,20},{28,24},{1,29},{... | collective-permute-start | bytes 786440 | tf_op jit(solution)/shard_map/ppermute | solution.py:25
  141.0 2.8 %copy-start = (bf16[6144,512]{1,0:T(8,128)(2,1)S(1)}, bf16[6144,512]{1,0:T(8,128)(2,1)}, u32[]{:S(2)}) copy-start(bf16[6144,512]{1,0:T(8,128)(2,1)} %all-gather.2.cloned.1.call-done) | copy-start | bytes 18874372
  149.9 27.4 %copy-start.1 = (bf16[1,256,192]{1,2,0:T(8,128)(2,1)S(1)}, bf16[1,256,192]{1,2,0:T(8,128)(2,1)}, u32[]{:S(2)}) copy-start(bf16[1,256,192]{1,2,0:T(8,128)(2,1)} %param.8) | copy-start | bytes 294916
  149.9 27.4 %copy-start.4 = (f32[192]{0:T(256)S(1)}, f32[192]{0:T(256)}, u32[]{:S(2)}) copy-start(f32[192]{0:T(256)} %param.15) | copy-start | bytes 2308
Sparse Core Ops, SparseCore 0:
  56.2 69.5 all-gather.1

commit v10 on v9

--- a/solution.py
+++ b/solution.py
@@ -29,10 +29,10 @@
     half = block.shape[0] // 2
     below2, above2 = shift(block, "y", NY, 2), shift(block, "y", NY, -2)
     below1, above1 = shift(block, "y", NY, 1), shift(block, "y", NY, -1)
-    late = above2 if zero is None else above2 + zero
-    below3, above3 = shift(below2, "y", NY, 1), shift(late, "y", NY, -1)
+    below3, above3 = shift(below2, "y", NY, 1), shift(above2, "y", NY, -1)
     far_top = shift(below2[:half], "y", NY, 2)
-    far_bottom = shift(above2[half:], "y", NY, -2)
+    late = above2[half:] if zero is None else above2[half:] + zero[half:]
+    far_bottom = shift(late, "y", NY, -2)
     return (below2, below1, block, above1, above2), (above3, far_top, far_bottom, below3)
 
 

time: 186 us -> 186 us (level)
  the two profiles are of different devices: /device:TPU:120 before, /device:TPU:64 now
where the time goes in v10:
time: 186 us
  starting transfers between devices  74.1 us (40%)
  blocking collectives  61.7 us (33%)
  waiting for transfers between devices  17.7 us (10%)
  between operations  14 us (8%)
  other arithmetic  5.79 us (3%)
  local copies, waits for them, and re-layouts  4.4 us (2%)
  matrix products  4.34 us (2%)
  Pallas kernels  3.56 us (2%)
    ppermute x16, starting transfers between devices, shift(): lax.ppermute(value, axis, [(i, (i + by) % count) for i in range(count)])  72.5 us
    all_gather x1, blocking collectives, per_device(): zgroup = lax.all_gather(mine, 'zh', axis=0, tiled=True)  32.3 us
    all_to_all x1, blocking collectives, per_device(): pieces = lax.all_to_all(part, 'zh', 0, 0)  29.4 us
    ppermute x16, waiting for transfers between devices, shift(): lax.ppermute(value, axis, [(i, (i + by) % count) for i in range(count)])  17.7 us
    dot_general x1, matrix products, per_device(): lax.dot_general(w_in, normed, (((0,), (0,)), ((), ())), preferred_element...  3.83 us
  transfers between devices with their start and end apart: 18, of which 7 were waited for; matrix products, arithmetic and copies ran while one was open for 5% of the time, Pallas kernels for 1%

profile of v10, /device:TPU:64, one launch (start us, length us, event | category | flops | bytes accessed | tf_op | source)
XLA Modules:
  0.0 185.6 jit_solution(9101160882319571557)
XLA Ops:
  6.5 0.0 all-gather.2.cloned.1.call-start
  6.5 1.6 collective-permute-start
  8.1 32.3 %all_gather.6 = bf16[768,256]{1,0:T(8,128)(2,1)S(1)} all-gather(bf16[192,256]{1,0:T(8,128)(2,1)} %bitcast.73), channel_id=1, replica_groups=mesh['x'=4,'zlh'=2,'zll'=2,'c'=2,'y'=8,'zh'=4] {'zh'}, dimensions={0}, use_global_device_ids=true | all-gather | bytes 491520 | tf_op jit(solution)/shard_map/all_gather | solution.py:109
  40.4 0.0 collective-permute-done
  40.4 0.7 fusion.14
  41.1 0.0 all-gather.2.cloned.1.call-update
  41.1 16.7 %collective-permute-start.1 = (bf16[768,256]{1,0:T(8,128)(2,1)S(1)}, bf16[768,256]{1,0:T(8,128)(2,1)S(1)}, u32[]{:S(2)}, u32[]{:S(2)}) collective-permute-start(bf16[768,256]{1,0:T(8,128)(2,1)S(1)} %all_gather.6), channel_id=1, source_target_pairs={{0,4},{4,8},{8,12},{12,16},{16,20},{20,24},{24,28},{28,0},{1,5},{5... | collective-permute-start | bytes 1179656 | tf_op jit(solution)/shard_map/ppermute | solution.py:25
  57.9 5.5 %collective-permute-start.2 = (bf16[768,256]{1,0:T(8,128)(2,1)S(1)}, bf16[768,256]{1,0:T(8,128)(2,1)S(1)}, u32[]{:S(2)}, u32[]{:S(2)}) collective-permute-start(bf16[768,256]{1,0:T(8,128)(2,1)S(1)} %all_gather.6), channel_id=1, source_target_pairs={{0,28},{4,0},{8,4},{12,8},{16,12},{20,16},{24,20},{28,24},{1,29},{... | collective-permute-start | bytes 1179656 | tf_op jit(solution)/shard_map/ppermute | solution.py:25
  63.4 0.0 slice-start
  63.4 0.2 broadcast_in_dim.51
  63.7 5.5 %collective-permute-done.1 = bf16[768,256]{1,0:T(8,128)(2,1)S(1)} collective-permute-done((bf16[768,256]{1,0:T(8,128)(2,1)S(1)}, bf16[768,256]{1,0:T(8,128)(2,1)S(1)}, u32[]{:S(2)}, u32[]{:S(2)}) %collective-permute-start.1) | collective-permute-done | bytes 393248 | tf_op jit(solution)/shard_map/ppermute | solution.py:25
  69.2 1.9 %collective-permute-start.3 = (bf16[768,256]{1,0:T(8,128)(2,1)S(1)}, bf16[768,256]{1,0:T(8,128)(2,1)S(1)}, u32[]{:S(2)}, u32[]{:S(2)}) collective-permute-start(bf16[768,256]{1,0:T(8,128)(2,1)S(1)} %collective-permute-done.1), channel_id=1, source_target_pairs={{0,4},{4,8},{8,12},{12,16},{16,20},{20,24},{24,28},{28,0},{1,5},{5... | collective-permute-start | bytes 1179656 | tf_op jit(solution)/shard_map/ppermute | solution.py:25
  71.1 0.0 collective-permute-done.2
  71.1 5.1 %collective-permute-start.4 = (bf16[768,256]{1,0:T(8,128)(2,1)S(1)}, bf16[768,256]{1,0:T(8,128)(2,1)S(1)}, u32[]{:S(2)}, u32[]{:S(2)}) collective-permute-start(bf16[768,256]{1,0:T(8,128)(2,1)S(1)} %collective-permute-done.2), channel_id=1, source_target_pairs={{0,28},{4,0},{8,4},{12,8},{16,12},{20,16},{24,20},{28,24},{1,29},{... | collective-permute-start | bytes 1179656 | tf_op jit(solution)/shard_map/ppermute | solution.py:25
  76.3 4.8 %collective-permute-done.3 = bf16[768,256]{1,0:T(8,128)(2,1)S(1)} collective-permute-done((bf16[768,256]{1,0:T(8,128)(2,1)S(1)}, bf16[768,256]{1,0:T(8,128)(2,1)S(1)}, u32[]{:S(2)}, u32[]{:S(2)}) %collective-permute-start.3) | collective-permute-done | bytes 393248 | tf_op jit(solution)/shard_map/ppermute | solution.py:25
  81.2 1.9 %collective-permute-start.5 = (bf16[768,256]{1,0:T(8,128)(2,1)S(1)}, bf16[768,256]{1,0:T(8,128)(2,1)S(1)}, u32[]{:S(2)}, u32[]{:S(2)}) collective-permute-start(bf16[768,256]{1,0:T(8,128)(2,1)S(1)} %collective-permute-done.3), channel_id=1, source_target_pairs={{0,4},{4,8},{8,12},{12,16},{16,20},{20,24},{24,28},{28,0},{1,5},{5... | collective-permute-start | bytes 1179656 | tf_op jit(solution)/shard_map/ppermute | solution.py:25
  83.1 0.0 collective-permute-done.4
  83.1 5.1 %collective-permute-start.6 = (bf16[768,256]{1,0:T(8,128)(2,1)S(1)}, bf16[768,256]{1,0:T(8,128)(2,1)S(1)}, u32[]{:S(2)}, u32[]{:S(2)}) collective-permute-start(bf16[768,256]{1,0:T(8,128)(2,1)S(1)} %collective-permute-done.4), channel_id=1, source_target_pairs={{0,28},{4,0},{8,4},{12,8},{16,12},{20,16},{24,20},{28,24},{1,29},{... | collective-permute-start | bytes 1179656 | tf_op jit(solution)/shard_map/ppermute | solution.py:25
  88.3 3.9 %collective-permute-done.5 = bf16[768,256]{1,0:T(8,128)(2,1)S(1)} collective-permute-done((bf16[768,256]{1,0:T(8,128)(2,1)S(1)}, bf16[768,256]{1,0:T(8,128)(2,1)S(1)}, u32[]{:S(2)}, u32[]{:S(2)}) %collective-permute-start.5) | collective-permute-done | bytes 393248 | tf_op jit(solution)/shard_map/ppermute | solution.py:25
  92.2 0.0 slice-start.1
  92.2 2.2 %collective-permute-start.7 = (bf16[384,256]{1,0:T(8,128)(2,1)S(1)}, bf16[384,256]{1,0:T(8,128)(2,1)S(1)}, u32[]{:S(2)}, u32[]{:S(2)}) collective-permute-start(bf16[384,256]{1,0:T(8,128)(2,1)S(1)} %slice.50), channel_id=1, source_target_pairs={{0,4},{4,8},{8,12},{12,16},{16,20},{20,24},{24,28},{28,0},{1,5},{5... | collective-permute-start | bytes 589832 | tf_op jit(solution)/shard_map/ppermute | solution.py:25
  94.4 0.0 collective-permute-done.6
  94.5 5.1 %collective-permute-start.8 = (bf16[384,256]{1,0:T(8,128)(2,1)S(1)}, bf16[384,256]{1,0:T(8,128)(2,1)S(1)}, u32[]{:S(2)}, u32[]{:S(2)}) collective-permute-start(bf16[384,256]{1,0:T(8,128)(2,1)S(1)} %slice.51), channel_id=1, source_target_pairs={{0,28},{4,0},{8,4},{12,8},{16,12},{20,16},{24,20},{28,24},{1,29},{... | collective-permute-start | bytes 589832 | tf_op jit(solution)/shard_map/ppermute | solution.py:25
  99.7 1.6 collective-permute-done.7
  101.3 1.5 collective-permute-done.8
  102.8 0.0 copy-start.2
  102.8 0.8 convert_reduce_fusion
  103.6 0.9 multiply_reduce_fusion
  104.5 1.1 fusion.2
  105.7 0.0 copy-start.5
  105.7 0.0 copy-start.6
  105.7 0.0 copy-start.3
  105.7 3.8 %convolution_bitcast_fusion = f32[768,256]{1,0:T(8,128)S(1)} fusion(bf16[6144,256]{1,0:T(8,128)(2,1)S(1)} %fusion.2, bf16[6144,768]{1,0:T(8,128)(2,1)S(1)} %bitcast.79), kind=kOutput, calls=%fused_computation.6 | convolution fusion | flops 2415919104 | bytes 13369344 | tf_op jit(solution)/shard_map/dot_general | solution.py:115
  109.7 0.3 fusion.30
  110.1 0.1 fusion.13
  110.1 0.2 convolution_convert_fusion
  110.3 1.0 fusion.5
  111.3 2.3 %collective-permute-start.9 = (bf16[512,256]{1,0:T(8,128)(2,1)S(1)}, bf16[512,256]{1,0:T(8,128)(2,1)S(1)}, u32[]{:S(2)}, u32[]{:S(2)}) collective-permute-start(bf16[512,256]{1,0:T(8,128)(2,1)S(1)} %pad_maximum_fusion.1), channel_id=1, source_target_pairs={{0,8},{4,12},{8,16},{12,20},{16,24},{20,28},{24,0},{28,4},{1,9},{5... | collective-permute-start | bytes 786440 | tf_op jit(solution)/shard_map/ppermute | solution.py:25
  113.6 5.7 %collective-permute-start.12 = (bf16[512,256]{1,0:T(8,128)(2,1)S(1)}, bf16[512,256]{1,0:T(8,128)(2,1)S(1)}, u32[]{:S(2)}, u32[]{:S(2)}) collective-permute-start(bf16[512,256]{1,0:T(8,128)(2,1)S(1)} %pad_maximum_fusion.1), channel_id=1, source_target_pairs={{0,24},{4,28},{8,0},{12,4},{16,8},{20,12},{24,16},{28,20},{1,25},{... | collective-permute-start | bytes 786440 | tf_op jit(solution)/shard_map/ppermute | solution.py:25
  119.3 2.9 %collective-permute-start.10 = (bf16[512,256]{1,0:T(8,128)(2,1)S(1)}, bf16[512,256]{1,0:T(8,128)(2,1)S(1)}, u32[]{:S(2)}, u32[]{:S(2)}) collective-permute-start(bf16[512,256]{1,0:T(8,128)(2,1)S(1)} %pad_maximum_fusion.1), channel_id=1, source_target_pairs={{0,4},{4,8},{8,12},{12,16},{16,20},{20,24},{24,28},{28,0},{1,5},{5... | collective-permute-start | bytes 786440 | tf_op jit(solution)/shard_map/ppermute | solution.py:25
  122.2 4.1 %collective-permute-start.11 = (bf16[512,256]{1,0:T(8,128)(2,1)S(1)}, bf16[512,256]{1,0:T(8,128)(2,1)S(1)}, u32[]{:S(2)}, u32[]{:S(2)}) collective-permute-start(bf16[512,256]{1,0:T(8,128)(2,1)S(1)} %pad_maximum_fusion.1), channel_id=1, source_target_pairs={{0,28},{4,0},{8,4},{12,8},{16,12},{20,16},{24,20},{28,24},{1,29},{... | collective-permute-start | bytes 786440 | tf_op jit(solution)/shard_map/ppermute | solution.py:25
  126.4 0.2 collective-permute-done.9
  126.5 4.0 %collective-permute-start.14 = (bf16[256,256]{1,0:T(8,128)(2,1)S(1)}, bf16[256,256]{1,0:T(8,128)(2,1)S(1)}, u32[]{:S(2)}, u32[]{:S(2)}) collective-permute-start(bf16[256,256]{1,0:T(8,128)(2,1)S(1)} %slice.56), channel_id=1, source_target_pairs={{0,8},{4,12},{8,16},{12,20},{16,24},{20,28},{24,0},{28,4},{1,9},{5... | collective-permute-start | bytes 393224 | tf_op jit(solution)/shard_map/ppermute | solution.py:25
  130.5 2.6 %collective-permute-start.16 = (bf16[512,256]{1,0:T(8,128)(2,1)S(1)}, bf16[512,256]{1,0:T(8,128)(2,1)S(1)}, u32[]{:S(2)}, u32[]{:S(2)}) collective-permute-start(bf16[512,256]{1,0:T(8,128)(2,1)S(1)} %collective-permute-done.9), channel_id=1, source_target_pairs={{0,4},{4,8},{8,12},{12,16},{16,20},{20,24},{24,28},{28,0},{1,5},{5... | collective-permute-start | bytes 786440 | tf_op jit(solution)/shard_map/ppermute | solution.py:25
  133.1 0.0 collective-permute-done.12
  133.1 4.5 %collective-permute-start.13 = (bf16[512,256]{1,0:T(8,128)(2,1)S(1)}, bf16[512,256]{1,0:T(8,128)(2,1)S(1)}, u32[]{:S(2)}, u32[]{:S(2)}) collective-permute-start(bf16[512,256]{1,0:T(8,128)(2,1)S(1)} %collective-permute-done.12), channel_id=1, source_target_pairs={{0,28},{4,0},{8,4},{12,8},{16,12},{20,16},{24,20},{28,24},{1,29},{... | collective-permute-start | bytes 786440 | tf_op jit(solution)/shard_map/ppermute | solution.py:25
  137.6 0.0 collective-permute-done.10
  137.7 0.0 collective-permute-done.11
  137.7 0.0 all-gather.2.cloned.1.call-done
  137.7 1.0 slice.58
  138.7 2.9 %collective-permute-start.15 = (bf16[256,256]{1,0:T(8,128)(2,1)S(1)}, bf16[256,256]{1,0:T(8,128)(2,1)S(1)}, u32[]{:S(2)}, u32[]{:S(2)}) collective-permute-start(bf16[256,256]{1,0:T(8,128)(2,1)S(1)} %fusion.18), channel_id=1, source_target_pairs={{0,24},{4,28},{8,0},{12,4},{16,8},{20,12},{24,16},{28,20},{1,25},{... | collective-permute-start | bytes 393224 | tf_op jit(solution)/shard_map/ppermute | solution.py:25
  141.7 2.8 %copy-done = bf16[6144,512]{1,0:T(8,128)(2,1)S(1)} copy-done((bf16[6144,512]{1,0:T(8,128)(2,1)S(1)}, bf16[6144,512]{1,0:T(8,128)(2,1)}, u32[]{:S(2)}) %copy-start) | copy-done | bytes 6291480
  144.5 2.2 %shard_map.82 = f32[768,256]{1,0:T(8,128)S(1)} custom-call(s32[1]{0:T(128)} %bitcast.1.first_ref, bf16[8,768,512]{2,1,0:T(8,128)(2,1)S(1)} %bitcast.70, bf16[5,512,256]{2,1,0:T(8,128)(2,1)S(1)} %bitcast_dynamic-update-slice_fusion.7.h_ref), custom_call_target="tpu_custom_call" | custom-call | flops 1006632960 | bytes 6029312 | tf_op jit(solution)/shard_map/pallas_call | solution.py:82
  146.7 0.0 collective-permute-done.14
  146.7 0.2 collective-permute-done.15
  146.9 0.0 collective-permute-done.13
  147.0 0.0 collective-permute-done.16
  147.0 0.1 pad_maximum_fusion.h_ref
  147.1 1.3 shard_map.83
  148.4 0.0 copy-start.1
  148.4 0.0 copy-start.4
  148.4 0.1 add_convert_fusion
  148.6 29.4 %all_to_all.5 = bf16[4,192,256]{2,1,0:T(8,128)(2,1)S(1)} all-to-all(bf16[4,192,256]{2,1,0:T(8,128)(2,1)S(1)} %bitcast.72), channel_id=1, replica_groups=mesh['x'=4,'zlh'=2,'zll'=2,'c'=2,'y'=8,'zh'=4] {'zh'}, dimensions={0} | all-to-all | bytes 786432 | tf_op jit(solution)/shard_map/all_to_all | solution.py:137
  178.0 0.7 fusion.23
  (41 shorter events, 0.7 us)
Async XLA Ops:
  6.5 131.2 %all-gather.2.cloned.1.call-start = ((), (), s32[]{:S(2)}) async-start(), calls=%async_computation.1 | async-start | bytes 6488064 | tf_op jit(solution)/shard_map/all_gather | solution.py:111
  6.5 33.9 %collective-permute-start = (bf16[192,512]{1,0:T(8,128)(2,1)}, bf16[192,512]{1,0:T(8,128)(2,1)S(1)}, u32[]{:S(2)}, u32[]{:S(2)}) collective-permute-start(bf16[192,512]{1,0:T(8,128)(2,1)} %bitcast.80), channel_id=1, source_target_pairs={{0,0},{4,128},{8,256},{12,384},{16,512},{20,640},{24,768},{28,896}... | collective-permute-start | bytes 589832 | tf_op jit(solution)/shard_map/ppermute | solution.py:64
  41.1 28.1 %collective-permute-start.1 = (bf16[768,256]{1,0:T(8,128)(2,1)S(1)}, bf16[768,256]{1,0:T(8,128)(2,1)S(1)}, u32[]{:S(2)}, u32[]{:S(2)}) collective-permute-start(bf16[768,256]{1,0:T(8,128)(2,1)S(1)} %all_gather.6), channel_id=1, source_target_pairs={{0,4},{4,8},{8,12},{12,16},{16,20},{20,24},{24,28},{28,0},{1,5},{5... | collective-permute-start | bytes 1179656 | tf_op jit(solution)/shard_map/ppermute | solution.py:25
  57.9 13.2 %collective-permute-start.2 = (bf16[768,256]{1,0:T(8,128)(2,1)S(1)}, bf16[768,256]{1,0:T(8,128)(2,1)S(1)}, u32[]{:S(2)}, u32[]{:S(2)}) collective-permute-start(bf16[768,256]{1,0:T(8,128)(2,1)S(1)} %all_gather.6), channel_id=1, source_target_pairs={{0,28},{4,0},{8,4},{12,8},{16,12},{20,16},{24,20},{28,24},{1,29},{... | collective-permute-start | bytes 1179656 | tf_op jit(solution)/shard_map/ppermute | solution.py:25
  63.4 42.3 %slice-start = ((s8[9437184]{0:T(1024)(128)(4,1)}), s8[4194304]{0:T(1024)(128)(4,1)S(1)}, s32[]{:S(2)}) async-start(s8[9437184]{0:T(1024)(128)(4,1)} %bitcast.78), calls=%async_computation.2 | async-start | bytes 8388608
  69.2 12.0 %collective-permute-start.3 = (bf16[768,256]{1,0:T(8,128)(2,1)S(1)}, bf16[768,256]{1,0:T(8,128)(2,1)S(1)}, u32[]{:S(2)}, u32[]{:S(2)}) collective-permute-start(bf16[768,256]{1,0:T(8,128)(2,1)S(1)} %collective-permute-done.1), channel_id=1, source_target_pairs={{0,4},{4,8},{8,12},{12,16},{16,20},{20,24},{24,28},{28,0},{1,5},{5... | collective-permute-start | bytes 1179656 | tf_op jit(solution)/shard_map/ppermute | solution.py:25
  71.1 12.0 %collective-permute-start.4 = (bf16[768,256]{1,0:T(8,128)(2,1)S(1)}, bf16[768,256]{1,0:T(8,128)(2,1)S(1)}, u32[]{:S(2)}, u32[]{:S(2)}) collective-permute-start(bf16[768,256]{1,0:T(8,128)(2,1)S(1)} %collective-permute-done.2), channel_id=1, source_target_pairs={{0,28},{4,0},{8,4},{12,8},{16,12},{20,16},{24,20},{28,24},{1,29},{... | collective-permute-start | bytes 1179656 | tf_op jit(solution)/shard_map/ppermute | solution.py:25
  81.2 11.0 %collective-permute-start.5 = (bf16[768,256]{1,0:T(8,128)(2,1)S(1)}, bf16[768,256]{1,0:T(8,128)(2,1)S(1)}, u32[]{:S(2)}, u32[]{:S(2)}) collective-permute-start(bf16[768,256]{1,0:T(8,128)(2,1)S(1)} %collective-permute-done.3), channel_id=1, source_target_pairs={{0,4},{4,8},{8,12},{12,16},{16,20},{20,24},{24,28},{28,0},{1,5},{5... | collective-permute-start | bytes 1179656 | tf_op jit(solution)/shard_map/ppermute | solution.py:25
  83.1 11.3 %collective-permute-start.6 = (bf16[768,256]{1,0:T(8,128)(2,1)S(1)}, bf16[768,256]{1,0:T(8,128)(2,1)S(1)}, u32[]{:S(2)}, u32[]{:S(2)}) collective-permute-start(bf16[768,256]{1,0:T(8,128)(2,1)S(1)} %collective-permute-done.4), channel_id=1, source_target_pairs={{0,28},{4,0},{8,4},{12,8},{16,12},{20,16},{24,20},{28,24},{1,29},{... | collective-permute-start | bytes 1179656 | tf_op jit(solution)/shard_map/ppermute | solution.py:25
  92.2 13.5 %slice-start.1 = ((s8[9437184]{0:T(1024)(128)(4,1)}), s8[4194304]{0:T(1024)(128)(4,1)S(1)}, s32[]{:S(2)}) async-start(s8[9437184]{0:T(1024)(128)(4,1)} %bitcast.78), calls=%async_computation.3 | async-start | bytes 8388608
  92.2 9.0 %collective-permute-start.7 = (bf16[384,256]{1,0:T(8,128)(2,1)S(1)}, bf16[384,256]{1,0:T(8,128)(2,1)S(1)}, u32[]{:S(2)}, u32[]{:S(2)}) collective-permute-start(bf16[384,256]{1,0:T(8,128)(2,1)S(1)} %slice.50), channel_id=1, source_target_pairs={{0,4},{4,8},{8,12},{12,16},{16,20},{20,24},{24,28},{28,0},{1,5},{5... | collective-permute-start | bytes 589832 | tf_op jit(solution)/shard_map/ppermute | solution.py:25
  94.5 8.3 %collective-permute-start.8 = (bf16[384,256]{1,0:T(8,128)(2,1)S(1)}, bf16[384,256]{1,0:T(8,128)(2,1)S(1)}, u32[]{:S(2)}, u32[]{:S(2)}) collective-permute-start(bf16[384,256]{1,0:T(8,128)(2,1)S(1)} %slice.51), channel_id=1, source_target_pairs={{0,28},{4,0},{8,4},{12,8},{16,12},{20,16},{24,20},{28,24},{1,29},{... | collective-permute-start | bytes 589832 | tf_op jit(solution)/shard_map/ppermute | solution.py:25
  102.8 1.7 copy-start.2
  103.6 2.1 %slice-start.2 = ((s8[9437184]{0:T(1024)(128)(4,1)}), s8[1048576]{0:T(1024)(128)(4,1)S(1)}, s32[]{:S(2)}) async-start(s8[9437184]{0:T(1024)(128)(4,1)} %bitcast.78), calls=%async_computation.4 | async-start | bytes 2097152
  105.7 4.0 %copy-start.5 = (f32[1,128]{1,0:T(1,128)S(1)}, f32[1,128]{1,0:T(1,128)}, u32[]{:S(2)}) copy-start(f32[1,128]{1,0:T(1,128)} %param.12) | copy-start | bytes 1540
  105.7 4.0 %copy-start.6 = (f32[1,128]{1,0:T(1,128)S(1)}, f32[1,128]{1,0:T(1,128)}, u32[]{:S(2)}) copy-start(f32[1,128]{1,0:T(1,128)} %param.11) | copy-start | bytes 1540
  105.7 4.6 %copy-start.3 = (f32[384]{0:T(512)S(1)}, f32[384]{0:T(512)}, u32[]{:S(2)}) copy-start(f32[384]{0:T(512)} %param.13) | copy-start | bytes 4612
  111.3 15.2 %collective-permute-start.9 = (bf16[512,256]{1,0:T(8,128)(2,1)S(1)}, bf16[512,256]{1,0:T(8,128)(2,1)S(1)}, u32[]{:S(2)}, u32[]{:S(2)}) collective-permute-start(bf16[512,256]{1,0:T(8,128)(2,1)S(1)} %pad_maximum_fusion.1), channel_id=1, source_target_pairs={{0,8},{4,12},{8,16},{12,20},{16,24},{20,28},{24,0},{28,4},{1,9},{5... | collective-permute-start | bytes 786440 | tf_op jit(solution)/shard_map/ppermute | solution.py:25
  113.6 19.5 %collective-permute-start.12 = (bf16[512,256]{1,0:T(8,128)(2,1)S(1)}, bf16[512,256]{1,0:T(8,128)(2,1)S(1)}, u32[]{:S(2)}, u32[]{:S(2)}) collective-permute-start(bf16[512,256]{1,0:T(8,128)(2,1)S(1)} %pad_maximum_fusion.1), channel_id=1, source_target_pairs={{0,24},{4,28},{8,0},{12,4},{16,8},{20,12},{24,16},{28,20},{1,25},{... | collective-permute-start | bytes 786440 | tf_op jit(solution)/shard_map/ppermute | solution.py:25
  119.3 18.3 %collective-permute-start.10 = (bf16[512,256]{1,0:T(8,128)(2,1)S(1)}, bf16[512,256]{1,0:T(8,128)(2,1)S(1)}, u32[]{:S(2)}, u32[]{:S(2)}) collective-permute-start(bf16[512,256]{1,0:T(8,128)(2,1)S(1)} %pad_maximum_fusion.1), channel_id=1, source_target_pairs={{0,4},{4,8},{8,12},{12,16},{16,20},{20,24},{24,28},{28,0},{1,5},{5... | collective-permute-start | bytes 786440 | tf_op jit(solution)/shard_map/ppermute | solution.py:25
  122.2 15.4 %collective-permute-start.11 = (bf16[512,256]{1,0:T(8,128)(2,1)S(1)}, bf16[512,256]{1,0:T(8,128)(2,1)S(1)}, u32[]{:S(2)}, u32[]{:S(2)}) collective-permute-start(bf16[512,256]{1,0:T(8,128)(2,1)S(1)} %pad_maximum_fusion.1), channel_id=1, source_target_pairs={{0,28},{4,0},{8,4},{12,8},{16,12},{20,16},{24,20},{28,24},{1,29},{... | collective-permute-start | bytes 786440 | tf_op jit(solution)/shard_map/ppermute | solution.py:25
  126.5 20.2 %collective-permute-start.14 = (bf16[256,256]{1,0:T(8,128)(2,1)S(1)}, bf16[256,256]{1,0:T(8,128)(2,1)S(1)}, u32[]{:S(2)}, u32[]{:S(2)}) collective-permute-start(bf16[256,256]{1,0:T(8,128)(2,1)S(1)} %slice.56), channel_id=1, source_target_pairs={{0,8},{4,12},{8,16},{12,20},{16,24},{20,28},{24,0},{28,4},{1,9},{5... | collective-permute-start | bytes 393224 | tf_op jit(solution)/shard_map/ppermute | solution.py:25
  130.5 16.5 %collective-permute-start.16 = (bf16[512,256]{1,0:T(8,128)(2,1)S(1)}, bf16[512,256]{1,0:T(8,128)(2,1)S(1)}, u32[]{:S(2)}, u32[]{:S(2)}) collective-permute-start(bf16[512,256]{1,0:T(8,128)(2,1)S(1)} %collective-permute-done.9), channel_id=1, source_target_pairs={{0,4},{4,8},{8,12},{12,16},{16,20},{20,24},{24,28},{28,0},{1,5},{5... | collective-permute-start | bytes 786440 | tf_op jit(solution)/shard_map/ppermute | solution.py:25
  133.1 13.8 %collective-permute-start.13 = (bf16[512,256]{1,0:T(8,128)(2,1)S(1)}, bf16[512,256]{1,0:T(8,128)(2,1)S(1)}, u32[]{:S(2)}, u32[]{:S(2)}) collective-permute-start(bf16[512,256]{1,0:T(8,128)(2,1)S(1)} %collective-permute-done.12), channel_id=1, source_target_pairs={{0,28},{4,0},{8,4},{12,8},{16,12},{20,16},{24,20},{28,24},{1,29},{... | collective-permute-start | bytes 786440 | tf_op jit(solution)/shard_map/ppermute | solution.py:25
  138.7 8.2 %collective-permute-start.15 = (bf16[256,256]{1,0:T(8,128)(2,1)S(1)}, bf16[256,256]{1,0:T(8,128)(2,1)S(1)}, u32[]{:S(2)}, u32[]{:S(2)}) collective-permute-start(bf16[256,256]{1,0:T(8,128)(2,1)S(1)} %fusion.18), channel_id=1, source_target_pairs={{0,24},{4,28},{8,0},{12,4},{16,8},{20,12},{24,16},{28,20},{1,25},{... | collective-permute-start | bytes 393224 | tf_op jit(solution)/shard_map/ppermute | solution.py:25
  141.7 2.8 %copy-start = (bf16[6144,512]{1,0:T(8,128)(2,1)S(1)}, bf16[6144,512]{1,0:T(8,128)(2,1)}, u32[]{:S(2)}) copy-start(bf16[6144,512]{1,0:T(8,128)(2,1)} %all-gather.2.cloned.1.call-done) | copy-start | bytes 18874372
  148.4 29.6 %copy-start.1 = (bf16[1,256,192]{1,2,0:T(8,128)(2,1)S(1)}, bf16[1,256,192]{1,2,0:T(8,128)(2,1)}, u32[]{:S(2)}) copy-start(bf16[1,256,192]{1,2,0:T(8,128)(2,1)} %param.8) | copy-start | bytes 294916
  148.4 29.6 %copy-start.4 = (f32[192]{0:T(256)S(1)}, f32[192]{0:T(256)}, u32[]{:S(2)}) copy-start(f32[192]{0:T(256)} %param.15) | copy-start | bytes 2308
Sparse Core Ops, SparseCore 0:
  41.3 85.0 all-gather.1
